TPU v7x, 512 devices: a whole 4x4x16 slice. The times are simulated.
512 devices in a mesh: dp: 16 (over x, y_lo, core), fsdp: 32 (over y_hi, z).
Axes of the slice: x: 4, y: 4 (y_hi: 2, y_lo: 2; y = y_hi * 2 + y_lo), z: 16, core: 2. Of those that a mesh axis runs over, the one named last changes fastest.
Arguments:
- hidden: bfloat16 [65536, 8192], P(('dp', 'fsdp')), may hold values from -6 to 6
- queries: bfloat16 [65536, 4096], P(('dp', 'fsdp')), may hold values from -4.5 to 4.5
- keys: bfloat16 [65536, 512], P(('dp', 'fsdp')), may hold values from -4.5 to 4.5
- document_numbers: int32 [16, 4096], P('dp', 'fsdp'), may hold values from 0 to 15, never falling along the last dimension, each value on 1 to 896 neighbouring positions
- adapter_down_weight: bfloat16 [8192, 64], P('fsdp'), may hold values from -0.0625 to 0.0625
- adapter_up_weight: bfloat16 [64, 512], replicated, may hold values from -0.75 to 0.75
- output_gradient: bfloat16 [65536, 4096], P(('dp', 'fsdp')), may hold values from -0.0234375 to 0.0234375
Outputs:
- grad_down: float32 [8192, 64], P('fsdp')
- up_factor_gradient: float32 [64, 512], replicated
Inputs may be any that keep to these rules, and one draw needn't show every extreme that they name: `document_numbers`: each document has at most 896 tokens, and some document has exactly 896.
All inputs are finite; a program needn't handle non-finite values.
Results may differ from a plain program's by a relative error of at most 0.0055.
Values may be sent and summed in bfloat16 or wider, within the bound.
No kernel may reach another device: no remote copies, remote signals or barrier semaphores. Data moves between devices by JAX's collectives and lax.ppermute only.
A program may use at most 64 MiB of HBM per device.

v0:
```python
import math

import jax
import jax.numpy as jnp
from jax import lax
from jax.sharding import PartitionSpec as P

QUERY_HEADS = 32
KEY_HEADS = 4
HEAD_SIZE = 128
ADAPTER_RANK = 64
SPAN = 8


def from_behind(block, axis, distance):
    devices = range(lax.axis_size(axis))
    route = [(i - distance, i) for i in devices if i - distance in devices]
    return lax.ppermute(block, axis, route)


def local(
    hidden, queries, keys, document_numbers, adapter_down_weight, adapter_up_weight, output_gradient
):
    token_rows = hidden.shape[0]
    query_group_size = QUERY_HEADS // KEY_HEADS
    score_scale = 1.0 / math.sqrt(HEAD_SIZE)
    column_indices = hidden
    rank_projection = jnp.dot(
        column_indices,
        lax.all_gather(adapter_down_weight, "fsdp", axis=0, tiled=True),
        preferred_element_type=jnp.float32,
    ).astype(jnp.bfloat16)
    segment = document_numbers.reshape(token_rows)
    key_parts = [keys]
    rank_parts = [rank_projection]
    doc_parts = [segment]
    for distance in range(1, SPAN):
        far_keys, far_rank = from_behind((keys, rank_projection), "fsdp", distance)
        far_docs = from_behind(segment, "fsdp", distance)
        key_parts.insert(0, far_keys)
        rank_parts.insert(0, far_rank)
        doc_parts.insert(0, far_docs)
    key_window_rows = jnp.concatenate(key_parts, axis=0)
    window_rank = jnp.concatenate(rank_parts, axis=0)
    window_docs = jnp.concatenate(doc_parts, axis=0)
    position = lax.axis_index("fsdp")
    query_pos = position * token_rows + jnp.arange(token_rows, dtype=jnp.int32)
    key_pos = (position - (SPAN - 1)) * token_rows + jnp.arange(SPAN * token_rows, dtype=jnp.int32)
    visible = (
        (window_docs[None, :] == segment[:, None])
        & (key_pos[None, :] <= query_pos[:, None])
        & (key_pos[None, :] >= 0)
    )
    query_head_rows = queries.reshape(token_rows, KEY_HEADS, query_group_size, HEAD_SIZE)
    head_gradients = output_gradient.reshape(token_rows, KEY_HEADS, query_group_size, HEAD_SIZE)
    up_weight_heads = adapter_up_weight.reshape(ADAPTER_RANK, KEY_HEADS, HEAD_SIZE)
    contrib = jnp.zeros((SPAN * token_rows, ADAPTER_RANK), jnp.float32)
    up_parts = []
    for query_group_index in range(KEY_HEADS):
        head_keys = key_window_rows[
            :, query_group_index * HEAD_SIZE : (query_group_index + 1) * HEAD_SIZE
        ]
        scores = (
            jnp.einsum(
                "tmd,kd->tmk",
                query_head_rows[:, query_group_index],
                head_keys,
                preferred_element_type=jnp.float32,
            )
            * score_scale
        )
        scores = jnp.where(visible[:, None, :], scores, -jnp.inf)
        row_max = jnp.max(scores, axis=-1, keepdims=True)
        weights = jnp.exp(scores - row_max)
        probs = (weights / jnp.sum(weights, axis=-1, keepdims=True)).astype(jnp.bfloat16)
        weighted_values = jnp.einsum(
            "tmk,kr->tmr", probs, window_rank, preferred_element_type=jnp.float32
        ).astype(jnp.bfloat16)
        visible_mask = jnp.einsum(
            "tmd,rd->tmr",
            head_gradients[:, query_group_index],
            up_weight_heads[:, query_group_index],
            preferred_element_type=jnp.float32,
        ).astype(jnp.bfloat16)
        contrib = contrib + jnp.einsum(
            "tmk,tmr->kr", probs, visible_mask, preferred_element_type=jnp.float32
        )
        up_parts.append(
            jnp.einsum(
                "tmr,tmd->rd",
                weighted_values,
                head_gradients[:, query_group_index],
                preferred_element_type=jnp.float32,
            )
        )
    up_local = jnp.concatenate(up_parts, axis=1)
    own_sums = contrib[(SPAN - 1) * token_rows :]
    for distance in range(1, SPAN):
        slot_rows = contrib[(SPAN - 1 - distance) * token_rows : (SPAN - distance) * token_rows]
        own_sums = own_sums + from_behind(slot_rows, "fsdp", -distance)
    key_grad = own_sums.astype(jnp.bfloat16)
    column_indices = hidden
    down_share = lax.psum_scatter(
        lax.dot_general(
            column_indices, key_grad, (((0,), (0,)), ((), ())), preferred_element_type=jnp.float32
        ),
        "fsdp",
        scatter_dimension=0,
        tiled=True,
    )
    grad_down = lax.psum(down_share, "dp")
    up_factor_gradient = lax.psum(up_local, ("dp", "fsdp"))
    return (grad_down, up_factor_gradient)


def solution(mesh):
    in_specs = (
        P(("dp", "fsdp"), None),
        P(("dp", "fsdp"), None),
        P(("dp", "fsdp"), None),
        P("dp", "fsdp"),
        P("fsdp", None),
        P(),
        P(("dp", "fsdp"), None),
    )
    out_specs = (P("fsdp", None), P())
    return jax.shard_map(local, mesh=mesh, in_specs=in_specs, out_specs=out_specs, check_vma=False)
```

profile of v0, /device:TPU:1, one launch (start us, length us, event | category | flops | bytes accessed | tf_op | source)
XLA Modules:
  0.0 1439.1 jit_solution(13832688556537154167)
XLA Ops:
  7.2 13.8 collective-permute-start
  21.1 7.0 collective-permute-start.1
  29.7 8.8 collective-permute-start.3
  38.6 6.6 collective-permute-start.4
  72.4 17.4 %collective-permute-done.8 = bf16[128,512]{1,0:T(8,128)(2,1)S(1)} collective-permute-done((bf16[128,512]{1,0:T(8,128)(2,1)S(1)}, bf16[128,512]{1,0:T(8,128)(2,1)S(1)}, u32[]{:S(2)}, u32[]{:S(2)}) %collective-permute-start.8) | collective-permute-done | bytes 131104 | tf_op jit(solution)/shard_map/ppermute | solution.py:18
  91.1 16.1 %collective-permute-done.9 = bf16[128,512]{1,0:T(8,128)(2,1)S(1)} collective-permute-done((bf16[128,512]{1,0:T(8,128)(2,1)S(1)}, bf16[128,512]{1,0:T(8,128)(2,1)S(1)}, u32[]{:S(2)}, u32[]{:S(2)}) %collective-permute-start.9) | collective-permute-done | bytes 131104 | tf_op jit(solution)/shard_map/ppermute | solution.py:18
  107.3 10.1 collective-permute-done.10
  117.4 7.3 collective-permute-done.11
  124.7 5.3 collective-permute-done.12
  130.0 4.0 collective-permute-done.13
  135.1 4.3 fusion.87
  139.4 4.4 fusion.86
  143.8 4.3 fusion.85
  165.5 4.3 fusion.88
  188.0 5.3 collective-permute-done.17
  195.6 5.6 collective-permute-done.19
  201.3 4.2 collective-permute-done.20
  209.6 7.8 collective-permute-start.21
  217.4 12.9 collective-permute-start.22
  230.3 6.9 collective-permute-start.23
  237.2 10.3 collective-permute-start.24
  264.6 588.7 %reduce-scatter.2.cloned.1.call-done = f32[256,64]{0,1:T(8,128)} async-done(((f32[8192,64]{0,1:T(8,128)}), f32[256,64]{0,1:T(8,128)}) %reduce-scatter.2.cloned.1.call-update) | async-done | bytes 65552 | tf_op jit(solution)/shard_map/reduce_scatter | solution.py:103
  853.3 462.7 %all-reduce.5.cloned.1.call-done = f32[64,512]{1,0:T(8,128)} async-done(((f32[64,512]{1,0:T(8,128)}), f32[64,512]{1,0:T(8,128)}) %all-reduce.5.cloned.1.call-update) | async-done | bytes 131088 | tf_op jit(solution)/shard_map/psum | solution.py:112
  1316.0 113.5 %all-reduce.3.cloned.1.call-done = f32[256,64]{0,1:T(8,128)} async-done(((f32[256,64]{0,1:T(8,128)}), f32[256,64]{0,1:T(8,128)}) %all-reduce.3.cloned.1.call-update) | async-done | bytes 65552 | tf_op jit(solution)/shard_map/psum | solution.py:111
  (113 shorter events, 92.9 us)
Async XLA Ops:
  7.2 200.3 %all-gather.2.cloned.1.call-start = ((), (), s32[]{:S(2)}) async-start(), calls=%async_computation.3 | async-start | bytes 1081344 | tf_op jit(solution)/shard_map/all_gather | solution.py:30
  7.2 44.1 %collective-permute-start = (s32[128]{0:T(128)}, s32[128]{0:T(128)S(1)}, u32[]{:S(2)}, u32[]{:S(2)}) collective-permute-start(s32[128]{0:T(128)} %bitcast.244), channel_id=1, source_target_pairs={{0,7},{1,8},{2,9},{3,10},{4,11},{5,12},{6,13},{7,14},{8,15},{9,16}... | collective-permute-start | bytes 1544 | tf_op jit(solution)/shard_map/ppermute | solution.py:18
  21.1 33.4 %collective-permute-start.1 = (s32[128]{0:T(128)}, s32[128]{0:T(128)S(1)}, u32[]{:S(2)}, u32[]{:S(2)}) collective-permute-start(s32[128]{0:T(128)} %bitcast.245), channel_id=1, source_target_pairs={{0,6},{1,7},{2,8},{3,9},{4,10},{5,11},{6,12},{7,13},{8,14},{9,15},... | collective-permute-start | bytes 1544 | tf_op jit(solution)/shard_map/ppermute | solution.py:18
  28.1 29.0 %collective-permute-start.2 = (s32[128]{0:T(128)}, s32[128]{0:T(128)S(1)}, u32[]{:S(2)}, u32[]{:S(2)}) collective-permute-start(s32[128]{0:T(128)} %bitcast.246), channel_id=1, source_target_pairs={{0,5},{1,6},{2,7},{3,8},{4,9},{5,10},{6,11},{7,12},{8,13},{9,14},{... | collective-permute-start | bytes 1544 | tf_op jit(solution)/shard_map/ppermute | solution.py:18
  29.7 30.8 %collective-permute-start.3 = (s32[128]{0:T(128)}, s32[128]{0:T(128)S(1)}, u32[]{:S(2)}, u32[]{:S(2)}) collective-permute-start(s32[128]{0:T(128)} %bitcast.247), channel_id=1, source_target_pairs={{0,4},{1,5},{2,6},{3,7},{4,8},{5,9},{6,10},{7,11},{8,12},{9,13},{1... | collective-permute-start | bytes 1544 | tf_op jit(solution)/shard_map/ppermute | solution.py:18
  38.6 23.9 %collective-permute-start.4 = (s32[128]{0:T(128)}, s32[128]{0:T(128)S(1)}, u32[]{:S(2)}, u32[]{:S(2)}) collective-permute-start(s32[128]{0:T(128)} %bitcast.248), channel_id=1, source_target_pairs={{0,3},{1,4},{2,5},{3,6},{4,7},{5,8},{6,9},{7,10},{8,11},{9,12},{10... | collective-permute-start | bytes 1544 | tf_op jit(solution)/shard_map/ppermute | solution.py:18
  45.2 808.1 %reduce-scatter.2.cloned.1.call-start = ((), (), s32[]{:S(2)}) async-start(), calls=%async_computation.1 | async-start | bytes 2162688 | tf_op jit(solution)/shard_map/reduce_scatter | solution.py:103
  57.2 13.6 collective-permute-start.7
  60.5 29.3 %collective-permute-start.8 = (bf16[128,512]{1,0:T(8,128)(2,1)S(1)}, bf16[128,512]{1,0:T(8,128)(2,1)S(1)}, u32[]{:S(2)}, u32[]{:S(2)}) collective-permute-start(bf16[128,512]{1,0:T(8,128)(2,1)S(1)} %copy-done.3), channel_id=1, source_target_pairs={{0,6},{1,7},{2,8},{3,9},{4,10},{5,11},{6,12},{7,13},{8,14},{9,15},... | collective-permute-start | bytes 393224 | tf_op jit(solution)/shard_map/ppermute | solution.py:18
  62.5 44.8 %collective-permute-start.9 = (bf16[128,512]{1,0:T(8,128)(2,1)S(1)}, bf16[128,512]{1,0:T(8,128)(2,1)S(1)}, u32[]{:S(2)}, u32[]{:S(2)}) collective-permute-start(bf16[128,512]{1,0:T(8,128)(2,1)S(1)} %copy-done.3), channel_id=1, source_target_pairs={{0,5},{1,6},{2,7},{3,8},{4,9},{5,10},{6,11},{7,12},{8,13},{9,14},{... | collective-permute-start | bytes 393224 | tf_op jit(solution)/shard_map/ppermute | solution.py:18
  64.4 52.9 %collective-permute-start.10 = (bf16[128,512]{1,0:T(8,128)(2,1)S(1)}, bf16[128,512]{1,0:T(8,128)(2,1)S(1)}, u32[]{:S(2)}, u32[]{:S(2)}) collective-permute-start(bf16[128,512]{1,0:T(8,128)(2,1)S(1)} %copy-done.3), channel_id=1, source_target_pairs={{0,4},{1,5},{2,6},{3,7},{4,8},{5,9},{6,10},{7,11},{8,12},{9,13},{1... | collective-permute-start | bytes 393224 | tf_op jit(solution)/shard_map/ppermute | solution.py:18
  66.6 58.0 %collective-permute-start.11 = (bf16[128,512]{1,0:T(8,128)(2,1)S(1)}, bf16[128,512]{1,0:T(8,128)(2,1)S(1)}, u32[]{:S(2)}, u32[]{:S(2)}) collective-permute-start(bf16[128,512]{1,0:T(8,128)(2,1)S(1)} %copy-done.3), channel_id=1, source_target_pairs={{0,3},{1,4},{2,5},{3,6},{4,7},{5,8},{6,9},{7,10},{8,11},{9,12},{10... | collective-permute-start | bytes 393224 | tf_op jit(solution)/shard_map/ppermute | solution.py:18
  70.7 59.3 %collective-permute-start.12 = (bf16[128,512]{1,0:T(8,128)(2,1)S(1)}, bf16[128,512]{1,0:T(8,128)(2,1)S(1)}, u32[]{:S(2)}, u32[]{:S(2)}) collective-permute-start(bf16[128,512]{1,0:T(8,128)(2,1)S(1)} %copy-done.3), channel_id=1, source_target_pairs={{0,2},{1,3},{2,4},{3,5},{4,6},{5,7},{6,8},{7,9},{8,10},{9,11},{10,... | collective-permute-start | bytes 393224 | tf_op jit(solution)/shard_map/ppermute | solution.py:18
  89.8 44.2 %collective-permute-start.13 = (bf16[128,512]{1,0:T(8,128)(2,1)S(1)}, bf16[128,512]{1,0:T(8,128)(2,1)S(1)}, u32[]{:S(2)}, u32[]{:S(2)}) collective-permute-start(bf16[128,512]{1,0:T(8,128)(2,1)S(1)} %copy-done.3), channel_id=1, source_target_pairs={{0,1},{1,2},{2,3},{3,4},{4,5},{5,6},{6,7},{7,8},{8,9},{9,10},{10,1... | collective-permute-start | bytes 393224 | tf_op jit(solution)/shard_map/ppermute | solution.py:18
  180.2 13.1 collective-permute-start.17
  181.5 14.2 collective-permute-start.18
  182.8 18.5 %collective-permute-start.19 = (f32[128,64]{0,1:T(8,128)S(1)}, f32[128,64]{0,1:T(8,128)S(1)}, u32[]{:S(2)}, u32[]{:S(2)}) collective-permute-start(f32[128,64]{0,1:T(8,128)S(1)} %get-tuple-element.4), channel_id=1, source_target_pairs={{6,0},{7,1},{8,2},{9,3},{10,4},{11,5},{12,6},{13,7},{14,8},{15,9},... | collective-permute-start | bytes 98312 | tf_op jit(solution)/shard_map/ppermute | solution.py:18
  185.0 20.4 %collective-permute-start.20 = (f32[128,64]{0,1:T(8,128)S(1)}, f32[128,64]{0,1:T(8,128)S(1)}, u32[]{:S(2)}, u32[]{:S(2)}) collective-permute-start(f32[128,64]{0,1:T(8,128)S(1)} %get-tuple-element.3), channel_id=1, source_target_pairs={{7,0},{8,1},{9,2},{10,3},{11,4},{12,5},{13,6},{14,7},{15,8},{16,9}... | collective-permute-start | bytes 98312 | tf_op jit(solution)/shard_map/ppermute | solution.py:18
  207.2 1108.8 %all-reduce.5.cloned.1.call-start = ((), (), s32[]{:S(2)}) async-start(), calls=%async_computation.4 | async-start | bytes 262144 | tf_op jit(solution)/shard_map/psum | solution.py:112
  209.6 39.3 %collective-permute-start.21 = (bf16[128,64]{0,1:T(8,128)(2,1)S(1)}, bf16[128,64]{0,1:T(8,128)(2,1)S(1)}, u32[]{:S(2)}, u32[]{:S(2)}) collective-permute-start(bf16[128,64]{0,1:T(8,128)(2,1)S(1)} %convolution_convert_fusion.8), channel_id=1, source_target_pairs={{0,7},{1,8},{2,9},{3,10},{4,11},{5,12},{6,13},{7,14},{8,15},{9,16}... | collective-permute-start | bytes 49160 | tf_op jit(solution)/shard_map/ppermute | solution.py:18
  217.4 34.3 %collective-permute-start.22 = (bf16[128,64]{0,1:T(8,128)(2,1)S(1)}, bf16[128,64]{0,1:T(8,128)(2,1)S(1)}, u32[]{:S(2)}, u32[]{:S(2)}) collective-permute-start(bf16[128,64]{0,1:T(8,128)(2,1)S(1)} %convolution_convert_fusion.8), channel_id=1, source_target_pairs={{0,6},{1,7},{2,8},{3,9},{4,10},{5,11},{6,12},{7,13},{8,14},{9,15},... | collective-permute-start | bytes 49160 | tf_op jit(solution)/shard_map/ppermute | solution.py:18
  230.3 23.6 %collective-permute-start.23 = (bf16[128,64]{0,1:T(8,128)(2,1)S(1)}, bf16[128,64]{0,1:T(8,128)(2,1)S(1)}, u32[]{:S(2)}, u32[]{:S(2)}) collective-permute-start(bf16[128,64]{0,1:T(8,128)(2,1)S(1)} %convolution_convert_fusion.8), channel_id=1, source_target_pairs={{0,5},{1,6},{2,7},{3,8},{4,9},{5,10},{6,11},{7,12},{8,13},{9,14},{... | collective-permute-start | bytes 49160 | tf_op jit(solution)/shard_map/ppermute | solution.py:18
  237.2 16.7 %collective-permute-start.24 = (bf16[128,64]{0,1:T(8,128)(2,1)S(1)}, bf16[128,64]{0,1:T(8,128)(2,1)S(1)}, u32[]{:S(2)}, u32[]{:S(2)}) collective-permute-start(bf16[128,64]{0,1:T(8,128)(2,1)S(1)} %convolution_convert_fusion.8), channel_id=1, source_target_pairs={{0,4},{1,5},{2,6},{3,7},{4,8},{5,9},{6,10},{7,11},{8,12},{9,13},{1... | collective-permute-start | bytes 49160 | tf_op jit(solution)/shard_map/ppermute | solution.py:18
  264.6 1165.0 %all-reduce.3.cloned.1.call-start = ((), (), s32[]{:S(2)}) async-start(), calls=%async_computation.2 | async-start | bytes 131072 | tf_op jit(solution)/shard_map/psum | solution.py:111
  (15 other events, 367.2 us)
Sparse Core Ops, SparseCore 0:
  45.3 161.9 all-gather.1
  211.7 641.5 reduce-scatter.1
  859.3 456.6 all-reduce.4
  1319.0 110.4 all-reduce.2
where the time goes:
time: 1440 us
  waiting for transfers between devices  1250 us (87%)
  starting transfers between devices  111 us (8%)
  matrix products  41.4 us (3%)
    reduce_scatter x1, waiting for transfers between devices, local(): lax.psum_scatter(lax.dot_general(column_indices, key_grad, (((0,), (0,)),...  589 us
    psum x1, waiting for transfers between devices, local(): up_factor_gradient = lax.psum(up_local, ('dp', 'fsdp'))  463 us
    psum x1, waiting for transfers between devices, local(): grad_down = lax.psum(down_share, 'dp')  114 us
    ppermute x28, starting transfers between devices, from_behind(): return lax.ppermute(block, axis, route)  111 us
    ppermute x28, waiting for transfers between devices, from_behind(): return lax.ppermute(block, axis, route)  81.7 us
  transfers between devices with their start and end apart: 32, of which 17 were waited for; matrix products, arithmetic and copies ran while one was open for 4% of the time, Pallas kernels for 0%

commit v1 on v0

v1 whole, which is shorter than its diff:
```python
import math

import jax
import jax.numpy as jnp
from jax import lax
from jax.experimental import pallas as pl
from jax.experimental.pallas import tpu as pltpu
from jax.sharding import PartitionSpec as P

QUERY_HEADS = 32
KEY_HEADS = 4
HEAD_SIZE = 128
ADAPTER_RANK = 64
SPAN = 8
TOKENS = 128
WINDOW = SPAN * TOKENS
N_DP = 16
N_FSDP = 32
MODEL_WIDTH = 8192
PAIRS = QUERY_HEADS // 2
VMEM_LIMIT = 48 * 1024 * 1024
BF16 = jnp.bfloat16
F32 = jnp.float32
NT = (((1,), (1,)), ((), ()))


def whole(*arrays):
    return [pl.BlockSpec(memory_space=pltpu.VMEM) for _ in arrays]


def params():
    return pltpu.CompilerParams(vmem_limit_bytes=VMEM_LIMIT)


def from_behind(block, distance):
    route = [(i, i + distance) for i in range(N_FSDP) if 0 <= i + distance < N_FSDP]
    return lax.ppermute(block, "fsdp", route)


def exchange(slots, axis):
    return lax.all_to_all(slots, axis, 0, 0, tiled=True)


def after(value, *others):
    return lax.optimization_barrier((value, *others))[0]


def lowrank_kernel(weight_ref, hidden_ref, out_ref):
    total = jnp.zeros((ADAPTER_RANK, TOKENS), F32)
    for f in range(N_FSDP):
        rows = jnp.concatenate(
            [weight_ref[half, :, f * 128 : f * 128 + 128] for half in range(2)], axis=1
        )
        total += lax.dot_general(
            rows, hidden_ref[:, f * 256 : f * 256 + 256], NT, preferred_element_type=F32
        )
    out_ref[...] = total.astype(BF16)


def attention_kernel(
    query_ref,
    gradient_ref,
    up_ref,
    keys3_ref,
    keys2_ref,
    keys1_ref,
    keys0_ref,
    bias_ref,
    probs_ref,
    contrib_ref,
    scores_ref,
    sums_ref,
):
    step = pl.program_id(0)
    factor = math.log2(math.e) / math.sqrt(HEAD_SIZE)
    queries = jnp.concatenate([query_ref[:, :128], query_ref[:, 128:]], axis=0)
    top = jnp.full((1, 256), -jnp.inf, F32)
    key_refs = (keys3_ref, keys2_ref, keys1_ref, keys0_ref)
    for b in range(SPAN):
        keys = key_refs[b // 2][(b % 2) * 128 : (b % 2) * 128 + 128, :]
        rows = slice(b * 128, b * 128 + 128)
        bias = bias_ref[rows, :]
        scores = lax.dot_general(keys, queries, NT, preferred_element_type=F32)
        scores = scores + jnp.concatenate([bias, bias], axis=1)
        scores_ref[rows, :] = scores
        top = jnp.maximum(top, jnp.max(scores, axis=0, keepdims=True))
    shift = top * factor
    total = jnp.zeros((1, 256), F32)
    for b in range(SPAN):
        rows = slice(b * 128, b * 128 + 128)
        weights = jnp.exp2(scores_ref[rows, :] * factor - shift)
        scores_ref[rows, :] = weights
        total += jnp.sum(weights, axis=0, keepdims=True)
    inverse = 1.0 / total
    reached = [
        lax.dot_general(
            gradient_ref[:, half * 128 : half * 128 + 128],
            up_ref[...],
            NT,
            preferred_element_type=F32,
        ).astype(BF16)
        for half in range(2)
    ]
    reached = jnp.concatenate(reached, axis=0)

    @pl.when(step == 0)
    def _():
        sums_ref[...] = jnp.zeros_like(sums_ref)

    for b in range(SPAN):
        rows = slice(b * 128, b * 128 + 128)
        probs = (scores_ref[rows, :] * inverse).astype(BF16)
        probs_ref[rows, :] = probs
        sums_ref[rows, :] += jnp.dot(probs, reached, preferred_element_type=F32)

    @pl.when(step == PAIRS - 1)
    def _():
        contrib_ref[...] = sums_ref[...].T


def attention(queries, gradients, up_weight, key_pairs, bias):
    pair = pl.BlockSpec((TOKENS, 256), lambda p: (0, p))
    keys = pl.BlockSpec((2 * TOKENS, HEAD_SIZE), lambda p: (0, p // 4))
    return pl.pallas_call(
        attention_kernel,
        grid=(PAIRS,),
        in_specs=[
            pair,
            pair,
            pl.BlockSpec((ADAPTER_RANK, HEAD_SIZE), lambda p: (0, p // 4)),
            keys,
            keys,
            keys,
            keys,
            pl.BlockSpec((WINDOW, TOKENS), lambda p: (0, 0)),
        ],
        out_specs=[
            pl.BlockSpec((WINDOW, 256), lambda p: (0, p)),
            pl.BlockSpec((ADAPTER_RANK, WINDOW), lambda p: (0, 0)),
        ],
        out_shape=[
            jax.ShapeDtypeStruct((WINDOW, QUERY_HEADS * TOKENS), BF16),
            jax.ShapeDtypeStruct((ADAPTER_RANK, WINDOW), F32),
        ],
        scratch_shapes=[pltpu.VMEM((WINDOW, 256), F32), pltpu.VMEM((WINDOW, ADAPTER_RANK), F32)],
        compiler_params=params(),
        cost_estimate=pl.CostEstimate(
            flops=3 * 10**9, bytes_accessed=12 * 2**20, transcendentals=4 * 2**20
        ),
        name="attention",
    )(queries, gradients, up_weight, *key_pairs, bias)


def mixed_kernel(probs_ref, rank_ref, gradient_ref, out_ref):
    step = pl.program_id(0)
    mixed = jnp.dot(rank_ref[...], probs_ref[...], preferred_element_type=F32).astype(BF16)
    gradients = jnp.concatenate([gradient_ref[:, :128], gradient_ref[:, 128:]], axis=0)
    share = jnp.dot(mixed, gradients, preferred_element_type=F32)

    @pl.when(step % 4 == 0)
    def _():
        out_ref[...] = share

    @pl.when(step % 4 != 0)
    def _():
        out_ref[...] += share


def mixed_share(probs, rank_window, gradients):
    return pl.pallas_call(
        mixed_kernel,
        grid=(PAIRS,),
        in_specs=[
            pl.BlockSpec((WINDOW, 256), lambda p: (0, p)),
            pl.BlockSpec((ADAPTER_RANK, WINDOW), lambda p: (0, 0)),
            pl.BlockSpec((TOKENS, 256), lambda p: (0, p)),
        ],
        out_specs=pl.BlockSpec((ADAPTER_RANK, HEAD_SIZE), lambda p: (0, p // 4)),
        out_shape=jax.ShapeDtypeStruct((ADAPTER_RANK, KEY_HEADS * HEAD_SIZE), F32),
        compiler_params=params(),
        cost_estimate=pl.CostEstimate(
            flops=6 * 10**8, bytes_accessed=10 * 2**20, transcendentals=0
        ),
        name="mixed",
    )(probs, rank_window, gradients)


DOWN = N_FSDP * 128
LANES = DOWN + 256


def shares_kernel(key_ref, hidden_ref, up_ref, out_ref):
    for f in range(N_FSDP):
        product = jnp.dot(
            key_ref[...], hidden_ref[:, f * 256 : f * 256 + 256], preferred_element_type=F32
        ).astype(BF16)
        for half in range(2):
            out_ref[half, :, f * 128 : f * 128 + 128] = product[:, half * 128 : half * 128 + 128]
    for half in range(2):
        out_ref[half, :, DOWN:] = up_ref[:, half * 256 : half * 256 + 256].astype(BF16)


def fold_dp_kernel(in_ref, out_ref):
    def total(columns):
        return sum(in_ref[d, :, columns].astype(F32) for d in range(N_DP))

    up = total(slice(DOWN, LANES))
    for f in range(N_FSDP):
        out_ref[f, :, :128] = total(slice(f * 128, f * 128 + 128))
        out_ref[f, :, 128:] = up


def fold_fsdp_kernel(in_ref, out_ref):
    total = sum(in_ref[f] for f in range(N_FSDP))
    for d in range(N_DP):
        out_ref[d] = total


def spread_kernel(in_ref, down_ref, up_ref):
    for half in range(2):
        for part in range(8):
            rows = slice(part * 8, part * 8 + 8)
            block = in_ref[half * 8 + part]
            down_ref[rows, half * 128 : half * 128 + 128] = block[:, :128]
            up_ref[rows, half * 256 : half * 256 + 256] = block[:, 128:]


def plain(kernel, name, out_shape, *arrays):
    return pl.pallas_call(
        kernel,
        in_specs=whole(*arrays),
        out_specs=jax.tree.map(lambda _: pl.BlockSpec(memory_space=pltpu.VMEM), out_shape),
        out_shape=out_shape,
        compiler_params=params(),
        name=name,
    )(*arrays)


def local(
    hidden, queries, keys, document_numbers, adapter_down_weight, adapter_up_weight, output_gradient
):
    position = lax.axis_index("fsdp")
    member = lax.axis_index("dp")
    half, part = member // 8, member % 8

    behind_one = from_behind(keys, 1)
    key_pairs = [jnp.concatenate([behind_one, keys], axis=0)]
    weight_slice = lax.dynamic_slice(
        adapter_down_weight.T, (part * 8, half * 128), (8, 128)
    )
    docs_row = document_numbers.reshape(1, TOKENS).astype(BF16)
    slot = jnp.concatenate([weight_slice, docs_row, jnp.zeros((7, 128), BF16)], axis=0)
    slots = jnp.broadcast_to(slot[None], (N_FSDP, 16, 128))
    slots, pair = lax.optimization_barrier((slots, key_pairs[0]))
    key_pairs = [pair]
    key_pairs.insert(0, from_behind(key_pairs[0], 2))
    row_parts = exchange(slots, "fsdp")
    weight_part = row_parts[:, :8].transpose(1, 0, 2).reshape(1, 8, DOWN)
    docs = row_parts[:, 8].astype(jnp.int32)
    weight_slots = jnp.broadcast_to(weight_part, (N_DP, 8, DOWN))
    weight_slots, pair = lax.optimization_barrier((weight_slots, key_pairs[0]))
    key_pairs[0] = pair
    key_pairs.insert(0, from_behind(key_pairs[0], 2))
    weight = exchange(weight_slots, "dp").reshape(2, ADAPTER_RANK, DOWN)
    key_pairs.insert(0, from_behind(key_pairs[0], 2))

    rank = plain(
        lowrank_kernel, "lowrank", jax.ShapeDtypeStruct((ADAPTER_RANK, TOKENS), BF16), weight, hidden
    )
    rank_window = rank
    for distance in (1, 2, 4):
        rank_window = jnp.concatenate([from_behind(rank_window, distance), rank_window], axis=1)

    padded = jnp.concatenate([jnp.full((SPAN - 1, TOKENS), -1, jnp.int32), docs], axis=0)
    window_docs = lax.dynamic_slice(padded, (position, 0), (SPAN, TOKENS)).reshape(WINDOW)
    own_docs = document_numbers.reshape(TOKENS)
    key_pos = jnp.arange(WINDOW, dtype=jnp.int32) - (SPAN - 1) * TOKENS
    visible = (window_docs[:, None] == own_docs[None, :]) & (
        key_pos[:, None] <= jnp.arange(TOKENS, dtype=jnp.int32)[None, :]
    )
    bias = jnp.where(visible, 0.0, -jnp.inf).astype(F32)

    probs, contrib = attention(queries, output_gradient, adapter_up_weight, key_pairs, bias)
    for distance in (4, 2, 1):
        lanes = distance * TOKENS
        sent = from_behind(contrib[:, :lanes].astype(BF16), -distance)
        contrib = contrib[:, lanes:] + sent.astype(F32)
    key_grad = contrib.astype(BF16)
    up_share = mixed_share(probs, rank_window, output_gradient)

    shares = plain(
        shares_kernel,
        "shares",
        jax.ShapeDtypeStruct((2, ADAPTER_RANK, LANES), BF16),
        key_grad,
        hidden,
        up_share,
    )
    shares = exchange(shares.reshape(N_DP, 8, LANES), "dp")
    shares = plain(
        fold_dp_kernel, "fold_dp", jax.ShapeDtypeStruct((N_FSDP, 8, 384), F32), shares
    )
    shares = exchange(shares, "fsdp")
    shares = plain(
        fold_fsdp_kernel, "fold_fsdp", jax.ShapeDtypeStruct((N_DP, 8, 384), F32), shares
    )
    shares = exchange(shares, "dp")
    down, up = plain(
        spread_kernel,
        "spread",
        (
            jax.ShapeDtypeStruct((ADAPTER_RANK, 256), F32),
            jax.ShapeDtypeStruct((ADAPTER_RANK, KEY_HEADS * HEAD_SIZE), F32),
        ),
        shares,
    )
    return (down.T, up)


def solution(mesh):
    in_specs = (
        P(("dp", "fsdp"), None),
        P(("dp", "fsdp"), None),
        P(("dp", "fsdp"), None),
        P("dp", "fsdp"),
        P("fsdp", None),
        P(),
        P(("dp", "fsdp"), None),
    )
    out_specs = (P("fsdp", None), P())
    return jax.shard_map(local, mesh=mesh, in_specs=in_specs, out_specs=out_specs, check_vma=False)
```

time: 1440 us -> 233 us (0.16)
  waiting for transfers between devices: 1250 us -> 33.5 us
  blocking collectives: 0 us -> 85 us
  matrix products: 41.4 us -> 0 us
  starting transfers between devices: 111 us -> 73.8 us
  Pallas kernels: 0 us -> 30.2 us
    reduce_scatter x1 -> x0, waiting for transfers between devices: 589 us -> none  [local(): lax.psum_scatter(lax.dot_general(column_indices, key_grad, (((0,), (0,)),...]
    psum x2 -> x0, waiting for transfers between devices: 576 us -> none  [the longest x1 463 us: local(): up_factor_gradient = lax.psum(up_local, ('dp', 'fsdp'))]
    all_to_all x0 -> x3, blocking collectives: none -> 85 us  [exchange(): return lax.all_to_all(slots, axis, 0, 0, tiled=True)]
    ppermute x28 -> x10, starting transfers between devices: 111 us -> 44.6 us  [from_behind(): return lax.ppermute(block, 'fsdp', route)]
    ppermute x28 -> x10, waiting for transfers between devices: 81.7 us -> 21.9 us  [from_behind(): return lax.ppermute(block, 'fsdp', route)]
    pallas_call x0 -> x7, Pallas kernels: none -> 30.2 us  [the longest x1 16.2 us: attention(): pl.pallas_call(attention_kernel, grid=(PAIRS,), in_specs=[pair, pair, pl....]
    all_to_all x0 -> x2, starting transfers between devices: none -> 29.2 us  [exchange(): return lax.all_to_all(slots, axis, 0, 0, tiled=True)]
    dot_general x10 -> x0, matrix products: 24.1 us -> none  [the longest x4 11.2 us: local(): jnp.einsum('tmk,tmr->kr', probs, visible_mask, preferred_element_type=jnp...]
  transfers between devices with their start and end apart: 32 -> 12, of which waited for: 17 -> 6; matrix products, arithmetic and copies ran while one was open for 4% -> 1% of each run, Pallas kernels for 0% -> 7%
where the time goes in v1:
time: 233 us; the launch traced here: 232 us
  blocking collectives  85 us (36%)
  starting transfers between devices  73.8 us (32%)
  waiting for transfers between devices  33.5 us (14%)
  Pallas kernels  30.2 us (13%)
  local copies, waits for them, and re-layouts  6.13 us (3%)
    all_to_all x3, blocking collectives, exchange(): return lax.all_to_all(slots, axis, 0, 0, tiled=True)  85 us
    ppermute x10, starting transfers between devices, from_behind(): return lax.ppermute(block, 'fsdp', route)  44.6 us
    all_to_all x2, starting transfers between devices, exchange(): return lax.all_to_all(slots, axis, 0, 0, tiled=True)  29.2 us
    ppermute x10, waiting for transfers between devices, from_behind(): return lax.ppermute(block, 'fsdp', route)  21.9 us
    pallas_call x1, Pallas kernels, attention(): pl.pallas_call(attention_kernel, grid=(PAIRS,), in_specs=[pair, pair, pl....  16.2 us
    pallas_call x1, Pallas kernels, mixed_share(): pl.pallas_call(mixed_kernel, grid=(PAIRS,), in_specs=[pl.BlockSpec((WINDO...  11.8 us
    all_to_all x2, waiting for transfers between devices, exchange(): return lax.all_to_all(slots, axis, 0, 0, tiled=True)  11.7 us
  transfers between devices with their start and end apart: 12, of which 6 were waited for; matrix products, arithmetic and copies ran while one was open for 1% of the time, Pallas kernels for 7%

profile of v1, /device:TPU:1, one launch (start us, length us, event | category | flops | bytes accessed | tf_op | source)
XLA Modules:
  0.0 231.7 jit_solution(3051027125915045975)
XLA Ops:
  0.6 4.4 %collective-permute-start = (bf16[128,512]{1,0:T(8,128)(2,1)}, bf16[128,512]{1,0:T(8,128)(2,1)S(1)}, u32[]{:S(2)}, u32[]{:S(2)}) collective-permute-start(bf16[128,512]{1,0:T(8,128)(2,1)} %param.9), channel_id=1, source_target_pairs={{0,1},{1,2},{2,3},{3,4},{4,5},{5,6},{6,7},{7,8},{8,9},{9,10},{10,1... | collective-permute-start | bytes 393224 | tf_op jit(solution)/shard_map/ppermute | solution.py:37
  5.9 1.4 collective-permute-done
  8.9 19.8 %all-to-all-start = ((bf16[32,16,128]{2,1,0:T(8,128)(2,1)}), bf16[32,16,128]{2,1,0:T(8,128)(2,1)S(1)}, u32[]{:S(2)}, u32[]{:S(2)}) async-start(bf16[32,16,128]{2,1,0:T(8,128)(2,1)} %broadcast_in_dim.28), calls=%async_computation | async-start | bytes 262144 | tf_op jit(solution)/shard_map/all_to_all | solution.py:41
  28.7 4.0 %collective-permute-start.1 = (bf16[256,512]{1,0:T(8,128)(2,1)S(1)}, bf16[256,512]{1,0:T(8,128)(2,1)S(1)}, u32[]{:S(2)}, u32[]{:S(2)}) collective-permute-start(bf16[256,512]{1,0:T(8,128)(2,1)S(1)} %pad_maximum_fusion.keys0_ref), channel_id=1, source_target_pairs={{0,2},{1,3},{2,4},{3,5},{4,6},{5,7},{6,8},{7,9},{8,10},{9,11},{10,... | collective-permute-start | bytes 786440 | tf_op jit(solution)/shard_map/ppermute | solution.py:37
  32.8 11.7 %all-to-all-done = bf16[32,16,128]{2,1,0:T(8,128)(2,1)S(1)} async-done(((bf16[32,16,128]{2,1,0:T(8,128)(2,1)}), bf16[32,16,128]{2,1,0:T(8,128)(2,1)S(1)}, u32[]{:S(2)}, u32[]{:S(2)}) %all-to-all-start) | async-done | bytes 131104 | tf_op jit(solution)/shard_map/all_to_all | solution.py:41
  45.7 9.3 %all-to-all-start.1 = ((bf16[16,8,4096]{2,1,0:T(8,128)(2,1)}), bf16[16,8,4096]{2,1,0:T(8,128)(2,1)S(1)}, u32[]{:S(2)}, u32[]{:S(2)}) async-start(bf16[16,8,4096]{2,1,0:T(8,128)(2,1)} %broadcast_in_dim.30), calls=%async_computation.1 | async-start | bytes 2097152 | tf_op jit(solution)/shard_map/all_to_all | solution.py:41
  55.0 2.4 %collective-permute-start.2 = (bf16[256,512]{1,0:T(8,128)(2,1)S(1)}, bf16[256,512]{1,0:T(8,128)(2,1)}, u32[]{:S(2)}, u32[]{:S(2)}) collective-permute-start(bf16[256,512]{1,0:T(8,128)(2,1)S(1)} %collective-permute-done.1.keys1_ref), channel_id=1, source_target_pairs={{0,2},{1,3},{2,4},{3,5},{4,6},{5,7},{6,8},{7,9},{8,10},{9,11},{10,... | collective-permute-start | bytes 786440 | tf_op jit(solution)/shard_map/ppermute | solution.py:37
  57.4 4.9 %collective-permute-done.2.keys2_ref = bf16[256,512]{1,0:T(8,128)(2,1)} collective-permute-done((bf16[256,512]{1,0:T(8,128)(2,1)S(1)}, bf16[256,512]{1,0:T(8,128)(2,1)}, u32[]{:S(2)}, u32[]{:S(2)}) %collective-permute-start.2) | collective-permute-done | bytes 262176 | tf_op jit(solution)/shard_map/ppermute | solution.py:37
  62.4 5.1 %collective-permute-start.3 = (bf16[256,512]{1,0:T(8,128)(2,1)}, bf16[256,512]{1,0:T(8,128)(2,1)S(1)}, u32[]{:S(2)}, u32[]{:S(2)}) collective-permute-start(bf16[256,512]{1,0:T(8,128)(2,1)} %collective-permute-done.2.keys2_ref), channel_id=1, source_target_pairs={{0,2},{1,3},{2,4},{3,5},{4,6},{5,7},{6,8},{7,9},{8,10},{9,11},{10,... | collective-permute-start | bytes 786440 | tf_op jit(solution)/shard_map/ppermute | solution.py:37
  67.9 10.8 %collective-permute-done.3.keys3_ref = bf16[256,512]{1,0:T(8,128)(2,1)S(1)} collective-permute-done((bf16[256,512]{1,0:T(8,128)(2,1)}, bf16[256,512]{1,0:T(8,128)(2,1)S(1)}, u32[]{:S(2)}, u32[]{:S(2)}) %collective-permute-start.3) | collective-permute-done | bytes 262176 | tf_op jit(solution)/shard_map/ppermute | solution.py:37
  78.7 1.2 copy-done.2
  82.1 16.2 %attention.1 = (bf16[1024,4096]{1,0:T(8,128)(2,1)}, f32[64,1024]{1,0:T(8,128)S(1)}) custom-call(bf16[128,4096]{1,0:T(8,128)(2,1)S(1)} %copy-done.6, bf16[128,4096]{1,0:T(8,128)(2,1)S(1)} %copy-done.2, bf16[64,512]{1,0:T(8,128)(2,1)S(1)} %copy-done.9, bf16[256,512]{1,0:T(8,128)(2,1)S(1)} %collective-permute-done.3.keys3_ref, ...), custom_call_target="tpu_custom_call" | custom-call | flops 3000000000 | bytes 12582912 | tf_op jit(solution)/shard_map/attention/pallas_call | solution.py:124
  99.1 1.3 collective-permute-start.4
  101.2 8.8 %collective-permute-start.7 = (bf16[64,128]{1,0:T(8,128)(2,1)S(1)}, bf16[64,128]{1,0:T(8,128)(2,1)S(1)}, u32[]{:S(2)}, u32[]{:S(2)}) collective-permute-start(bf16[64,128]{1,0:T(8,128)(2,1)S(1)} %lowrank.1), channel_id=1, source_target_pairs={{0,1},{1,2},{2,3},{3,4},{4,5},{5,6},{6,7},{7,8},{8,9},{9,10},{10,1... | collective-permute-start | bytes 49160 | tf_op jit(solution)/shard_map/ppermute | solution.py:37
  110.0 3.4 %collective-permute-done.4 = bf16[64,512]{1,0:T(8,128)(2,1)S(1)} collective-permute-done((bf16[64,512]{1,0:T(8,128)(2,1)}, bf16[64,512]{1,0:T(8,128)(2,1)S(1)}, u32[]{:S(2)}, u32[]{:S(2)}) %collective-permute-start.4) | collective-permute-done | bytes 65568 | tf_op jit(solution)/shard_map/ppermute | solution.py:37
  113.5 1.3 collective-permute-start.5
  114.8 5.8 %collective-permute-start.8 = (bf16[64,256]{1,0:T(8,128)(2,1)S(1)}, bf16[64,256]{1,0:T(8,128)(2,1)S(1)}, u32[]{:S(2)}, u32[]{:S(2)}) collective-permute-start(bf16[64,256]{1,0:T(8,128)(2,1)S(1)} %pad_maximum_fusion.3), channel_id=1, source_target_pairs={{0,2},{1,3},{2,4},{3,5},{4,6},{5,7},{6,8},{7,9},{8,10},{9,11},{10,... | collective-permute-start | bytes 98312 | tf_op jit(solution)/shard_map/ppermute | solution.py:37
  120.6 1.3 collective-permute-start.6
  122.0 10.2 %collective-permute-start.9 = (bf16[64,512]{1,0:T(8,128)(2,1)S(1)}, bf16[64,512]{1,0:T(8,128)(2,1)S(1)}, u32[]{:S(2)}, u32[]{:S(2)}) collective-permute-start(bf16[64,512]{1,0:T(8,128)(2,1)S(1)} %pad_maximum_fusion.2), channel_id=1, source_target_pairs={{0,4},{1,5},{2,6},{3,7},{4,8},{5,9},{6,10},{7,11},{8,12},{9,13},{1... | collective-permute-start | bytes 196616 | tf_op jit(solution)/shard_map/ppermute | solution.py:37
  132.2 1.3 collective-permute-done.9
  133.5 11.8 %mixed.1.up_ref = f32[64,512]{1,0:T(8,128)S(1)} custom-call(bf16[1024,4096]{1,0:T(8,128)(2,1)} %get-tuple-element.14.probs_ref, bf16[64,1024]{1,0:T(8,128)(2,1)S(1)} %pad_maximum_fusion.1.rank_ref, bf16[128,4096]{1,0:T(8,128)(2,1)S(1)} %copy-done.3), custom_call_target="tpu_custom_call" | custom-call | flops 600000000 | bytes 10485760 | tf_op jit(solution)/shard_map/mixed/pallas_call | solution.py:170
  145.8 27.3 %all_to_all.25.in_ref = bf16[16,8,4352]{2,1,0:T(8,128)(2,1)S(1)} all-to-all(bf16[16,8,4352]{2,1,0:T(8,128)(2,1)S(1)} %bitcast.15), channel_id=1, replica_groups=mesh['dp'=16,'fsdp'=32] {'dp'}, dimensions={0} | all-to-all | bytes 2228224 | tf_op jit(solution)/shard_map/all_to_all | solution.py:41
  173.2 47.2 %all_to_all.26.in_ref = f32[32,8,384]{2,1,0:T(8,128)S(1)} all-to-all(f32[32,8,384]{2,1,0:T(8,128)S(1)} %fold_dp.1), channel_id=1, replica_groups=mesh['dp'=16,'fsdp'=32] {'fsdp'}, dimensions={0} | all-to-all | bytes 786432 | tf_op jit(solution)/shard_map/all_to_all | solution.py:41
  220.5 10.5 %all_to_all.27.in_ref = f32[16,8,384]{2,1,0:T(8,128)S(1)} all-to-all(f32[16,8,384]{2,1,0:T(8,128)S(1)} %fold_fsdp.1), channel_id=1, replica_groups=mesh['dp'=16,'fsdp'=32] {'dp'}, dimensions={0} | all-to-all | bytes 393216 | tf_op jit(solution)/shard_map/all_to_all | solution.py:41
  (55 shorter events, 9.2 us)
Async XLA Ops:
  0.6 5.2 %copy-start = (bf16[256,64]{0,1:T(8,128)(2,1)S(1)}, bf16[256,64]{0,1:T(8,128)(2,1)}, u32[]{:S(2)}) copy-start(bf16[256,64]{0,1:T(8,128)(2,1)} %param.11) | copy-start | bytes 98308
  0.6 6.6 %collective-permute-start = (bf16[128,512]{1,0:T(8,128)(2,1)}, bf16[128,512]{1,0:T(8,128)(2,1)S(1)}, u32[]{:S(2)}, u32[]{:S(2)}) collective-permute-start(bf16[128,512]{1,0:T(8,128)(2,1)} %param.9), channel_id=1, source_target_pairs={{0,1},{1,2},{2,3},{3,4},{4,5},{5,6},{6,7},{7,8},{8,9},{9,10},{10,1... | collective-permute-start | bytes 393224 | tf_op jit(solution)/shard_map/ppermute | solution.py:37
  5.9 61.6 %copy-start.10 = (s32[1,128]{1,0:T(1,128)S(1)}, s32[1,128]{1,0:T(1,128)}, u32[]{:S(2)}) copy-start(s32[1,128]{1,0:T(1,128)} %param.10) | copy-start | bytes 1540
  8.9 69.9 %copy-start.9 = (bf16[64,512]{1,0:T(8,128)(2,1)S(1)}, bf16[64,512]{1,0:T(8,128)(2,1)}, u32[]{:S(2)}) copy-start(bf16[64,512]{1,0:T(8,128)(2,1)} %up_ref.1) | copy-start | bytes 196612
  8.9 35.6 %all-to-all-start = ((bf16[32,16,128]{2,1,0:T(8,128)(2,1)}), bf16[32,16,128]{2,1,0:T(8,128)(2,1)S(1)}, u32[]{:S(2)}, u32[]{:S(2)}) async-start(bf16[32,16,128]{2,1,0:T(8,128)(2,1)} %broadcast_in_dim.28), calls=%async_computation | async-start | bytes 262144 | tf_op jit(solution)/shard_map/all_to_all | solution.py:41
  28.7 15.7 %collective-permute-start.1 = (bf16[256,512]{1,0:T(8,128)(2,1)S(1)}, bf16[256,512]{1,0:T(8,128)(2,1)S(1)}, u32[]{:S(2)}, u32[]{:S(2)}) collective-permute-start(bf16[256,512]{1,0:T(8,128)(2,1)S(1)} %pad_maximum_fusion.keys0_ref), channel_id=1, source_target_pairs={{0,2},{1,3},{2,4},{3,5},{4,6},{5,7},{6,8},{7,9},{8,10},{9,11},{10,... | collective-permute-start | bytes 786440 | tf_op jit(solution)/shard_map/ppermute | solution.py:37
  44.5 23.0 %copy-start.7 = (bf16[256,512]{1,0:T(8,128)(2,1)}, bf16[256,512]{1,0:T(8,128)(2,1)S(1)}, u32[]{:S(2)}) copy-start(bf16[256,512]{1,0:T(8,128)(2,1)S(1)} %collective-permute-done.1.keys1_ref) | copy-start | bytes 786436
  45.7 54.7 %all-to-all-start.1 = ((bf16[16,8,4096]{2,1,0:T(8,128)(2,1)}), bf16[16,8,4096]{2,1,0:T(8,128)(2,1)S(1)}, u32[]{:S(2)}, u32[]{:S(2)}) async-start(bf16[16,8,4096]{2,1,0:T(8,128)(2,1)} %broadcast_in_dim.30), calls=%async_computation.1 | async-start | bytes 2097152 | tf_op jit(solution)/shard_map/all_to_all | solution.py:41
  55.0 7.4 %collective-permute-start.2 = (bf16[256,512]{1,0:T(8,128)(2,1)S(1)}, bf16[256,512]{1,0:T(8,128)(2,1)}, u32[]{:S(2)}, u32[]{:S(2)}) collective-permute-start(bf16[256,512]{1,0:T(8,128)(2,1)S(1)} %collective-permute-done.1.keys1_ref), channel_id=1, source_target_pairs={{0,2},{1,3},{2,4},{3,5},{4,6},{5,7},{6,8},{7,9},{8,10},{9,11},{10,... | collective-permute-start | bytes 786440 | tf_op jit(solution)/shard_map/ppermute | solution.py:37
  62.4 16.4 %collective-permute-start.3 = (bf16[256,512]{1,0:T(8,128)(2,1)}, bf16[256,512]{1,0:T(8,128)(2,1)S(1)}, u32[]{:S(2)}, u32[]{:S(2)}) collective-permute-start(bf16[256,512]{1,0:T(8,128)(2,1)} %collective-permute-done.2.keys2_ref), channel_id=1, source_target_pairs={{0,2},{1,3},{2,4},{3,5},{4,6},{5,7},{6,8},{7,9},{8,10},{9,11},{10,... | collective-permute-start | bytes 786440 | tf_op jit(solution)/shard_map/ppermute | solution.py:37
  67.9 32.5 %copy-start.1 = (bf16[128,8192]{1,0:T(8,128)(2,1)S(1)}, bf16[128,8192]{1,0:T(8,128)(2,1)}, u32[]{:S(2)}) copy-start(bf16[128,8192]{1,0:T(8,128)(2,1)} %hidden_ref.3) | copy-start | bytes 6291460
  78.7 1.2 copy-start.2
  80.0 1.2 copy-start.6
  81.2 0.9 copy-start.8
  98.3 0.7 copy-start.4
  99.1 14.4 %collective-permute-start.4 = (bf16[64,512]{1,0:T(8,128)(2,1)}, bf16[64,512]{1,0:T(8,128)(2,1)S(1)}, u32[]{:S(2)}, u32[]{:S(2)}) collective-permute-start(bf16[64,512]{1,0:T(8,128)(2,1)} %slice.51), channel_id=1, source_target_pairs={{4,0},{5,1},{6,2},{7,3},{8,4},{9,5},{10,6},{11,7},{12,8},{13,9},{1... | collective-permute-start | bytes 196616 | tf_op jit(solution)/shard_map/ppermute | solution.py:37
  100.4 13.1 %copy-start.5 = (f32[64,1024]{1,0:T(8,128)S(1)}, f32[64,1024]{1,0:T(8,128)}, u32[]{:S(2)}) copy-start(f32[64,1024]{1,0:T(8,128)} %copy-done.4) | copy-start | bytes 786436
  100.4 33.2 %copy-start.3 = (bf16[128,4096]{1,0:T(8,128)(2,1)S(1)}, bf16[128,4096]{1,0:T(8,128)(2,1)}, u32[]{:S(2)}) copy-start(bf16[128,4096]{1,0:T(8,128)(2,1)} %gradient_ref.3) | copy-start | bytes 3145732
  101.2 13.6 %collective-permute-start.7 = (bf16[64,128]{1,0:T(8,128)(2,1)S(1)}, bf16[64,128]{1,0:T(8,128)(2,1)S(1)}, u32[]{:S(2)}, u32[]{:S(2)}) collective-permute-start(bf16[64,128]{1,0:T(8,128)(2,1)S(1)} %lowrank.1), channel_id=1, source_target_pairs={{0,1},{1,2},{2,3},{3,4},{4,5},{5,6},{6,7},{7,8},{8,9},{9,10},{10,1... | collective-permute-start | bytes 49160 | tf_op jit(solution)/shard_map/ppermute | solution.py:37
  113.5 7.1 %collective-permute-start.5 = (bf16[64,256]{1,0:T(8,128)(2,1)S(1)}, bf16[64,256]{1,0:T(8,128)(2,1)S(1)}, u32[]{:S(2)}, u32[]{:S(2)}) collective-permute-start(bf16[64,256]{1,0:T(8,128)(2,1)S(1)} %slice.52), channel_id=1, source_target_pairs={{2,0},{3,1},{4,2},{5,3},{6,4},{7,5},{8,6},{9,7},{10,8},{11,9},{12,... | collective-permute-start | bytes 98312 | tf_op jit(solution)/shard_map/ppermute | solution.py:37
  114.8 7.1 %collective-permute-start.8 = (bf16[64,256]{1,0:T(8,128)(2,1)S(1)}, bf16[64,256]{1,0:T(8,128)(2,1)S(1)}, u32[]{:S(2)}, u32[]{:S(2)}) collective-permute-start(bf16[64,256]{1,0:T(8,128)(2,1)S(1)} %pad_maximum_fusion.3), channel_id=1, source_target_pairs={{0,2},{1,3},{2,4},{3,5},{4,6},{5,7},{6,8},{7,9},{8,10},{9,11},{10,... | collective-permute-start | bytes 98312 | tf_op jit(solution)/shard_map/ppermute | solution.py:37
  120.6 11.6 %collective-permute-start.6 = (bf16[64,128]{1,0:T(8,128)(2,1)S(1)}, bf16[64,128]{1,0:T(8,128)(2,1)S(1)}, u32[]{:S(2)}, u32[]{:S(2)}) collective-permute-start(bf16[64,128]{1,0:T(8,128)(2,1)S(1)} %slice.53), channel_id=1, source_target_pairs={{1,0},{2,1},{3,2},{4,3},{5,4},{6,5},{7,6},{8,7},{9,8},{10,9},{11,1... | collective-permute-start | bytes 49160 | tf_op jit(solution)/shard_map/ppermute | solution.py:37
  122.0 11.6 %collective-permute-start.9 = (bf16[64,512]{1,0:T(8,128)(2,1)S(1)}, bf16[64,512]{1,0:T(8,128)(2,1)S(1)}, u32[]{:S(2)}, u32[]{:S(2)}) collective-permute-start(bf16[64,512]{1,0:T(8,128)(2,1)S(1)} %pad_maximum_fusion.2), channel_id=1, source_target_pairs={{0,4},{1,5},{2,6},{3,7},{4,8},{5,9},{6,10},{7,11},{8,12},{9,13},{1... | collective-permute-start | bytes 196616 | tf_op jit(solution)/shard_map/ppermute | solution.py:37

commit v2 on v1

v2 whole, which is shorter than its diff:
```python
import functools
import math

import jax
import jax.numpy as jnp
from jax import lax
from jax.experimental import pallas as pl
from jax.experimental.pallas import tpu as pltpu
from jax.sharding import PartitionSpec as P

QUERY_HEADS = 32
KEY_HEADS = 4
HEAD_SIZE = 128
ADAPTER_RANK = 64
SPAN = 8
TOKENS = 128
WINDOW = SPAN * TOKENS
N_DP = 16
N_FSDP = 32
MODEL_WIDTH = 8192
VMEM_LIMIT = 20 * 1024 * 1024
BF16 = jnp.bfloat16
F32 = jnp.float32
NT = (((1,), (1,)), ((), ()))


def whole(*arrays):
    return [pl.BlockSpec(memory_space=pltpu.VMEM) for _ in arrays]


def params():
    return pltpu.CompilerParams(vmem_limit_bytes=VMEM_LIMIT)


def from_behind(block, distance):
    route = [(i, i + distance) for i in range(N_FSDP) if 0 <= i + distance < N_FSDP]
    return lax.ppermute(block, "fsdp", route)


def exchange(slots, axis):
    return lax.all_to_all(slots, axis, 0, 0, tiled=True)


def lowrank_kernel(weight_ref, hidden_ref, out_ref):
    total = jnp.zeros((ADAPTER_RANK, TOKENS), F32)
    for f in range(N_FSDP):
        rows = jnp.concatenate(
            [weight_ref[half, :, f * 128 : f * 128 + 128] for half in range(2)], axis=1
        )
        total += lax.dot_general(
            rows, hidden_ref[:, f * 256 : f * 256 + 256], NT, preferred_element_type=F32
        )
    out_ref[...] = total.astype(BF16)


def score_kernel(query_ref, keys_ref, bias_ref, weights_ref, stats_ref):
    factor = math.log2(math.e) / math.sqrt(HEAD_SIZE)

    def key_head(g, carry):
        keys = keys_ref[:, pl.ds(pl.multiple_of(g * HEAD_SIZE, HEAD_SIZE), HEAD_SIZE)]
        for m in range(QUERY_HEADS // KEY_HEADS):
            lanes = pl.ds(pl.multiple_of((g * 8 + m) * 128, 128), 128)
            scores = lax.dot_general(keys, query_ref[:, lanes], NT, preferred_element_type=F32)
            scores = scores + bias_ref[...]
            top = jnp.maximum(jnp.max(scores, axis=0, keepdims=True), -1e30) * factor
            weights = jnp.exp2(scores * factor - top)
            stats_ref[0:1, lanes] = top
            stats_ref[1:2, lanes] = jnp.sum(weights, axis=0, keepdims=True)
            weights_ref[:, lanes] = weights.astype(BF16)
        return carry

    lax.fori_loop(0, KEY_HEADS, key_head, 0)


def score(queries, keys, bias):
    return plain(
        score_kernel,
        "score",
        (
            jax.ShapeDtypeStruct((2 * TOKENS, QUERY_HEADS * TOKENS), BF16),
            jax.ShapeDtypeStruct((2, QUERY_HEADS * TOKENS), F32),
        ),
        queries,
        keys,
        bias,
    )


def reached_kernel(gradient_ref, up_ref, out_ref):
    def key_head(g, carry):
        up = up_ref[:, pl.ds(pl.multiple_of(g * HEAD_SIZE, HEAD_SIZE), HEAD_SIZE)]
        for m in range(QUERY_HEADS // KEY_HEADS):
            lanes = pl.ds(pl.multiple_of((g * 8 + m) * 128, 128), 128)
            out_ref[:, lanes] = lax.dot_general(
                up, gradient_ref[:, lanes], NT, preferred_element_type=F32
            )
        return carry

    lax.fori_loop(0, KEY_HEADS, key_head, 0)


def sums_of(weights_ref, scale, reached):
    shares = (reached.astype(BF16).astype(F32) * scale).astype(BF16)
    return lax.dot_general(weights_ref[...], shares, NT, preferred_element_type=F32).T


def far_kernel(w3_ref, w2_ref, s3_ref, s2_ref, s1_ref, s0_ref, reached_ref, far_ref, scale_ref):
    stats = [ref[...] for ref in (s3_ref, s2_ref, s1_ref, s0_ref)]
    top = stats[0][0:1]
    for s in stats[1:]:
        top = jnp.maximum(top, s[0:1])
    parts = [jnp.exp2(s[0:1] - top) for s in stats]
    inverse = 1.0 / sum(part * s[1:2] for part, s in zip(parts, stats))
    scales = [part * inverse for part in parts]
    for i, scale in enumerate(scales):
        scale_ref[i : i + 1, :] = scale
    reached = reached_ref[...]
    far_ref[:, :256] = sums_of(w3_ref, scales[0], reached).astype(BF16)
    far_ref[:, 256:] = sums_of(w2_ref, scales[1], reached).astype(BF16)


def near_kernel(w1_ref, w0_ref, scale_ref, reached_ref, near_ref):
    reached = reached_ref[...]
    near_ref[:, :256] = sums_of(w1_ref, scale_ref[2:3, :], reached)
    near_ref[:, 256:] = sums_of(w0_ref, scale_ref[3:4, :], reached)


def mixed_kernel(first, w3_ref, w2_ref, w1_ref, w0_ref, scale_ref, rank_ref, gradient_ref, out_ref):
    for g in range(2):
        share = jnp.zeros((ADAPTER_RANK, HEAD_SIZE), F32)
        for m in range(QUERY_HEADS // KEY_HEADS):
            h = (first + g) * 8 + m
            lanes = slice(h * 128, h * 128 + 128)
            mixed = jnp.zeros((ADAPTER_RANK, TOKENS), F32)
            for i, ref in enumerate((w3_ref, w2_ref, w1_ref, w0_ref)):
                rank = rank_ref[:, i * 256 : i * 256 + 256]
                part = jnp.dot(rank, ref[:, lanes], preferred_element_type=F32)
                mixed += part * scale_ref[i : i + 1, lanes]
            share += jnp.dot(
                mixed.astype(BF16), gradient_ref[:, lanes], preferred_element_type=F32
            )
        out_ref[:, g * 128 : g * 128 + 128] = share


DOWN = N_FSDP * 128
LANES = DOWN + 256


def shares_kernel(key_ref, hidden_ref, up0_ref, up1_ref, out_ref):
    for f in range(N_FSDP):
        product = jnp.dot(
            key_ref[...], hidden_ref[:, f * 256 : f * 256 + 256], preferred_element_type=F32
        ).astype(BF16)
        for half in range(2):
            out_ref[half, :, f * 128 : f * 128 + 128] = product[:, half * 128 : half * 128 + 128]
    for half, up_ref in enumerate((up0_ref, up1_ref)):
        out_ref[half, :, DOWN:] = up_ref[...].astype(BF16)


def fold_dp_kernel(in_ref, out_ref):
    def total(columns):
        return sum(in_ref[d, :, columns].astype(F32) for d in range(N_DP))

    up = total(slice(DOWN, LANES)).astype(BF16)
    for f in range(N_FSDP):
        out_ref[f, :, :128] = total(slice(f * 128, f * 128 + 128)).astype(BF16)
        out_ref[f, :, 128:] = up


def fold_fsdp_kernel(in_ref, out_ref):
    total = sum(in_ref[f].astype(F32) for f in range(N_FSDP))
    for d in range(N_DP):
        out_ref[d] = total


def spread_kernel(in_ref, down_ref, up_ref):
    for half in range(2):
        for part in range(8):
            rows = slice(part * 8, part * 8 + 8)
            block = in_ref[half * 8 + part]
            down_ref[rows, half * 128 : half * 128 + 128] = block[:, :128]
            up_ref[rows, half * 256 : half * 256 + 256] = block[:, 128:]


def plain(kernel, name, out_shape, *arrays):
    return pl.pallas_call(
        kernel,
        in_specs=whole(*arrays),
        out_specs=jax.tree.map(lambda _: pl.BlockSpec(memory_space=pltpu.VMEM), out_shape),
        out_shape=out_shape,
        compiler_params=params(),
        cost_estimate=pl.CostEstimate(flops=10**10, bytes_accessed=2**27, transcendentals=0),
        name=name,
    )(*arrays)


def local(
    hidden, queries, keys, document_numbers, adapter_down_weight, adapter_up_weight, output_gradient
):
    position = lax.axis_index("fsdp")
    member = lax.axis_index("dp")
    half, part = member // 8, member % 8

    keys1, keys2, keys3 = [from_behind(keys, distance) for distance in (1, 2, 3)]
    weight_slice = lax.dynamic_slice(adapter_down_weight.T, (part * 8, half * 128), (8, 128))
    docs_row = document_numbers.reshape(1, TOKENS).astype(BF16)
    slot = jnp.concatenate([weight_slice, docs_row, jnp.zeros((7, 128), BF16)], axis=0)
    slots = jnp.broadcast_to(slot[None], (N_FSDP, 16, 128))
    row_parts = exchange(slots, "fsdp")
    pair0 = jnp.concatenate([keys1, keys], axis=0)
    pair1 = jnp.concatenate([keys3, keys2], axis=0)
    pair2 = from_behind(pair1, 2)
    weight_part = row_parts[:, :8].transpose(1, 0, 2).reshape(1, 8, DOWN)
    docs = row_parts[:, 8].astype(jnp.int32)
    weight_slots = jnp.broadcast_to(weight_part, (N_DP, 8, DOWN))
    weight = exchange(weight_slots, "dp").reshape(2, ADAPTER_RANK, DOWN)
    pair2 = lax.optimization_barrier((pair2, weight_slots))[0]
    pair3 = from_behind(pair2, 2)

    padded = jnp.concatenate([jnp.full((SPAN - 1, TOKENS), -1, jnp.int32), docs], axis=0)
    window_docs = lax.dynamic_slice(padded, (position, 0), (SPAN, TOKENS)).reshape(WINDOW)
    own_docs = document_numbers.reshape(TOKENS)
    key_pos = jnp.arange(WINDOW, dtype=jnp.int32) - (SPAN - 1) * TOKENS
    visible = (window_docs[:, None] == own_docs[None, :]) & (
        key_pos[:, None] <= jnp.arange(TOKENS, dtype=jnp.int32)[None, :]
    )
    bias = jnp.where(visible, 0.0, -jnp.inf).astype(F32)
    biases = [bias[i * 256 : i * 256 + 256] for i in range(4)]

    reached = plain(
        reached_kernel,
        "reached",
        jax.ShapeDtypeStruct((ADAPTER_RANK, QUERY_HEADS * TOKENS), F32),
        output_gradient,
        adapter_up_weight,
    )
    w0, s0 = score(queries, pair0, biases[3])
    w1, s1 = score(queries, pair1, biases[2])
    pair2, w1 = lax.optimization_barrier((pair2, w1))
    w2, s2 = score(queries, pair2, biases[1])
    rank = plain(
        lowrank_kernel, "lowrank", jax.ShapeDtypeStruct((ADAPTER_RANK, TOKENS), BF16), weight, hidden
    )
    rank1 = jnp.concatenate([from_behind(rank, 1), rank], axis=1)
    pair3, w2, rank = lax.optimization_barrier((pair3, w2, rank))
    w3, s3 = score(queries, pair3, biases[0])
    w3, rank1 = lax.optimization_barrier((w3, rank1))
    rank2 = jnp.concatenate([from_behind(rank1, 2), rank1], axis=1)
    far, scale = plain(
        far_kernel,
        "far",
        (
            jax.ShapeDtypeStruct((ADAPTER_RANK, WINDOW // 2), BF16),
            jax.ShapeDtypeStruct((4, QUERY_HEADS * TOKENS), F32),
        ),
        w3,
        w2,
        s3,
        s2,
        s1,
        s0,
        reached,
    )
    near = plain(
        near_kernel,
        "near",
        jax.ShapeDtypeStruct((ADAPTER_RANK, WINDOW // 2), F32),
        w1,
        w0,
        scale,
        reached,
    )
    came = from_behind(far, -4)
    came, rank2 = lax.optimization_barrier((came, rank2))
    near = near + came.astype(F32)
    rank3 = jnp.concatenate([from_behind(rank2, 4), rank2], axis=1)
    came = from_behind(near[:, :256], -2)
    came, rank3 = lax.optimization_barrier((came, rank3))
    near = near[:, 256:] + came
    came = from_behind(near[:, :128], -1)
    ups = [
        plain(
            functools.partial(mixed_kernel, first),
            "mixed",
            jax.ShapeDtypeStruct((ADAPTER_RANK, 2 * HEAD_SIZE), F32),
            w3,
            w2,
            w1,
            w0,
            scale,
            rank3,
            output_gradient,
        )
        for first in (0, 2)
    ]
    key_grad = (near[:, 128:] + came).astype(BF16)

    shares = plain(
        shares_kernel,
        "shares",
        jax.ShapeDtypeStruct((2, ADAPTER_RANK, LANES), BF16),
        key_grad,
        hidden,
        *ups,
    )
    shares = exchange(shares.reshape(N_DP, 8, LANES), "dp")
    shares = plain(
        fold_dp_kernel, "fold_dp", jax.ShapeDtypeStruct((N_FSDP, 8, 384), BF16), shares
    )
    shares = exchange(shares, "fsdp")
    shares = plain(
        fold_fsdp_kernel, "fold_fsdp", jax.ShapeDtypeStruct((N_DP, 8, 384), F32), shares
    )
    shares = exchange(shares, "dp")
    down, up = plain(
        spread_kernel,
        "spread",
        (
            jax.ShapeDtypeStruct((ADAPTER_RANK, 256), F32),
            jax.ShapeDtypeStruct((ADAPTER_RANK, KEY_HEADS * HEAD_SIZE), F32),
        ),
        shares,
    )
    return (down.T, up)


def solution(mesh):
    in_specs = (
        P(("dp", "fsdp"), None),
        P(("dp", "fsdp"), None),
        P(("dp", "fsdp"), None),
        P("dp", "fsdp"),
        P("fsdp", None),
        P(),
        P(("dp", "fsdp"), None),
    )
    out_specs = (P("fsdp", None), P())
    return jax.shard_map(local, mesh=mesh, in_specs=in_specs, out_specs=out_specs, check_vma=False)
```

time: 233 us -> 180 us (0.77)
  blocking collectives: 85 us -> 68.5 us
  starting transfers between devices: 73.8 us -> 57.8 us
  waiting for transfers between devices: 33.5 us -> 21 us
  Pallas kernels: 30.2 us -> 19.3 us
  local copies, waits for them, and re-layouts: 6.13 us -> 10.7 us
    pallas_call x2 -> x0, Pallas kernels: 28 us -> none  [the longest x1 16.2 us: attention(): pl.pallas_call(attention_kernel, grid=(PAIRS,), in_specs=[pair, pair, pl....]
    pallas_call x5 -> x14, Pallas kernels: 2.15 us -> 19.3 us  [plain(): pl.pallas_call(kernel, in_specs=whole(*arrays), out_specs=jax.tree.map(la...]
    all_to_all x3, blocking collectives: 85 us -> 68.5 us  [exchange(): return lax.all_to_all(slots, axis, 0, 0, tiled=True)]
    ppermute x10 -> x11, waiting for transfers between devices: 21.9 us -> 10.2 us  [from_behind(): return lax.ppermute(block, 'fsdp', route)]
    all_to_all x2, starting transfers between devices: 29.2 us -> 19.3 us  [exchange(): return lax.all_to_all(slots, axis, 0, 0, tiled=True)]
    ppermute x10 -> x11, starting transfers between devices: 44.6 us -> 38.5 us  [from_behind(): return lax.ppermute(block, 'fsdp', route)]
    unnamed x23 -> x36, local copies, waits for them, and re-layouts: 3.49 us -> 8.74 us
  transfers between devices with their start and end apart: 12 -> 13, of which waited for: 6 -> 4; matrix products, arithmetic and copies ran while one was open for 1% -> 2% of each run, Pallas kernels for 7% -> 9%
where the time goes in v2:
time: 180 us
  blocking collectives  68.5 us (38%)
  starting transfers between devices  57.8 us (32%)
  waiting for transfers between devices  21 us (12%)
  Pallas kernels  19.3 us (11%)
  local copies, waits for them, and re-layouts  10.7 us (6%)
    all_to_all x3, blocking collectives, exchange(): return lax.all_to_all(slots, axis, 0, 0, tiled=True)  68.5 us
    ppermute x11, starting transfers between devices, from_behind(): return lax.ppermute(block, 'fsdp', route)  38.5 us
    all_to_all x2, starting transfers between devices, exchange(): return lax.all_to_all(slots, axis, 0, 0, tiled=True)  19.3 us
    pallas_call x14, Pallas kernels, plain(): pl.pallas_call(kernel, in_specs=whole(*arrays), out_specs=jax.tree.map(la...  19.3 us
    all_to_all x2, waiting for transfers between devices, exchange(): return lax.all_to_all(slots, axis, 0, 0, tiled=True)  10.8 us
    ppermute x11, waiting for transfers between devices, from_behind(): return lax.ppermute(block, 'fsdp', route)  10.2 us
    unnamed x36, local copies, waits for them, and re-layouts  8.74 us
  transfers between devices with their start and end apart: 13, of which 4 were waited for; matrix products, arithmetic and copies ran while one was open for 2% of the time, Pallas kernels for 9%

profile of v2, /device:TPU:1, one launch (start us, length us, event | category | flops | bytes accessed | tf_op | source)
XLA Modules:
  0.0 179.6 jit_solution(12803211722909293187)
XLA Ops:
  0.6 7.1 %collective-permute-start = (bf16[128,512]{1,0:T(8,128)(2,1)}, bf16[128,512]{1,0:T(8,128)(2,1)S(1)}, u32[]{:S(2)}, u32[]{:S(2)}) collective-permute-start(bf16[128,512]{1,0:T(8,128)(2,1)} %param.9), channel_id=1, source_target_pairs={{0,3},{1,4},{2,5},{3,6},{4,7},{5,8},{6,9},{7,10},{8,11},{9,12},{10... | collective-permute-start | bytes 393224 | tf_op jit(solution)/shard_map/ppermute | solution.py:37
  7.7 6.1 %collective-permute-start.1 = (bf16[128,512]{1,0:T(8,128)(2,1)}, bf16[128,512]{1,0:T(8,128)(2,1)S(1)}, u32[]{:S(2)}, u32[]{:S(2)}) collective-permute-start(bf16[128,512]{1,0:T(8,128)(2,1)} %param.9), channel_id=1, source_target_pairs={{0,2},{1,3},{2,4},{3,5},{4,6},{5,7},{6,8},{7,9},{8,10},{9,11},{10,... | collective-permute-start | bytes 393224 | tf_op jit(solution)/shard_map/ppermute | solution.py:37
  13.9 3.5 %collective-permute-start.3 = (bf16[128,512]{1,0:T(8,128)(2,1)}, bf16[128,512]{1,0:T(8,128)(2,1)S(1)}, u32[]{:S(2)}, u32[]{:S(2)}) collective-permute-start(bf16[128,512]{1,0:T(8,128)(2,1)} %param.9), channel_id=1, source_target_pairs={{0,1},{1,2},{2,3},{3,4},{4,5},{5,6},{6,7},{7,8},{8,9},{9,10},{10,1... | collective-permute-start | bytes 393224 | tf_op jit(solution)/shard_map/ppermute | solution.py:37
  18.9 11.2 %all-to-all-start = ((bf16[32,16,128]{2,1,0:T(8,128)(2,1)}), bf16[32,16,128]{2,1,0:T(8,128)(2,1)S(1)}, u32[]{:S(2)}, u32[]{:S(2)}) async-start(bf16[32,16,128]{2,1,0:T(8,128)(2,1)} %broadcast_in_dim.28), calls=%async_computation | async-start | bytes 262144 | tf_op jit(solution)/shard_map/all_to_all | solution.py:41
  34.4 4.0 %collective-permute-start.2 = (bf16[256,512]{1,0:T(8,128)(2,1)S(1)}, bf16[256,512]{1,0:T(8,128)(2,1)S(1)}, u32[]{:S(2)}, u32[]{:S(2)}) collective-permute-start(bf16[256,512]{1,0:T(8,128)(2,1)S(1)} %constant_dynamic-update-slice_fusion.keys_ref), channel_id=1, source_target_pairs={{0,2},{1,3},{2,4},{3,5},{4,6},{5,7},{6,8},{7,9},{8,10},{9,11},{10,... | collective-permute-start | bytes 786440 | tf_op jit(solution)/shard_map/ppermute | solution.py:37
  38.5 7.4 %all-to-all-done = bf16[32,16,128]{2,1,0:T(8,128)(2,1)S(1)} async-done(((bf16[32,16,128]{2,1,0:T(8,128)(2,1)}), bf16[32,16,128]{2,1,0:T(8,128)(2,1)S(1)}, u32[]{:S(2)}, u32[]{:S(2)}) %all-to-all-start) | async-done | bytes 131104 | tf_op jit(solution)/shard_map/all_to_all | solution.py:41
  47.1 8.1 %all-to-all-start.1 = ((bf16[16,8,4096]{2,1,0:T(8,128)(2,1)}), bf16[16,8,4096]{2,1,0:T(8,128)(2,1)S(1)}, u32[]{:S(2)}, u32[]{:S(2)}) async-start(bf16[16,8,4096]{2,1,0:T(8,128)(2,1)} %broadcast_in_dim.30), calls=%async_computation.1 | async-start | bytes 2097152 | tf_op jit(solution)/shard_map/all_to_all | solution.py:41
  55.6 1.9 %collective-permute-start.4 = (bf16[256,512]{1,0:T(8,128)(2,1)S(1)}, bf16[256,512]{1,0:T(8,128)(2,1)S(1)}, u32[]{:S(2)}, u32[]{:S(2)}) collective-permute-start(bf16[256,512]{1,0:T(8,128)(2,1)S(1)} %collective-permute-done.2.keys_ref), channel_id=1, source_target_pairs={{0,2},{1,3},{2,4},{3,5},{4,6},{5,7},{6,8},{7,9},{8,10},{9,11},{10,... | collective-permute-start | bytes 786440 | tf_op jit(solution)/shard_map/ppermute | solution.py:37
  57.6 2.1 %score.4 = (bf16[256,4096]{1,0:T(8,128)(2,1)S(1)}, f32[2,4096]{1,0:T(2,128)S(1)}) custom-call(bf16[128,4096]{1,0:T(8,128)(2,1)S(1)} %copy-done.3, bf16[256,512]{1,0:T(8,128)(2,1)S(1)} %constant_dynamic-update-slice_fusion.keys_ref, f32[256,128]{1,0:T(8,128)S(1)} %get-tuple-element.51.bias_ref), custom_call_target="tpu_custom_call" | custom-call | flops 10000000000 | bytes 134217728 | tf_op jit(solution)/shard_map/score/pallas_call | solution.py:186
  61.1 2.1 %score.5 = (bf16[256,4096]{1,0:T(8,128)(2,1)S(1)}, f32[2,4096]{1,0:T(2,128)S(1)}) custom-call(bf16[128,4096]{1,0:T(8,128)(2,1)S(1)} %copy-done.3, bf16[256,512]{1,0:T(8,128)(2,1)S(1)} %pad_maximum_fusion.keys_ref, f32[256,128]{1,0:T(8,128)S(1)} %get-tuple-element.50.bias_ref), custom_call_target="tpu_custom_call" | custom-call | flops 10000000000 | bytes 134217728 | tf_op jit(solution)/shard_map/score/pallas_call | solution.py:186
  64.5 2.1 %score.6 = (bf16[256,4096]{1,0:T(8,128)(2,1)S(1)}, f32[2,4096]{1,0:T(2,128)S(1)}) custom-call(bf16[128,4096]{1,0:T(8,128)(2,1)S(1)} %copy-done.3, bf16[256,512]{1,0:T(8,128)(2,1)S(1)} %collective-permute-done.2.keys_ref, f32[256,128]{1,0:T(8,128)S(1)} %get-tuple-element.49.bias_ref), custom_call_target="tpu_custom_call" | custom-call | flops 10000000000 | bytes 134217728 | tf_op jit(solution)/shard_map/score/pallas_call | solution.py:186
  68.1 3.4 %all-to-all-done.1 = bf16[16,8,4096]{2,1,0:T(8,128)(2,1)S(1)} async-done(((bf16[16,8,4096]{2,1,0:T(8,128)(2,1)}), bf16[16,8,4096]{2,1,0:T(8,128)(2,1)S(1)}, u32[]{:S(2)}, u32[]{:S(2)}) %all-to-all-start.1) | async-done | bytes 1048608 | tf_op jit(solution)/shard_map/all_to_all | solution.py:41
  71.5 1.6 copy-done.1
  73.9 4.1 %collective-permute-start.5 = (bf16[64,128]{1,0:T(8,128)(2,1)S(1)}, bf16[64,128]{1,0:T(8,128)(2,1)S(1)}, u32[]{:S(2)}, u32[]{:S(2)}) collective-permute-start(bf16[64,128]{1,0:T(8,128)(2,1)S(1)} %lowrank.1), channel_id=1, source_target_pairs={{0,1},{1,2},{2,3},{3,4},{4,5},{5,6},{6,7},{7,8},{8,9},{9,10},{10,1... | collective-permute-start | bytes 49160 | tf_op jit(solution)/shard_map/ppermute | solution.py:37
  78.0 2.1 %score.7 = (bf16[256,4096]{1,0:T(8,128)(2,1)S(1)}, f32[2,4096]{1,0:T(2,128)S(1)}) custom-call(bf16[128,4096]{1,0:T(8,128)(2,1)S(1)} %copy-done.3, bf16[256,512]{1,0:T(8,128)(2,1)S(1)} %collective-permute-done.4.keys_ref, f32[256,128]{1,0:T(8,128)S(1)} %get-tuple-element.48.bias_ref), custom_call_target="tpu_custom_call" | custom-call | flops 10000000000 | bytes 134217728 | tf_op jit(solution)/shard_map/score/pallas_call | solution.py:186
  82.8 2.0 %collective-permute-start.7 = (bf16[64,256]{1,0:T(8,128)(2,1)S(1)}, bf16[64,256]{1,0:T(8,128)(2,1)S(1)}, u32[]{:S(2)}, u32[]{:S(2)}) collective-permute-start(bf16[64,256]{1,0:T(8,128)(2,1)S(1)} %pad_maximum_fusion.3), channel_id=1, source_target_pairs={{0,2},{1,3},{2,4},{3,5},{4,6},{5,7},{6,8},{7,9},{8,10},{9,11},{10,... | collective-permute-start | bytes 98312 | tf_op jit(solution)/shard_map/ppermute | solution.py:37
  86.2 5.5 %collective-permute-done.6 = bf16[64,512]{1,0:T(8,128)(2,1)S(1)} collective-permute-done((bf16[64,512]{1,0:T(8,128)(2,1)S(1)}, bf16[64,512]{1,0:T(8,128)(2,1)S(1)}, u32[]{:S(2)}, u32[]{:S(2)}) %collective-permute-start.6) | collective-permute-done | bytes 65568 | tf_op jit(solution)/shard_map/ppermute | solution.py:37
  91.7 5.8 %collective-permute-start.9 = (bf16[64,512]{1,0:T(8,128)(2,1)S(1)}, bf16[64,512]{1,0:T(8,128)(2,1)S(1)}, u32[]{:S(2)}, u32[]{:S(2)}) collective-permute-start(bf16[64,512]{1,0:T(8,128)(2,1)S(1)} %pad_maximum_fusion.2), channel_id=1, source_target_pairs={{0,4},{1,5},{2,6},{3,7},{4,8},{5,9},{6,10},{7,11},{8,12},{9,13},{1... | collective-permute-start | bytes 196616 | tf_op jit(solution)/shard_map/ppermute | solution.py:37
  98.9 4.7 %collective-permute-done.8 = f32[64,256]{1,0:T(8,128)S(1)} collective-permute-done((f32[64,256]{1,0:T(8,128)S(1)}, f32[64,256]{1,0:T(8,128)S(1)}, u32[]{:S(2)}, u32[]{:S(2)}) %collective-permute-start.8) | collective-permute-done | bytes 65568 | tf_op jit(solution)/shard_map/ppermute | solution.py:37
  104.9 2.4 %mixed.2.up0_ref = f32[64,256]{1,0:T(8,128)S(1)} custom-call(bf16[256,4096]{1,0:T(8,128)(2,1)S(1)} %get-tuple-element.33.w3_ref, bf16[256,4096]{1,0:T(8,128)(2,1)S(1)} %copy-done.12, bf16[256,4096]{1,0:T(8,128)(2,1)S(1)} %copy-done.8, bf16[256,4096]{1,0:T(8,128)(2,1)S(1)} %copy-done.10, f32[4,4096]{1,0:T(4,128)S(1)} %get-tuple-element.39.scale_ref, ...), custom_call_target="tpu_custom_call" | custom-call | flops 10000000000 | bytes 134217728 | tf_op jit(solution)/shard_map/mixed/pallas_call | solution.py:186
  107.3 2.4 %mixed.3.up1_ref = f32[64,256]{1,0:T(8,128)S(1)} custom-call(bf16[256,4096]{1,0:T(8,128)(2,1)S(1)} %get-tuple-element.33.w3_ref, bf16[256,4096]{1,0:T(8,128)(2,1)S(1)} %copy-done.12, bf16[256,4096]{1,0:T(8,128)(2,1)S(1)} %copy-done.8, bf16[256,4096]{1,0:T(8,128)(2,1)S(1)} %copy-done.10, f32[4,4096]{1,0:T(4,128)S(1)} %get-tuple-element.39.scale_ref, ...), custom_call_target="tpu_custom_call" | custom-call | flops 10000000000 | bytes 134217728 | tf_op jit(solution)/shard_map/mixed/pallas_call | solution.py:186
  110.2 25.6 %all_to_all.25.in_ref = bf16[16,8,4352]{2,1,0:T(8,128)(2,1)S(1)} all-to-all(bf16[16,8,4352]{2,1,0:T(8,128)(2,1)S(1)} %bitcast.15), channel_id=1, replica_groups=mesh['dp'=16,'fsdp'=32] {'dp'}, dimensions={0} | all-to-all | bytes 2228224 | tf_op jit(solution)/shard_map/all_to_all | solution.py:41
  136.0 30.8 %all_to_all.26.in_ref = bf16[32,8,384]{2,1,0:T(8,128)(2,1)S(1)} all-to-all(bf16[32,8,384]{2,1,0:T(8,128)(2,1)S(1)} %fold_dp.1), channel_id=1, replica_groups=mesh['dp'=16,'fsdp'=32] {'fsdp'}, dimensions={0} | all-to-all | bytes 393216 | tf_op jit(solution)/shard_map/all_to_all | solution.py:41
  166.8 12.0 %all_to_all.27.in_ref = f32[16,8,384]{2,1,0:T(8,128)S(1)} all-to-all(f32[16,8,384]{2,1,0:T(8,128)S(1)} %fold_fsdp.1), channel_id=1, replica_groups=mesh['dp'=16,'fsdp'=32] {'dp'}, dimensions={0} | all-to-all | bytes 393216 | tf_op jit(solution)/shard_map/all_to_all | solution.py:41
  (78 shorter events, 20.2 us)
Async XLA Ops:
  0.6 17.6 %copy-start = (bf16[256,64]{0,1:T(8,128)(2,1)S(1)}, bf16[256,64]{0,1:T(8,128)(2,1)}, u32[]{:S(2)}) copy-start(bf16[256,64]{0,1:T(8,128)(2,1)} %param.11) | copy-start | bytes 98308
  0.6 33.7 %collective-permute-start = (bf16[128,512]{1,0:T(8,128)(2,1)}, bf16[128,512]{1,0:T(8,128)(2,1)S(1)}, u32[]{:S(2)}, u32[]{:S(2)}) collective-permute-start(bf16[128,512]{1,0:T(8,128)(2,1)} %param.9), channel_id=1, source_target_pairs={{0,3},{1,4},{2,5},{3,6},{4,7},{5,8},{6,9},{7,10},{8,11},{9,12},{10... | collective-permute-start | bytes 393224 | tf_op jit(solution)/shard_map/ppermute | solution.py:37
  7.7 26.6 %collective-permute-start.1 = (bf16[128,512]{1,0:T(8,128)(2,1)}, bf16[128,512]{1,0:T(8,128)(2,1)S(1)}, u32[]{:S(2)}, u32[]{:S(2)}) collective-permute-start(bf16[128,512]{1,0:T(8,128)(2,1)} %param.9), channel_id=1, source_target_pairs={{0,2},{1,3},{2,4},{3,5},{4,6},{5,7},{6,8},{7,9},{8,10},{9,11},{10,... | collective-permute-start | bytes 393224 | tf_op jit(solution)/shard_map/ppermute | solution.py:37
  13.9 24.6 %collective-permute-start.3 = (bf16[128,512]{1,0:T(8,128)(2,1)}, bf16[128,512]{1,0:T(8,128)(2,1)S(1)}, u32[]{:S(2)}, u32[]{:S(2)}) collective-permute-start(bf16[128,512]{1,0:T(8,128)(2,1)} %param.9), channel_id=1, source_target_pairs={{0,1},{1,2},{2,3},{3,4},{4,5},{5,6},{6,7},{7,8},{8,9},{9,10},{10,1... | collective-permute-start | bytes 393224 | tf_op jit(solution)/shard_map/ppermute | solution.py:37
  18.9 27.0 %all-to-all-start = ((bf16[32,16,128]{2,1,0:T(8,128)(2,1)}), bf16[32,16,128]{2,1,0:T(8,128)(2,1)S(1)}, u32[]{:S(2)}, u32[]{:S(2)}) async-start(bf16[32,16,128]{2,1,0:T(8,128)(2,1)} %broadcast_in_dim.28), calls=%async_computation | async-start | bytes 262144 | tf_op jit(solution)/shard_map/all_to_all | solution.py:41
  32.2 6.2 %copy-start.15 = (bf16[128,512]{1,0:T(8,128)(2,1)S(1)}, bf16[128,512]{1,0:T(8,128)(2,1)}, u32[]{:S(2)}) copy-start(bf16[128,512]{1,0:T(8,128)(2,1)} %param.9) | copy-start | bytes 393220
  34.4 20.9 %copy-start.16 = (s32[1,128]{1,0:T(1,128)S(1)}, s32[1,128]{1,0:T(1,128)}, u32[]{:S(2)}) copy-start(s32[1,128]{1,0:T(1,128)} %param.10) | copy-start | bytes 1540
  34.4 20.8 %collective-permute-start.2 = (bf16[256,512]{1,0:T(8,128)(2,1)S(1)}, bf16[256,512]{1,0:T(8,128)(2,1)S(1)}, u32[]{:S(2)}, u32[]{:S(2)}) collective-permute-start(bf16[256,512]{1,0:T(8,128)(2,1)S(1)} %constant_dynamic-update-slice_fusion.keys_ref), channel_id=1, source_target_pairs={{0,2},{1,3},{2,4},{3,5},{4,6},{5,7},{6,8},{7,9},{8,10},{9,11},{10,... | collective-permute-start | bytes 786440 | tf_op jit(solution)/shard_map/ppermute | solution.py:37
  47.1 10.5 %copy-start.3 = (bf16[128,4096]{1,0:T(8,128)(2,1)S(1)}, bf16[128,4096]{1,0:T(8,128)(2,1)}, u32[]{:S(2)}) copy-start(bf16[128,4096]{1,0:T(8,128)(2,1)} %query_ref.7) | copy-start | bytes 3145732
  47.1 24.4 %all-to-all-start.1 = ((bf16[16,8,4096]{2,1,0:T(8,128)(2,1)}), bf16[16,8,4096]{2,1,0:T(8,128)(2,1)S(1)}, u32[]{:S(2)}, u32[]{:S(2)}) async-start(bf16[16,8,4096]{2,1,0:T(8,128)(2,1)} %broadcast_in_dim.30), calls=%async_computation.1 | async-start | bytes 2097152 | tf_op jit(solution)/shard_map/all_to_all | solution.py:41
  55.6 22.3 %collective-permute-start.4 = (bf16[256,512]{1,0:T(8,128)(2,1)S(1)}, bf16[256,512]{1,0:T(8,128)(2,1)S(1)}, u32[]{:S(2)}, u32[]{:S(2)}) collective-permute-start(bf16[256,512]{1,0:T(8,128)(2,1)S(1)} %collective-permute-done.2.keys_ref), channel_id=1, source_target_pairs={{0,2},{1,3},{2,4},{3,5},{4,6},{5,7},{6,8},{7,9},{8,10},{9,11},{10,... | collective-permute-start | bytes 786440 | tf_op jit(solution)/shard_map/ppermute | solution.py:37
  71.5 1.6 copy-start.1
  73.9 6.3 %collective-permute-start.5 = (bf16[64,128]{1,0:T(8,128)(2,1)S(1)}, bf16[64,128]{1,0:T(8,128)(2,1)S(1)}, u32[]{:S(2)}, u32[]{:S(2)}) collective-permute-start(bf16[64,128]{1,0:T(8,128)(2,1)S(1)} %lowrank.1), channel_id=1, source_target_pairs={{0,1},{1,2},{2,3},{3,4},{4,5},{5,6},{6,7},{7,8},{8,9},{9,10},{10,1... | collective-permute-start | bytes 49160 | tf_op jit(solution)/shard_map/ppermute | solution.py:37
  78.0 2.2 %copy-start.12 = (bf16[256,4096]{1,0:T(8,128)(2,1)S(1)}, bf16[256,4096]{1,0:T(8,128)(2,1)}, u32[]{:S(2)}) copy-start(bf16[256,4096]{1,0:T(8,128)(2,1)} %copy-done.11) | copy-start | bytes 6291460
  78.0 2.2 %copy-start.14 = (f32[64,4096]{1,0:T(8,128)S(1)}, f32[64,4096]{1,0:T(8,128)}, u32[]{:S(2)}) copy-start(f32[64,4096]{1,0:T(8,128)} %copy-done.13) | copy-start | bytes 3145732
  80.2 4.7 %copy-start.8 = (bf16[256,4096]{1,0:T(8,128)(2,1)S(1)}, bf16[256,4096]{1,0:T(8,128)(2,1)}, u32[]{:S(2)}) copy-start(bf16[256,4096]{1,0:T(8,128)(2,1)} %copy-done.7) | copy-start | bytes 6291460
  80.2 4.7 %copy-start.10 = (bf16[256,4096]{1,0:T(8,128)(2,1)S(1)}, bf16[256,4096]{1,0:T(8,128)(2,1)}, u32[]{:S(2)}) copy-start(bf16[256,4096]{1,0:T(8,128)(2,1)} %copy-done.9) | copy-start | bytes 6291460
  81.5 10.1 %collective-permute-start.6 = (bf16[64,512]{1,0:T(8,128)(2,1)S(1)}, bf16[64,512]{1,0:T(8,128)(2,1)S(1)}, u32[]{:S(2)}, u32[]{:S(2)}) collective-permute-start(bf16[64,512]{1,0:T(8,128)(2,1)S(1)} %get-tuple-element.40), channel_id=1, source_target_pairs={{4,0},{5,1},{6,2},{7,3},{8,4},{9,5},{10,6},{11,7},{12,8},{13,9},{1... | collective-permute-start | bytes 196616 | tf_op jit(solution)/shard_map/ppermute | solution.py:37
  82.8 3.4 %collective-permute-start.7 = (bf16[64,256]{1,0:T(8,128)(2,1)S(1)}, bf16[64,256]{1,0:T(8,128)(2,1)S(1)}, u32[]{:S(2)}, u32[]{:S(2)}) collective-permute-start(bf16[64,256]{1,0:T(8,128)(2,1)S(1)} %pad_maximum_fusion.3), channel_id=1, source_target_pairs={{0,2},{1,3},{2,4},{3,5},{4,6},{5,7},{6,8},{7,9},{8,10},{9,11},{10,... | collective-permute-start | bytes 98312 | tf_op jit(solution)/shard_map/ppermute | solution.py:37
  84.9 20.0 %copy-start.5 = (bf16[128,4096]{1,0:T(8,128)(2,1)S(1)}, bf16[128,4096]{1,0:T(8,128)(2,1)}, u32[]{:S(2)}) copy-start(bf16[128,4096]{1,0:T(8,128)(2,1)} %gradient_ref.5) | copy-start | bytes 3145732
  91.7 7.2 %collective-permute-start.9 = (bf16[64,512]{1,0:T(8,128)(2,1)S(1)}, bf16[64,512]{1,0:T(8,128)(2,1)S(1)}, u32[]{:S(2)}, u32[]{:S(2)}) collective-permute-start(bf16[64,512]{1,0:T(8,128)(2,1)S(1)} %pad_maximum_fusion.2), channel_id=1, source_target_pairs={{0,4},{1,5},{2,6},{3,7},{4,8},{5,9},{6,10},{7,11},{8,12},{9,13},{1... | collective-permute-start | bytes 196616 | tf_op jit(solution)/shard_map/ppermute | solution.py:37
  97.5 6.0 %collective-permute-start.8 = (f32[64,256]{1,0:T(8,128)S(1)}, f32[64,256]{1,0:T(8,128)S(1)}, u32[]{:S(2)}, u32[]{:S(2)}) collective-permute-start(f32[64,256]{1,0:T(8,128)S(1)} %slice.47), channel_id=1, source_target_pairs={{2,0},{3,1},{4,2},{5,3},{6,4},{7,5},{8,6},{9,7},{10,8},{11,9},{12,... | collective-permute-start | bytes 196616 | tf_op jit(solution)/shard_map/ppermute | solution.py:37
  103.6 6.1 %collective-permute-start.10 = (f32[64,128]{1,0:T(8,128)S(1)}, f32[64,128]{1,0:T(8,128)S(1)}, u32[]{:S(2)}, u32[]{:S(2)}) collective-permute-start(f32[64,128]{1,0:T(8,128)S(1)} %slice.49), channel_id=1, source_target_pairs={{1,0},{2,1},{3,2},{4,3},{5,4},{6,5},{7,6},{8,7},{9,8},{10,9},{11,1... | collective-permute-start | bytes 98312 | tf_op jit(solution)/shard_map/ppermute | solution.py:37
  107.3 2.4 %copy-start.2 = (bf16[128,8192]{1,0:T(8,128)(2,1)S(1)}, bf16[128,8192]{1,0:T(8,128)(2,1)}, u32[]{:S(2)}) copy-start(bf16[128,8192]{1,0:T(8,128)(2,1)} %hidden_ref.3) | copy-start | bytes 6291460
  (6 other events, 7.1 us)

commit v3 on v2

v3 whole, which is shorter than its diff:
```python
import math

import jax
import jax.numpy as jnp
from jax import lax
from jax.experimental import pallas as pl
from jax.experimental.pallas import tpu as pltpu
from jax.sharding import PartitionSpec as P

QUERY_HEADS = 32
KEY_HEADS = 4
HEAD_SIZE = 128
ADAPTER_RANK = 64
SPAN = 8
TOKENS = 128
WINDOW = SPAN * TOKENS
N_DP = 16
N_FSDP = 32
MODEL_WIDTH = 8192
VMEM_LIMIT = 60 * 1024 * 1024
GROUP = QUERY_HEADS // KEY_HEADS
COST = pl.CostEstimate(flops=10**10, bytes_accessed=2**27, transcendentals=0)
BF16 = jnp.bfloat16
F32 = jnp.float32
NT = (((1,), (1,)), ((), ()))


def whole(*arrays):
    return [pl.BlockSpec(memory_space=pltpu.VMEM) for _ in arrays]


def params():
    return pltpu.CompilerParams(vmem_limit_bytes=VMEM_LIMIT)


def from_behind(block, distance):
    route = [(i, i + distance) for i in range(N_FSDP) if 0 <= i + distance < N_FSDP]
    return lax.ppermute(block, "fsdp", route)


def exchange(slots, axis):
    return lax.all_to_all(slots, axis, 0, 0, tiled=True)


def lowrank_kernel(weight_ref, hidden_ref, out_ref, total_ref):
    step = pl.program_id(0)
    total = jnp.zeros((ADAPTER_RANK, TOKENS), F32)
    for f in range(8):
        rows = jnp.concatenate(
            [weight_ref[half, :, f * 128 : f * 128 + 128] for half in range(2)], axis=1
        )
        total += lax.dot_general(
            rows, hidden_ref[:, f * 256 : f * 256 + 256], NT, preferred_element_type=F32
        )

    @pl.when(step == 0)
    def _():
        total_ref[...] = total

    @pl.when(step > 0)
    def _():
        total_ref[...] += total

    @pl.when(step == 3)
    def _():
        out_ref[...] = total_ref[...].astype(BF16)


def score_pair(query_ref, keys, bias_ref, rows, weights_ref, stats_ref, at):
    factor = math.log2(math.e) / math.sqrt(HEAD_SIZE)
    for m in range(GROUP):
        lanes = slice(m * 128, m * 128 + 128)
        scores = lax.dot_general(keys, query_ref[:, lanes], NT, preferred_element_type=F32)
        scores = scores + bias_ref[rows, :]
        top = jnp.maximum(jnp.max(scores, axis=0, keepdims=True), -1e30) * factor
        weights = jnp.exp2(scores * factor - top)
        stats_ref[at : at + 1, lanes] = top
        stats_ref[at + 1 : at + 2, lanes] = jnp.sum(weights, axis=0, keepdims=True)
        weights_ref[:, lanes] = weights.astype(BF16)


def score_kernel(
    query_ref,
    keys2_ref,
    keys1_ref,
    keys0_ref,
    bias_ref,
    w2_ref,
    w1_ref,
    w0_ref,
    stats_ref,
):
    refs = ((keys2_ref, w2_ref), (keys1_ref, w1_ref), (keys0_ref, w0_ref))
    for i, (keys_ref, w_ref) in enumerate(refs):
        rows = slice(256 + i * 256, 512 + i * 256)
        score_pair(query_ref, keys_ref[...], bias_ref, rows, w_ref, stats_ref, 2 * i)
    stats_ref[6:8, :] = jnp.zeros((2, GROUP * TOKENS), F32)


def reached_kernel(gradient_ref, up_ref, reached_ref):
    for m in range(GROUP):
        lanes = slice(m * 128, m * 128 + 128)
        reached_ref[:, lanes] = lax.dot_general(
            up_ref[...], gradient_ref[:, lanes], NT, preferred_element_type=F32
        ).astype(BF16)


def sums_of(weights_ref, scale, reached):
    shares = (reached * scale).astype(BF16)
    return lax.dot_general(weights_ref[...], shares, NT, preferred_element_type=F32)


def add_up(sums_ref, out_ref, pairs):
    step = pl.program_id(0)
    for i, sums in enumerate(pairs):
        rows = slice(i * 256, i * 256 + 256)

        @pl.when(step == 0)
        def _(rows=rows, sums=sums):
            sums_ref[rows, :] = sums

        @pl.when(step > 0)
        def _(rows=rows, sums=sums):
            sums_ref[rows, :] += sums

    @pl.when(step == KEY_HEADS - 1)
    def _():
        out_ref[...] = sums_ref[...].T.astype(out_ref.dtype)


def far_kernel(
    query_ref,
    keys3_ref,
    bias_ref,
    w2_ref,
    stats_ref,
    reached_ref,
    w3_ref,
    scale_ref,
    far_ref,
    own_ref,
    sums_ref,
):
    score_pair(query_ref, keys3_ref[...], bias_ref, slice(0, 256), w3_ref, own_ref, 0)
    stats = [own_ref[0:2, :]] + [stats_ref[2 * i : 2 * i + 2, :] for i in range(3)]
    top = stats[0][0:1]
    for s in stats[1:]:
        top = jnp.maximum(top, s[0:1])
    parts = [jnp.exp2(s[0:1] - top) for s in stats]
    inverse = 1.0 / sum(part * s[1:2] for part, s in zip(parts, stats))
    scales = [part * inverse for part in parts]
    for i, scale in enumerate(scales):
        scale_ref[i : i + 1, :] = scale
    reached = reached_ref[...].astype(F32)
    pairs = [sums_of(w3_ref, scales[0], reached), sums_of(w2_ref, scales[1], reached)]
    add_up(sums_ref, far_ref, pairs)


def near_kernel(w1_ref, w0_ref, scale_ref, reached_ref, near_ref, sums_ref):
    reached = reached_ref[...].astype(F32)
    pairs = [
        sums_of(w1_ref, scale_ref[2:3, :], reached),
        sums_of(w0_ref, scale_ref[3:4, :], reached),
    ]
    add_up(sums_ref, near_ref, pairs)


def mixed_kernel(w3_ref, w2_ref, w1_ref, w0_ref, scale_ref, rank_ref, gradient_ref, out_ref):
    share = jnp.zeros((ADAPTER_RANK, HEAD_SIZE), F32)
    for m in range(GROUP):
        lanes = slice(m * 128, m * 128 + 128)
        mixed = jnp.zeros((ADAPTER_RANK, TOKENS), F32)
        for i, ref in enumerate((w3_ref, w2_ref, w1_ref, w0_ref)):
            rank = rank_ref[:, i * 256 : i * 256 + 256]
            part = jnp.dot(rank, ref[:, lanes], preferred_element_type=F32)
            mixed += part * scale_ref[i : i + 1, lanes]
        share += jnp.dot(mixed.astype(BF16), gradient_ref[:, lanes], preferred_element_type=F32)
    out_ref[...] = share


DOWN = N_FSDP * 128
LANES = DOWN + 256


def shares_kernel(key_ref, hidden_ref, up0_ref, up1_ref, out_ref):
    step = pl.program_id(0)
    for f in range(8):
        product = jnp.dot(
            key_ref[...], hidden_ref[:, f * 256 : f * 256 + 256], preferred_element_type=F32
        ).astype(BF16)
        lanes = pl.ds(pl.multiple_of(step * 1024 + f * 128, 128), 128)
        for half in range(2):
            out_ref[half, :, lanes] = product[:, half * 128 : half * 128 + 128]

    @pl.when(step == 0)
    def _():
        for half, up_ref in enumerate((up0_ref, up1_ref)):
            out_ref[half, :, DOWN:] = up_ref[...].astype(BF16)


def fold_dp_kernel(in_ref, out_ref):
    def total(columns):
        return sum(in_ref[d, :, columns].astype(F32) for d in range(N_DP))

    up = total(slice(DOWN, LANES)).astype(BF16)
    for f in range(N_FSDP):
        out_ref[f, :, :128] = total(slice(f * 128, f * 128 + 128)).astype(BF16)
        out_ref[f, :, 128:] = up


def fold_fsdp_kernel(in_ref, out_ref):
    total = sum(in_ref[f].astype(F32) for f in range(N_FSDP))
    for d in range(N_DP):
        out_ref[d] = total


def spread_kernel(in_ref, down_ref, up_ref):
    for half in range(2):
        for part in range(8):
            rows = slice(part * 8, part * 8 + 8)
            block = in_ref[half * 8 + part]
            down_ref[rows, half * 128 : half * 128 + 128] = block[:, :128]
            up_ref[rows, half * 256 : half * 256 + 256] = block[:, 128:]


def plain(kernel, name, out_shape, *arrays):
    return pl.pallas_call(
        kernel,
        in_specs=whole(*arrays),
        out_specs=jax.tree.map(lambda _: pl.BlockSpec(memory_space=pltpu.VMEM), out_shape),
        out_shape=out_shape,
        compiler_params=params(),
        cost_estimate=COST,
        name=name,
    )(*arrays)


def by_steps(kernel, name, steps, out_specs, out_shape, given, scratch=()):
    return pl.pallas_call(
        kernel,
        grid=(steps,),
        in_specs=[spec for spec, _ in given],
        out_specs=out_specs,
        out_shape=out_shape,
        scratch_shapes=list(scratch),
        compiler_params=params(),
        cost_estimate=COST,
        name=name,
    )(*[array for _, array in given])


def columns(rows, lanes, first=0):
    return pl.BlockSpec((rows, lanes), lambda g: (0, first + g))


def fixed(*shape):
    return pl.BlockSpec(shape, lambda g: (0,) * len(shape))


def local(
    hidden, queries, keys, document_numbers, adapter_down_weight, adapter_up_weight, output_gradient
):
    position = lax.axis_index("fsdp")
    member = lax.axis_index("dp")
    half, part = member // 8, member % 8

    keys1, keys2, keys3 = [from_behind(keys, distance) for distance in (1, 2, 3)]
    weight_slice = lax.dynamic_slice(adapter_down_weight.T, (part * 8, half * 128), (8, 128))
    docs_row = document_numbers.reshape(1, TOKENS).astype(BF16)
    slot = jnp.concatenate([weight_slice, docs_row, jnp.zeros((7, 128), BF16)], axis=0)
    slots = jnp.broadcast_to(slot[None], (N_FSDP, 16, 128))
    row_parts = exchange(slots, "fsdp")
    pair0 = jnp.concatenate([keys1, keys], axis=0)
    pair1 = jnp.concatenate([keys3, keys2], axis=0)
    pair2 = from_behind(pair1, 2)
    weight_part = row_parts[:, :8].transpose(1, 0, 2).reshape(1, 8, DOWN)
    docs = row_parts[:, 8].astype(jnp.int32)
    weight_slots = jnp.broadcast_to(weight_part, (N_DP, 8, DOWN))
    weight = exchange(weight_slots, "dp").reshape(2, ADAPTER_RANK, DOWN)
    pair2 = lax.optimization_barrier((pair2, weight_slots))[0]
    pair3 = from_behind(pair2, 2)

    padded = jnp.concatenate([jnp.full((SPAN - 1, TOKENS), -1, jnp.int32), docs], axis=0)
    window_docs = lax.dynamic_slice(padded, (position, 0), (SPAN, TOKENS)).reshape(WINDOW)
    own_docs = document_numbers.reshape(TOKENS)
    key_pos = jnp.arange(WINDOW, dtype=jnp.int32) - (SPAN - 1) * TOKENS
    visible = (window_docs[:, None] == own_docs[None, :]) & (
        key_pos[:, None] <= jnp.arange(TOKENS, dtype=jnp.int32)[None, :]
    )
    bias = jnp.where(visible, 0.0, -jnp.inf).astype(F32)
    lanes = GROUP * TOKENS
    queries_by, keys_by, weights_by = columns(TOKENS, lanes), columns(256, 128), columns(256, lanes)
    weights_shape = jax.ShapeDtypeStruct((2 * TOKENS, QUERY_HEADS * TOKENS), BF16)
    stats_by, stats_shape = columns(8, lanes), jax.ShapeDtypeStruct((8, QUERY_HEADS * TOKENS), F32)
    reached_by = columns(ADAPTER_RANK, lanes)
    sums = pltpu.VMEM((512, ADAPTER_RANK), F32)
    reached = by_steps(
        reached_kernel,
        "reached",
        KEY_HEADS,
        reached_by,
        jax.ShapeDtypeStruct((ADAPTER_RANK, QUERY_HEADS * TOKENS), BF16),
        [
            (queries_by, output_gradient),
            (columns(ADAPTER_RANK, HEAD_SIZE), adapter_up_weight),
        ],
    )
    w2, w1, w0, stats = by_steps(
        score_kernel,
        "score",
        KEY_HEADS,
        [weights_by] * 3 + [stats_by],
        [weights_shape] * 3 + [stats_shape],
        [
            (queries_by, queries),
            (keys_by, pair2),
            (keys_by, pair1),
            (keys_by, pair0),
            (fixed(WINDOW, TOKENS), bias),
        ],
    )
    rank = by_steps(
        lowrank_kernel,
        "lowrank",
        4,
        fixed(ADAPTER_RANK, TOKENS),
        jax.ShapeDtypeStruct((ADAPTER_RANK, TOKENS), BF16),
        [
            (pl.BlockSpec((2, ADAPTER_RANK, 1024), lambda j: (0, 0, j)), weight),
            (columns(TOKENS, 2048), hidden),
        ],
        [pltpu.VMEM((ADAPTER_RANK, TOKENS), F32)],
    )
    rank1 = jnp.concatenate([from_behind(rank, 1), rank], axis=1)
    pair3, rank, stats = lax.optimization_barrier((pair3, rank, stats))
    w3, scale, far = by_steps(
        far_kernel,
        "far",
        KEY_HEADS,
        [weights_by, stats_by, fixed(ADAPTER_RANK, WINDOW // 2)],
        [weights_shape, stats_shape, jax.ShapeDtypeStruct((ADAPTER_RANK, WINDOW // 2), BF16)],
        [
            (queries_by, queries),
            (keys_by, pair3),
            (fixed(256, TOKENS), bias),
            (weights_by, w2),
            (stats_by, stats),
            (reached_by, reached),
        ],
        [pltpu.VMEM((8, lanes), F32), sums],
    )
    near = by_steps(
        near_kernel,
        "near",
        KEY_HEADS,
        fixed(ADAPTER_RANK, WINDOW // 2),
        jax.ShapeDtypeStruct((ADAPTER_RANK, WINDOW // 2), F32),
        [(weights_by, w1), (weights_by, w0), (stats_by, scale), (reached_by, reached)],
        [sums],
    )
    came = from_behind(far, -4)
    rank2 = jnp.concatenate([from_behind(rank1, 2), rank1], axis=1)
    near = near + came.astype(F32)
    rank3 = jnp.concatenate([from_behind(rank2, 4), rank2], axis=1)
    came = from_behind(near[:, :256], -2)
    near = near[:, 256:] + came
    came = from_behind(near[:, :128], -1)
    ups = [
        by_steps(
            mixed_kernel,
            "mixed",
            2,
            columns(ADAPTER_RANK, HEAD_SIZE),
            jax.ShapeDtypeStruct((ADAPTER_RANK, 2 * HEAD_SIZE), F32),
            [(columns(256, lanes, first), w) for w in (w3, w2, w1, w0)]
            + [
                (columns(8, lanes, first), scale),
                (fixed(ADAPTER_RANK, WINDOW), rank3),
                (columns(TOKENS, lanes, first), output_gradient),
            ],
        )
        for first in (0, 2)
    ]
    key_grad = (near[:, 128:] + came).astype(BF16)

    shares = by_steps(
        shares_kernel,
        "shares",
        4,
        fixed(2, ADAPTER_RANK, LANES),
        jax.ShapeDtypeStruct((2, ADAPTER_RANK, LANES), BF16),
        [
            (fixed(ADAPTER_RANK, TOKENS), key_grad),
            (columns(TOKENS, 2048), hidden),
            (fixed(ADAPTER_RANK, 256), ups[0]),
            (fixed(ADAPTER_RANK, 256), ups[1]),
        ],
    )
    shares = exchange(shares.reshape(N_DP, 8, LANES), "dp")
    shares = plain(
        fold_dp_kernel, "fold_dp", jax.ShapeDtypeStruct((N_FSDP, 8, 384), BF16), shares
    )
    shares = exchange(shares, "fsdp")
    shares = plain(
        fold_fsdp_kernel, "fold_fsdp", jax.ShapeDtypeStruct((N_DP, 8, 384), F32), shares
    )
    shares = exchange(shares, "dp")
    down, up = plain(
        spread_kernel,
        "spread",
        (
            jax.ShapeDtypeStruct((ADAPTER_RANK, 256), F32),
            jax.ShapeDtypeStruct((ADAPTER_RANK, KEY_HEADS * HEAD_SIZE), F32),
        ),
        shares,
    )
    return (down.T, up)


def solution(mesh):
    in_specs = (
        P(("dp", "fsdp"), None),
        P(("dp", "fsdp"), None),
        P(("dp", "fsdp"), None),
        P("dp", "fsdp"),
        P("fsdp", None),
        P(),
        P(("dp", "fsdp"), None),
    )
    out_specs = (P("fsdp", None), P())
    return jax.shard_map(local, mesh=mesh, in_specs=in_specs, out_specs=out_specs, check_vma=False)
```

time: 180 us -> 201 us (1.12)
  Pallas kernels: 19.3 us -> 46.5 us
  waiting for transfers between devices: 21 us -> 13.2 us
  local copies, waits for them, and re-layouts: 10.7 us -> 3.58 us
  other arithmetic: 1.19 us -> 4.85 us
  blocking collectives: 68.5 us -> 71 us
    pallas_call x0 -> x8, Pallas kernels: none -> 41.1 us  [by_steps(): pl.pallas_call(kernel, grid=(steps,), in_specs=[spec for spec, _ in given...]
    pallas_call x14 -> x3, Pallas kernels: 19.3 us -> 5.34 us  [plain(): pl.pallas_call(kernel, in_specs=whole(*arrays), out_specs=jax.tree.map(la...]
    ppermute x11, waiting for transfers between devices: 10.2 us -> 0.03 us  [from_behind(): return lax.ppermute(block, 'fsdp', route)]
    unnamed x36 -> x18, local copies, waits for them, and re-layouts: 8.74 us -> 1.71 us
    all_to_all x3, blocking collectives: 68.5 us -> 71 us  [exchange(): return lax.all_to_all(slots, axis, 0, 0, tiled=True)]
    all_to_all x2, waiting for transfers between devices: 10.8 us -> 13.1 us  [exchange(): return lax.all_to_all(slots, axis, 0, 0, tiled=True)]
  transfers between devices with their start and end apart: 13 -> 13, of which waited for: 4 -> 2; matrix products, arithmetic and copies ran while one was open for 2% -> 3% of each run, Pallas kernels for 9% -> 19%
where the time goes in v3:
time: 201 us; the launch traced here: 199 us
  blocking collectives  71 us (35%)
  starting transfers between devices  59.3 us (30%)
  Pallas kernels  46.5 us (23%)
  waiting for transfers between devices  13.2 us (7%)
  other arithmetic  4.85 us (2%)
  local copies, waits for them, and re-layouts  3.58 us (2%)
    all_to_all x3, blocking collectives, exchange(): return lax.all_to_all(slots, axis, 0, 0, tiled=True)  71 us
    pallas_call x8, Pallas kernels, by_steps(): pl.pallas_call(kernel, grid=(steps,), in_specs=[spec for spec, _ in given...  41.1 us
    ppermute x11, starting transfers between devices, from_behind(): return lax.ppermute(block, 'fsdp', route)  40.1 us
    all_to_all x2, starting transfers between devices, exchange(): return lax.all_to_all(slots, axis, 0, 0, tiled=True)  19.2 us
    all_to_all x2, waiting for transfers between devices, exchange(): return lax.all_to_all(slots, axis, 0, 0, tiled=True)  13.1 us
    pallas_call x3, Pallas kernels, plain(): pl.pallas_call(kernel, in_specs=whole(*arrays), out_specs=jax.tree.map(la...  5.34 us
  transfers between devices with their start and end apart: 13, of which 2 were waited for; matrix products, arithmetic and copies ran while one was open for 3% of the time, Pallas kernels for 19%

profile of v3, /device:TPU:1, one launch (start us, length us, event | category | flops | bytes accessed | tf_op | source)
XLA Modules:
  0.0 199.3 jit_solution(17808762537222131766)
XLA Ops:
  0.6 7.1 %collective-permute-start = (bf16[128,512]{1,0:T(8,128)(2,1)}, bf16[128,512]{1,0:T(8,128)(2,1)S(1)}, u32[]{:S(2)}, u32[]{:S(2)}) collective-permute-start(bf16[128,512]{1,0:T(8,128)(2,1)} %param.9), channel_id=1, source_target_pairs={{0,3},{1,4},{2,5},{3,6},{4,7},{5,8},{6,9},{7,10},{8,11},{9,12},{10... | collective-permute-start | bytes 393224 | tf_op jit(solution)/shard_map/ppermute | solution.py:38
  7.7 6.1 %collective-permute-start.1 = (bf16[128,512]{1,0:T(8,128)(2,1)}, bf16[128,512]{1,0:T(8,128)(2,1)S(1)}, u32[]{:S(2)}, u32[]{:S(2)}) collective-permute-start(bf16[128,512]{1,0:T(8,128)(2,1)} %param.9), channel_id=1, source_target_pairs={{0,2},{1,3},{2,4},{3,5},{4,6},{5,7},{6,8},{7,9},{8,10},{9,11},{10,... | collective-permute-start | bytes 393224 | tf_op jit(solution)/shard_map/ppermute | solution.py:38
  13.9 3.5 %collective-permute-start.3 = (bf16[128,512]{1,0:T(8,128)(2,1)}, bf16[128,512]{1,0:T(8,128)(2,1)S(1)}, u32[]{:S(2)}, u32[]{:S(2)}) collective-permute-start(bf16[128,512]{1,0:T(8,128)(2,1)} %param.9), channel_id=1, source_target_pairs={{0,1},{1,2},{2,3},{3,4},{4,5},{5,6},{6,7},{7,8},{8,9},{9,10},{10,1... | collective-permute-start | bytes 393224 | tf_op jit(solution)/shard_map/ppermute | solution.py:38
  18.9 11.2 %all-to-all-start = ((bf16[32,16,128]{2,1,0:T(8,128)(2,1)}), bf16[32,16,128]{2,1,0:T(8,128)(2,1)S(1)}, u32[]{:S(2)}, u32[]{:S(2)}) async-start(bf16[32,16,128]{2,1,0:T(8,128)(2,1)} %broadcast_in_dim.28), calls=%async_computation | async-start | bytes 262144 | tf_op jit(solution)/shard_map/all_to_all | solution.py:42
  30.2 3.8 %reached.1.reached_ref = bf16[64,4096]{1,0:T(8,128)(2,1)} custom-call(bf16[128,4096]{1,0:T(8,128)(2,1)} %gradient_ref.5, bf16[64,512]{1,0:T(8,128)(2,1)} %up_ref.1), custom_call_target="tpu_custom_call" | custom-call | flops 10000000000 | bytes 134217728 | tf_op jit(solution)/shard_map/reached/pallas_call | solution.py:239
  34.1 4.0 %collective-permute-start.2 = (bf16[256,512]{1,0:T(8,128)(2,1)S(1)}, bf16[256,512]{1,0:T(8,128)(2,1)S(1)}, u32[]{:S(2)}, u32[]{:S(2)}) collective-permute-start(bf16[256,512]{1,0:T(8,128)(2,1)S(1)} %constant_dynamic-update-slice_fusion.keys1_ref), channel_id=1, source_target_pairs={{0,2},{1,3},{2,4},{3,5},{4,6},{5,7},{6,8},{7,9},{8,10},{9,11},{10,... | collective-permute-start | bytes 786440 | tf_op jit(solution)/shard_map/ppermute | solution.py:38
  38.9 7.0 %all-to-all-done = bf16[32,16,128]{2,1,0:T(8,128)(2,1)S(1)} async-done(((bf16[32,16,128]{2,1,0:T(8,128)(2,1)}), bf16[32,16,128]{2,1,0:T(8,128)(2,1)S(1)}, u32[]{:S(2)}, u32[]{:S(2)}) %all-to-all-start) | async-done | bytes 131104 | tf_op jit(solution)/shard_map/all_to_all | solution.py:42
  47.0 7.9 %all-to-all-start.1 = ((bf16[16,8,4096]{2,1,0:T(8,128)(2,1)}), bf16[16,8,4096]{2,1,0:T(8,128)(2,1)S(1)}, u32[]{:S(2)}, u32[]{:S(2)}) async-start(bf16[16,8,4096]{2,1,0:T(8,128)(2,1)} %broadcast_in_dim.30), calls=%async_computation.1 | async-start | bytes 2097152 | tf_op jit(solution)/shard_map/all_to_all | solution.py:42
  55.0 1.9 collective-permute-start.4
  58.1 7.5 %score.1 = (bf16[256,4096]{1,0:T(8,128)(2,1)}, bf16[256,4096]{1,0:T(8,128)(2,1)}, bf16[256,4096]{1,0:T(8,128)(2,1)}, f32[8,4096]{1,0:T(8,128)}) custom-call(bf16[128,4096]{1,0:T(8,128)(2,1)} %query_ref.3, bf16[256,512]{1,0:T(8,128)(2,1)} %copy-done.6, bf16[256,512]{1,0:T(8,128)(2,1)} %copy-done.4, bf16[256,512]{1,0:T(8,128)(2,1)} %pad_maximum_fusion.keys0_ref, ...), custom_call_target="tpu_custom_call" | custom-call | flops 10000000000 | bytes 134217728 | tf_op jit(solution)/shard_map/score/pallas_call | solution.py:239
  65.6 6.1 %all-to-all-done.1 = bf16[16,8,4096]{2,1,0:T(8,128)(2,1)S(1)} async-done(((bf16[16,8,4096]{2,1,0:T(8,128)(2,1)}), bf16[16,8,4096]{2,1,0:T(8,128)(2,1)S(1)}, u32[]{:S(2)}, u32[]{:S(2)}) %all-to-all-start.1) | async-done | bytes 1048608 | tf_op jit(solution)/shard_map/all_to_all | solution.py:42
  72.7 3.9 %lowrank.1 = bf16[64,128]{1,0:T(8,128)(2,1)} custom-call(bf16[2,64,4096]{2,1,0:T(8,128)(2,1)} %bitcast.16, bf16[128,8192]{1,0:T(8,128)(2,1)} %hidden_ref.3), custom_call_target="tpu_custom_call" | custom-call | flops 10000000000 | bytes 134217728 | tf_op jit(solution)/shard_map/lowrank/pallas_call | solution.py:239
  76.5 3.6 %collective-permute-start.8 = (bf16[64,128]{1,0:T(8,128)(2,1)}, bf16[64,128]{1,0:T(8,128)(2,1)S(1)}, u32[]{:S(2)}, u32[]{:S(2)}) collective-permute-start(bf16[64,128]{1,0:T(8,128)(2,1)} %lowrank.1), channel_id=1, source_target_pairs={{0,1},{1,2},{2,3},{3,4},{4,5},{5,6},{6,7},{7,8},{8,9},{9,10},{10,1... | collective-permute-start | bytes 49160 | tf_op jit(solution)/shard_map/ppermute | solution.py:38
  80.9 6.6 %far.1 = (bf16[256,4096]{1,0:T(8,128)(2,1)}, f32[8,4096]{1,0:T(8,128)}, bf16[64,512]{1,0:T(8,128)(2,1)}) custom-call(bf16[128,4096]{1,0:T(8,128)(2,1)} %query_ref.3, bf16[256,512]{1,0:T(8,128)(2,1)} %copy-done.7, f32[1024,128]{1,0:T(8,128)} %fusion.1.bias_ref, bf16[256,4096]{1,0:T(8,128)(2,1)} %get-tuple-element.19.w2_ref, ...), custom_call_target="tpu_custom_call" | custom-call | flops 10000000000 | bytes 134217728 | tf_op jit(solution)/shard_map/far/pallas_call | solution.py:239
  90.1 4.7 %near.1 = f32[64,512]{1,0:T(8,128)} custom-call(bf16[256,4096]{1,0:T(8,128)(2,1)} %get-tuple-element.15.w1_ref, bf16[256,4096]{1,0:T(8,128)(2,1)} %get-tuple-element.16.w0_ref, f32[8,4096]{1,0:T(8,128)} %get-tuple-element.21.scale_ref, bf16[64,4096]{1,0:T(8,128)(2,1)} %reached.1.reached_ref), custom_call_target="tpu_custom_call" | custom-call | flops 10000000000 | bytes 134217728 | tf_op jit(solution)/shard_map/near/pallas_call | solution.py:239
  94.9 8.6 %collective-permute-start.10 = (bf16[64,512]{1,0:T(8,128)(2,1)S(1)}, bf16[64,512]{1,0:T(8,128)(2,1)S(1)}, u32[]{:S(2)}, u32[]{:S(2)}) collective-permute-start(bf16[64,512]{1,0:T(8,128)(2,1)S(1)} %pad_maximum_fusion.2), channel_id=1, source_target_pairs={{0,4},{1,5},{2,6},{3,7},{4,8},{5,9},{6,10},{7,11},{8,12},{9,13},{1... | collective-permute-start | bytes 196616 | tf_op jit(solution)/shard_map/ppermute | solution.py:38
  106.5 5.3 %mixed.2.up0_ref = f32[64,256]{1,0:T(8,128)} custom-call(bf16[256,4096]{1,0:T(8,128)(2,1)} %get-tuple-element.23.w3_ref, bf16[256,4096]{1,0:T(8,128)(2,1)} %get-tuple-element.19.w2_ref, bf16[256,4096]{1,0:T(8,128)(2,1)} %get-tuple-element.15.w1_ref, bf16[256,4096]{1,0:T(8,128)(2,1)} %get-tuple-element.16.w0_ref, f32[8,4096]{1,0:T(8,128)} %get-tuple-element.21.scale_ref, ...), custom_call_target="tpu_custom_call" | custom-call | flops 10000000000 | bytes 134217728 | tf_op jit(solution)/shard_map/mixed/pallas_call | solution.py:239
  113.1 5.3 %mixed.3.up1_ref = f32[64,256]{1,0:T(8,128)} custom-call(bf16[256,4096]{1,0:T(8,128)(2,1)} %get-tuple-element.23.w3_ref, bf16[256,4096]{1,0:T(8,128)(2,1)} %get-tuple-element.19.w2_ref, bf16[256,4096]{1,0:T(8,128)(2,1)} %get-tuple-element.15.w1_ref, bf16[256,4096]{1,0:T(8,128)(2,1)} %get-tuple-element.16.w0_ref, f32[8,4096]{1,0:T(8,128)} %get-tuple-element.21.scale_ref, ...), custom_call_target="tpu_custom_call" | custom-call | flops 10000000000 | bytes 134217728 | tf_op jit(solution)/shard_map/mixed/pallas_call | solution.py:239
  119.1 3.9 %shares.1 = bf16[2,64,4352]{2,1,0:T(8,128)(2,1)} custom-call(bf16[64,128]{1,0:T(8,128)(2,1)} %fusion.2.key_ref, bf16[128,8192]{1,0:T(8,128)(2,1)} %hidden_ref.3, f32[64,256]{1,0:T(8,128)} %mixed.2.up0_ref, f32[64,256]{1,0:T(8,128)} %mixed.3.up1_ref), custom_call_target="tpu_custom_call" | custom-call | flops 10000000000 | bytes 134217728 | tf_op jit(solution)/shard_map/shares/pallas_call | solution.py:239
  123.0 25.1 %all_to_all.25.in_ref = bf16[16,8,4352]{2,1,0:T(8,128)(2,1)} all-to-all(bf16[16,8,4352]{2,1,0:T(8,128)(2,1)} %bitcast.15), channel_id=1, replica_groups=mesh['dp'=16,'fsdp'=32] {'dp'}, dimensions={0} | all-to-all | bytes 2228224 | tf_op jit(solution)/shard_map/all_to_all | solution.py:42
  148.1 2.1 %fold_dp.1 = bf16[32,8,384]{2,1,0:T(8,128)(2,1)} custom-call(bf16[16,8,4352]{2,1,0:T(8,128)(2,1)} %all_to_all.25.in_ref), custom_call_target="tpu_custom_call" | custom-call | flops 10000000000 | bytes 134217728 | tf_op jit(solution)/shard_map/fold_dp/pallas_call | solution.py:227
  150.2 32.3 %all_to_all.26.in_ref = bf16[32,8,384]{2,1,0:T(8,128)(2,1)} all-to-all(bf16[32,8,384]{2,1,0:T(8,128)(2,1)} %fold_dp.1), channel_id=1, replica_groups=mesh['dp'=16,'fsdp'=32] {'fsdp'}, dimensions={0} | all-to-all | bytes 393216 | tf_op jit(solution)/shard_map/all_to_all | solution.py:42
  182.4 1.6 fold_fsdp.1
  184.1 13.6 %all_to_all.27.in_ref = f32[16,8,384]{2,1,0:T(8,128)} all-to-all(f32[16,8,384]{2,1,0:T(8,128)} %fold_fsdp.1), channel_id=1, replica_groups=mesh['dp'=16,'fsdp'=32] {'dp'}, dimensions={0} | all-to-all | bytes 393216 | tf_op jit(solution)/shard_map/all_to_all | solution.py:42
  (56 shorter events, 15.2 us)
Async XLA Ops:
  0.6 17.6 %copy-start = (bf16[256,64]{0,1:T(8,128)(2,1)S(1)}, bf16[256,64]{0,1:T(8,128)(2,1)}, u32[]{:S(2)}) copy-start(bf16[256,64]{0,1:T(8,128)(2,1)} %param.11) | copy-start | bytes 98308
  0.6 33.4 %collective-permute-start = (bf16[128,512]{1,0:T(8,128)(2,1)}, bf16[128,512]{1,0:T(8,128)(2,1)S(1)}, u32[]{:S(2)}, u32[]{:S(2)}) collective-permute-start(bf16[128,512]{1,0:T(8,128)(2,1)} %param.9), channel_id=1, source_target_pairs={{0,3},{1,4},{2,5},{3,6},{4,7},{5,8},{6,9},{7,10},{8,11},{9,12},{10... | collective-permute-start | bytes 393224 | tf_op jit(solution)/shard_map/ppermute | solution.py:38
  7.7 26.3 %collective-permute-start.1 = (bf16[128,512]{1,0:T(8,128)(2,1)}, bf16[128,512]{1,0:T(8,128)(2,1)S(1)}, u32[]{:S(2)}, u32[]{:S(2)}) collective-permute-start(bf16[128,512]{1,0:T(8,128)(2,1)} %param.9), channel_id=1, source_target_pairs={{0,2},{1,3},{2,4},{3,5},{4,6},{5,7},{6,8},{7,9},{8,10},{9,11},{10,... | collective-permute-start | bytes 393224 | tf_op jit(solution)/shard_map/ppermute | solution.py:38
  13.9 24.3 %collective-permute-start.3 = (bf16[128,512]{1,0:T(8,128)(2,1)}, bf16[128,512]{1,0:T(8,128)(2,1)S(1)}, u32[]{:S(2)}, u32[]{:S(2)}) collective-permute-start(bf16[128,512]{1,0:T(8,128)(2,1)} %param.9), channel_id=1, source_target_pairs={{0,1},{1,2},{2,3},{3,4},{4,5},{5,6},{6,7},{7,8},{8,9},{9,10},{10,1... | collective-permute-start | bytes 393224 | tf_op jit(solution)/shard_map/ppermute | solution.py:38
  18.9 27.0 %all-to-all-start = ((bf16[32,16,128]{2,1,0:T(8,128)(2,1)}), bf16[32,16,128]{2,1,0:T(8,128)(2,1)S(1)}, u32[]{:S(2)}, u32[]{:S(2)}) async-start(bf16[32,16,128]{2,1,0:T(8,128)(2,1)} %broadcast_in_dim.28), calls=%async_computation | async-start | bytes 262144 | tf_op jit(solution)/shard_map/all_to_all | solution.py:42
  30.2 8.0 %copy-start.3 = (bf16[128,512]{1,0:T(8,128)(2,1)S(1)}, bf16[128,512]{1,0:T(8,128)(2,1)}, u32[]{:S(2)}) copy-start(bf16[128,512]{1,0:T(8,128)(2,1)} %param.9) | copy-start | bytes 393220
  34.0 22.9 %copy-start.5 = (s32[1,128]{1,0:T(1,128)S(1)}, s32[1,128]{1,0:T(1,128)}, u32[]{:S(2)}) copy-start(s32[1,128]{1,0:T(1,128)} %param.10) | copy-start | bytes 1540
  34.1 24.0 %copy-start.4 = (bf16[256,512]{1,0:T(8,128)(2,1)}, bf16[256,512]{1,0:T(8,128)(2,1)S(1)}, u32[]{:S(2)}) copy-start(bf16[256,512]{1,0:T(8,128)(2,1)S(1)} %constant_dynamic-update-slice_fusion.keys1_ref) | copy-start | bytes 786436
  34.1 20.9 %collective-permute-start.2 = (bf16[256,512]{1,0:T(8,128)(2,1)S(1)}, bf16[256,512]{1,0:T(8,128)(2,1)S(1)}, u32[]{:S(2)}, u32[]{:S(2)}) collective-permute-start(bf16[256,512]{1,0:T(8,128)(2,1)S(1)} %constant_dynamic-update-slice_fusion.keys1_ref), channel_id=1, source_target_pairs={{0,2},{1,3},{2,4},{3,5},{4,6},{5,7},{6,8},{7,9},{8,10},{9,11},{10,... | collective-permute-start | bytes 786440 | tf_op jit(solution)/shard_map/ppermute | solution.py:38
  47.0 24.7 %all-to-all-start.1 = ((bf16[16,8,4096]{2,1,0:T(8,128)(2,1)}), bf16[16,8,4096]{2,1,0:T(8,128)(2,1)S(1)}, u32[]{:S(2)}, u32[]{:S(2)}) async-start(bf16[16,8,4096]{2,1,0:T(8,128)(2,1)} %broadcast_in_dim.30), calls=%async_computation.1 | async-start | bytes 2097152 | tf_op jit(solution)/shard_map/all_to_all | solution.py:42
  54.9 3.2 %copy-start.6 = (bf16[256,512]{1,0:T(8,128)(2,1)}, bf16[256,512]{1,0:T(8,128)(2,1)S(1)}, u32[]{:S(2)}) copy-start(bf16[256,512]{1,0:T(8,128)(2,1)S(1)} %collective-permute-done.2.keys2_ref) | copy-start | bytes 786436
  55.0 25.2 %collective-permute-start.4 = (bf16[256,512]{1,0:T(8,128)(2,1)S(1)}, bf16[256,512]{1,0:T(8,128)(2,1)S(1)}, u32[]{:S(2)}, u32[]{:S(2)}) collective-permute-start(bf16[256,512]{1,0:T(8,128)(2,1)S(1)} %collective-permute-done.2.keys2_ref), channel_id=1, source_target_pairs={{0,2},{1,3},{2,4},{3,5},{4,6},{5,7},{6,8},{7,9},{8,10},{9,11},{10,... | collective-permute-start | bytes 786440 | tf_op jit(solution)/shard_map/ppermute | solution.py:38
  71.7 1.0 copy-start.1
  76.5 12.3 %collective-permute-start.8 = (bf16[64,128]{1,0:T(8,128)(2,1)}, bf16[64,128]{1,0:T(8,128)(2,1)S(1)}, u32[]{:S(2)}, u32[]{:S(2)}) collective-permute-start(bf16[64,128]{1,0:T(8,128)(2,1)} %lowrank.1), channel_id=1, source_target_pairs={{0,1},{1,2},{2,3},{3,4},{4,5},{5,6},{6,7},{7,8},{8,9},{9,10},{10,1... | collective-permute-start | bytes 49160 | tf_op jit(solution)/shard_map/ppermute | solution.py:38
  80.2 0.7 copy-start.7
  80.9 7.9 %copy-start.2 = (bf16[64,128]{1,0:T(8,128)(2,1)S(1)}, bf16[64,128]{1,0:T(8,128)(2,1)}, u32[]{:S(2)}) copy-start(bf16[64,128]{1,0:T(8,128)(2,1)} %lowrank.1) | copy-start | bytes 49156
  87.5 16.0 %collective-permute-start.5 = (bf16[64,512]{1,0:T(8,128)(2,1)}, bf16[64,512]{1,0:T(8,128)(2,1)S(1)}, u32[]{:S(2)}, u32[]{:S(2)}) collective-permute-start(bf16[64,512]{1,0:T(8,128)(2,1)} %get-tuple-element.22), channel_id=1, source_target_pairs={{4,0},{5,1},{6,2},{7,3},{8,4},{9,5},{10,6},{11,7},{12,8},{13,9},{1... | collective-permute-start | bytes 196616 | tf_op jit(solution)/shard_map/ppermute | solution.py:38
  88.8 6.0 %collective-permute-start.9 = (bf16[64,256]{1,0:T(8,128)(2,1)S(1)}, bf16[64,256]{1,0:T(8,128)(2,1)S(1)}, u32[]{:S(2)}, u32[]{:S(2)}) collective-permute-start(bf16[64,256]{1,0:T(8,128)(2,1)S(1)} %pad_maximum_fusion.3), channel_id=1, source_target_pairs={{0,2},{1,3},{2,4},{3,5},{4,6},{5,7},{6,8},{7,9},{8,10},{9,11},{10,... | collective-permute-start | bytes 98312 | tf_op jit(solution)/shard_map/ppermute | solution.py:38
  94.9 10.9 %collective-permute-start.10 = (bf16[64,512]{1,0:T(8,128)(2,1)S(1)}, bf16[64,512]{1,0:T(8,128)(2,1)S(1)}, u32[]{:S(2)}, u32[]{:S(2)}) collective-permute-start(bf16[64,512]{1,0:T(8,128)(2,1)S(1)} %pad_maximum_fusion.2), channel_id=1, source_target_pairs={{0,4},{1,5},{2,6},{3,7},{4,8},{5,9},{6,10},{7,11},{8,12},{9,13},{1... | collective-permute-start | bytes 196616 | tf_op jit(solution)/shard_map/ppermute | solution.py:38
  104.5 7.3 %collective-permute-start.6 = (f32[64,256]{1,0:T(8,128)S(1)}, f32[64,256]{1,0:T(8,128)S(1)}, u32[]{:S(2)}, u32[]{:S(2)}) collective-permute-start(f32[64,256]{1,0:T(8,128)S(1)} %slice.27), channel_id=1, source_target_pairs={{2,0},{3,1},{4,2},{5,3},{6,4},{7,5},{8,6},{9,7},{10,8},{11,9},{12,... | collective-permute-start | bytes 196616 | tf_op jit(solution)/shard_map/ppermute | solution.py:38
  111.8 6.7 %collective-permute-start.7 = (f32[64,128]{1,0:T(8,128)S(1)}, f32[64,128]{1,0:T(8,128)S(1)}, u32[]{:S(2)}, u32[]{:S(2)}) collective-permute-start(f32[64,128]{1,0:T(8,128)S(1)} %slice.29), channel_id=1, source_target_pairs={{1,0},{2,1},{3,2},{4,3},{5,4},{6,5},{7,6},{8,7},{9,8},{10,9},{11,1... | collective-permute-start | bytes 98312 | tf_op jit(solution)/shard_map/ppermute | solution.py:38

commit v4 on v2

--- a/solution.py
+++ b/solution.py
@@ -18,7 +18,8 @@
 N_DP = 16
 N_FSDP = 32
 MODEL_WIDTH = 8192
-VMEM_LIMIT = 20 * 1024 * 1024
+GROUP = QUERY_HEADS // KEY_HEADS
+COST = pl.CostEstimate(flops=10**10, bytes_accessed=2**27, transcendentals=0)
 BF16 = jnp.bfloat16
 F32 = jnp.float32
 NT = (((1,), (1,)), ((), ()))
@@ -28,8 +29,8 @@
     return [pl.BlockSpec(memory_space=pltpu.VMEM) for _ in arrays]
 
 
-def params():
-    return pltpu.CompilerParams(vmem_limit_bytes=VMEM_LIMIT)
+def params(mebibytes):
+    return pltpu.CompilerParams(vmem_limit_bytes=mebibytes * 1024 * 1024)
 
 
 def from_behind(block, distance):
@@ -41,71 +42,107 @@
     return lax.all_to_all(slots, axis, 0, 0, tiled=True)
 
 
-def lowrank_kernel(weight_ref, hidden_ref, out_ref):
+def lowrank_kernel(weight_hbm, hidden_hbm, out_ref, weight_ref, hidden_ref, arrived):
+    copies = []
+    for j in range(4):
+        lanes = pl.ds(j * 1024, 1024)
+        wide = pl.ds(j * 2048, 2048)
+        copies.append(
+            (
+                pltpu.make_async_copy(
+                    weight_hbm.at[:, :, lanes], weight_ref.at[:, :, lanes], arrived.at[0, j]
+                ),
+                pltpu.make_async_copy(
+                    hidden_hbm.at[:, wide], hidden_ref.at[:, wide], arrived.at[1, j]
+                ),
+            )
+        )
+    for pair in copies:
+        for copy in pair:
+            copy.start()
     total = jnp.zeros((ADAPTER_RANK, TOKENS), F32)
-    for f in range(N_FSDP):
-        rows = jnp.concatenate(
-            [weight_ref[half, :, f * 128 : f * 128 + 128] for half in range(2)], axis=1
-        )
-        total += lax.dot_general(
-            rows, hidden_ref[:, f * 256 : f * 256 + 256], NT, preferred_element_type=F32
-        )
+    for j, pair in enumerate(copies):
+        for copy in pair:
+            copy.wait()
+        for f in range(8 * j, 8 * j + 8):
+            rows = jnp.concatenate(
+                [weight_ref[half, :, f * 128 : f * 128 + 128] for half in range(2)], axis=1
+            )
+            total += lax.dot_general(
+                rows, hidden_ref[:, f * 256 : f * 256 + 256], NT, preferred_element_type=F32
+            )
     out_ref[...] = total.astype(BF16)
 
 
-def score_kernel(query_ref, keys_ref, bias_ref, weights_ref, stats_ref):
+def score_pair(query_ref, keys, bias_ref, rows, weights_ref, stats_ref, at):
     factor = math.log2(math.e) / math.sqrt(HEAD_SIZE)
-
+    for m in range(GROUP):
+        lanes = slice(m * 128, m * 128 + 128)
+        scores = lax.dot_general(keys, query_ref[:, lanes], NT, preferred_element_type=F32)
+        scores = scores + bias_ref[rows, :]
+        top = jnp.maximum(jnp.max(scores, axis=0, keepdims=True), -1e30) * factor
+        weights = jnp.exp2(scores * factor - top)
+        stats_ref[at : at + 1, lanes] = top
+        stats_ref[at + 1 : at + 2, lanes] = jnp.sum(weights, axis=0, keepdims=True)
+        weights_ref[:, lanes] = weights.astype(BF16)
+
+
+def score_kernel(
+    query_ref,
+    keys2_ref,
+    keys1_ref,
+    keys0_ref,
+    bias_ref,
+    w2_ref,
+    w1_ref,
+    w0_ref,
+    stats_ref,
+):
+    refs = ((keys2_ref, w2_ref), (keys1_ref, w1_ref), (keys0_ref, w0_ref))
+    for i, (keys_ref, w_ref) in enumerate(refs):
+        rows = slice(256 + i * 256, 512 + i * 256)
+        score_pair(query_ref, keys_ref[...], bias_ref, rows, w_ref, stats_ref, 2 * i)
+    stats_ref[6:8, :] = jnp.zeros((2, GROUP * TOKENS), F32)
+
+
+def last_score_kernel(query_ref, keys_ref, bias_ref, weights_ref, stats_ref):
     def key_head(g, carry):
         keys = keys_ref[:, pl.ds(pl.multiple_of(g * HEAD_SIZE, HEAD_SIZE), HEAD_SIZE)]
-        for m in range(QUERY_HEADS // KEY_HEADS):
-            lanes = pl.ds(pl.multiple_of((g * 8 + m) * 128, 128), 128)
-            scores = lax.dot_general(keys, query_ref[:, lanes], NT, preferred_element_type=F32)
-            scores = scores + bias_ref[...]
-            top = jnp.maximum(jnp.max(scores, axis=0, keepdims=True), -1e30) * factor
-            weights = jnp.exp2(scores * factor - top)
-            stats_ref[0:1, lanes] = top
-            stats_ref[1:2, lanes] = jnp.sum(weights, axis=0, keepdims=True)
-            weights_ref[:, lanes] = weights.astype(BF16)
+        lanes = pl.ds(pl.multiple_of(g * GROUP * 128, 128), GROUP * 128)
+        score_pair(
+            query_ref.at[:, lanes],
+            keys,
+            bias_ref,
+            slice(0, 256),
+            weights_ref.at[:, lanes],
+            stats_ref.at[:, lanes],
+            0,
+        )
         return carry
 
     lax.fori_loop(0, KEY_HEADS, key_head, 0)
-
-
-def score(queries, keys, bias):
-    return plain(
-        score_kernel,
-        "score",
-        (
-            jax.ShapeDtypeStruct((2 * TOKENS, QUERY_HEADS * TOKENS), BF16),
-            jax.ShapeDtypeStruct((2, QUERY_HEADS * TOKENS), F32),
-        ),
-        queries,
-        keys,
-        bias,
-    )
 
 
 def reached_kernel(gradient_ref, up_ref, out_ref):
     def key_head(g, carry):
         up = up_ref[:, pl.ds(pl.multiple_of(g * HEAD_SIZE, HEAD_SIZE), HEAD_SIZE)]
-        for m in range(QUERY_HEADS // KEY_HEADS):
-            lanes = pl.ds(pl.multiple_of((g * 8 + m) * 128, 128), 128)
+        for m in range(GROUP):
+            lanes = pl.ds(pl.multiple_of((g * GROUP + m) * 128, 128), 128)
             out_ref[:, lanes] = lax.dot_general(
                 up, gradient_ref[:, lanes], NT, preferred_element_type=F32
-            )
+            ).astype(BF16)
         return carry
 
     lax.fori_loop(0, KEY_HEADS, key_head, 0)
 
 
 def sums_of(weights_ref, scale, reached):
-    shares = (reached.astype(BF16).astype(F32) * scale).astype(BF16)
+    shares = (reached * scale).astype(BF16)
     return lax.dot_general(weights_ref[...], shares, NT, preferred_element_type=F32).T
 
 
-def far_kernel(w3_ref, w2_ref, s3_ref, s2_ref, s1_ref, s0_ref, reached_ref, far_ref, scale_ref):
-    stats = [ref[...] for ref in (s3_ref, s2_ref, s1_ref, s0_ref)]
+def far_kernel(w3_ref, w2_ref, last_ref, stats_ref, reached_ref, far_ref, scale_ref):
+    stats = [last_ref[...]] + [stats_ref[2 * i : 2 * i + 2, :] for i in range(3)]
     top = stats[0][0:1]
     for s in stats[1:]:
         top = jnp.maximum(top, s[0:1])
@@ -114,13 +151,13 @@
     scales = [part * inverse for part in parts]
     for i, scale in enumerate(scales):
         scale_ref[i : i + 1, :] = scale
-    reached = reached_ref[...]
+    reached = reached_ref[...].astype(F32)
     far_ref[:, :256] = sums_of(w3_ref, scales[0], reached).astype(BF16)
     far_ref[:, 256:] = sums_of(w2_ref, scales[1], reached).astype(BF16)
 
 
 def near_kernel(w1_ref, w0_ref, scale_ref, reached_ref, near_ref):
-    reached = reached_ref[...]
+    reached = reached_ref[...].astype(F32)
     near_ref[:, :256] = sums_of(w1_ref, scale_ref[2:3, :], reached)
     near_ref[:, 256:] = sums_of(w0_ref, scale_ref[3:4, :], reached)
 
@@ -188,10 +225,32 @@
         in_specs=whole(*arrays),
         out_specs=jax.tree.map(lambda _: pl.BlockSpec(memory_space=pltpu.VMEM), out_shape),
         out_shape=out_shape,
-        compiler_params=params(),
-        cost_estimate=pl.CostEstimate(flops=10**10, bytes_accessed=2**27, transcendentals=0),
+        compiler_params=params(20),
+        cost_estimate=COST,
         name=name,
     )(*arrays)
+
+
+def by_steps(kernel, name, steps, out_specs, out_shape, given, scratch=()):
+    return pl.pallas_call(
+        kernel,
+        grid=(steps,),
+        in_specs=[spec for spec, _ in given],
+        out_specs=out_specs,
+        out_shape=out_shape,
+        scratch_shapes=list(scratch),
+        compiler_params=params(60),
+        cost_estimate=COST,
+        name=name,
+    )(*[array for _, array in given])
+
+
+def columns(rows, lanes, first=0):
+    return pl.BlockSpec((rows, lanes), lambda g: (0, first + g))
+
+
+def fixed(*shape):
+    return pl.BlockSpec(shape, lambda g: (0,) * len(shape))
 
 
 def local(
@@ -225,40 +284,67 @@
         key_pos[:, None] <= jnp.arange(TOKENS, dtype=jnp.int32)[None, :]
     )
     bias = jnp.where(visible, 0.0, -jnp.inf).astype(F32)
-    biases = [bias[i * 256 : i * 256 + 256] for i in range(4)]
-
+    lanes = GROUP * TOKENS
+    columns_of = QUERY_HEADS * TOKENS
+    queries_by, keys_by, weights_by = columns(TOKENS, lanes), columns(256, 128), columns(256, lanes)
+    weights_shape = jax.ShapeDtypeStruct((2 * TOKENS, columns_of), BF16)
+    w2, w1, w0, stats = by_steps(
+        score_kernel,
+        "score",
+        KEY_HEADS,
+        [weights_by] * 3 + [columns(8, lanes)],
+        [weights_shape] * 3 + [jax.ShapeDtypeStruct((8, columns_of), F32)],
+        [
+            (queries_by, queries),
+            (keys_by, pair2),
+            (keys_by, pair1),
+            (keys_by, pair0),
+            (fixed(WINDOW, TOKENS), bias),
+        ],
+    )
     reached = plain(
         reached_kernel,
         "reached",
-        jax.ShapeDtypeStruct((ADAPTER_RANK, QUERY_HEADS * TOKENS), F32),
+        jax.ShapeDtypeStruct((ADAPTER_RANK, columns_of), BF16),
         output_gradient,
         adapter_up_weight,
     )
-    w0, s0 = score(queries, pair0, biases[3])
-    w1, s1 = score(queries, pair1, biases[2])
-    pair2, w1 = lax.optimization_barrier((pair2, w1))
-    w2, s2 = score(queries, pair2, biases[1])
-    rank = plain(
-        lowrank_kernel, "lowrank", jax.ShapeDtypeStruct((ADAPTER_RANK, TOKENS), BF16), weight, hidden
-    )
+    anywhere = pl.BlockSpec(memory_space=pl.ANY)
+    rank = pl.pallas_call(
+        lowrank_kernel,
+        in_specs=[anywhere, anywhere],
+        out_specs=pl.BlockSpec(memory_space=pltpu.VMEM),
+        out_shape=jax.ShapeDtypeStruct((ADAPTER_RANK, TOKENS), BF16),
+        scratch_shapes=[
+            pltpu.VMEM((2, ADAPTER_RANK, DOWN), BF16),
+            pltpu.VMEM((TOKENS, MODEL_WIDTH), BF16),
+            pltpu.SemaphoreType.DMA((2, 4)),
+        ],
+        compiler_params=params(60),
+        cost_estimate=COST,
+        name="lowrank",
+    )(weight, hidden)
     rank1 = jnp.concatenate([from_behind(rank, 1), rank], axis=1)
-    pair3, w2, rank = lax.optimization_barrier((pair3, w2, rank))
-    w3, s3 = score(queries, pair3, biases[0])
-    w3, rank1 = lax.optimization_barrier((w3, rank1))
-    rank2 = jnp.concatenate([from_behind(rank1, 2), rank1], axis=1)
+    pair3, rank, stats = lax.optimization_barrier((pair3, rank, stats))
+    w3, last = plain(
+        last_score_kernel,
+        "last_score",
+        (weights_shape, jax.ShapeDtypeStruct((2, columns_of), F32)),
+        queries,
+        pair3,
+        bias[:256],
+    )
     far, scale = plain(
         far_kernel,
         "far",
         (
             jax.ShapeDtypeStruct((ADAPTER_RANK, WINDOW // 2), BF16),
-            jax.ShapeDtypeStruct((4, QUERY_HEADS * TOKENS), F32),
+            jax.ShapeDtypeStruct((4, columns_of), F32),
         ),
         w3,
         w2,
-        s3,
-        s2,
-        s1,
-        s0,
+        last,
+        stats,
         reached,
     )
     near = plain(
@@ -271,11 +357,10 @@
         reached,
     )
     came = from_behind(far, -4)
-    came, rank2 = lax.optimization_barrier((came, rank2))
+    rank2 = jnp.concatenate([from_behind(rank1, 2), rank1], axis=1)
     near = near + came.astype(F32)
     rank3 = jnp.concatenate([from_behind(rank2, 4), rank2], axis=1)
     came = from_behind(near[:, :256], -2)
-    came, rank3 = lax.optimization_barrier((came, rank3))
     near = near[:, 256:] + came
     came = from_behind(near[:, :128], -1)
     ups = [

time: 180 us -> 179 us (level)
  local copies, waits for them, and re-layouts: 10.7 us -> 5.78 us
  starting transfers between devices: 57.8 us -> 61.7 us
  Pallas kernels: 19.3 us -> 22.8 us
  waiting for transfers between devices: 21 us -> 18.2 us
  blocking collectives: 68.5 us -> 66.4 us
    pallas_call x0 -> x2, Pallas kernels: none -> 10.8 us  [the longest x1 7.51 us: by_steps(): pl.pallas_call(kernel, grid=(steps,), in_specs=[spec for spec, _ in given...]
    pallas_call x14 -> x10, Pallas kernels: 19.3 us -> 12 us  [plain(): pl.pallas_call(kernel, in_specs=whole(*arrays), out_specs=jax.tree.map(la...]
    ppermute x11, waiting for transfers between devices: 10.2 us -> 3.72 us  [from_behind(): return lax.ppermute(block, 'fsdp', route)]
    unnamed x36, local copies, waits for them, and re-layouts: 8.74 us -> 3.9 us
    ppermute x11, starting transfers between devices: 38.5 us -> 42.5 us  [from_behind(): return lax.ppermute(block, 'fsdp', route)]
    all_to_all x2, waiting for transfers between devices: 10.8 us -> 14.4 us  [exchange(): return lax.all_to_all(slots, axis, 0, 0, tiled=True)]
    all_to_all x3, blocking collectives: 68.5 us -> 66.4 us  [exchange(): return lax.all_to_all(slots, axis, 0, 0, tiled=True)]
  transfers between devices with their start and end apart: 13 -> 13, of which waited for: 4 -> 5; matrix products, arithmetic and copies ran while one was open for 2% -> 2% of each run, Pallas kernels for 9% -> 12%
where the time goes in v4:
time: 179 us; the launch traced here: 178 us
  blocking collectives  66.4 us (37%)
  starting transfers between devices  61.7 us (34%)
  Pallas kernels  22.8 us (13%)
  waiting for transfers between devices  18.2 us (10%)
  local copies, waits for them, and re-layouts  5.78 us (3%)
  other arithmetic  1.89 us (1%)
    all_to_all x3, blocking collectives, exchange(): return lax.all_to_all(slots, axis, 0, 0, tiled=True)  66.4 us
    ppermute x11, starting transfers between devices, from_behind(): return lax.ppermute(block, 'fsdp', route)  42.5 us
    all_to_all x2, starting transfers between devices, exchange(): return lax.all_to_all(slots, axis, 0, 0, tiled=True)  19.2 us
    all_to_all x2, waiting for transfers between devices, exchange(): return lax.all_to_all(slots, axis, 0, 0, tiled=True)  14.4 us
    pallas_call x10, Pallas kernels, plain(): pl.pallas_call(kernel, in_specs=whole(*arrays), out_specs=jax.tree.map(la...  12 us
    pallas_call x1, Pallas kernels, by_steps(): pl.pallas_call(kernel, grid=(steps,), in_specs=[spec for spec, _ in given...  7.51 us
    unnamed x36, local copies, waits for them, and re-layouts  3.9 us
    ppermute x11, waiting for transfers between devices, from_behind(): return lax.ppermute(block, 'fsdp', route)  3.72 us
  transfers between devices with their start and end apart: 13, of which 5 were waited for; matrix products, arithmetic and copies ran while one was open for 2% of the time, Pallas kernels for 12%

profile of v4, /device:TPU:1, one launch (start us, length us, event | category | flops | bytes accessed | tf_op | source)
XLA Modules:
  0.0 177.9 jit_solution(9337614497856907089)
XLA Ops:
  0.6 7.1 %collective-permute-start = (bf16[128,512]{1,0:T(8,128)(2,1)}, bf16[128,512]{1,0:T(8,128)(2,1)S(1)}, u32[]{:S(2)}, u32[]{:S(2)}) collective-permute-start(bf16[128,512]{1,0:T(8,128)(2,1)} %param.9), channel_id=1, source_target_pairs={{0,3},{1,4},{2,5},{3,6},{4,7},{5,8},{6,9},{7,10},{8,11},{9,12},{10... | collective-permute-start | bytes 393224 | tf_op jit(solution)/shard_map/ppermute | solution.py:38
  7.7 6.1 %collective-permute-start.1 = (bf16[128,512]{1,0:T(8,128)(2,1)}, bf16[128,512]{1,0:T(8,128)(2,1)S(1)}, u32[]{:S(2)}, u32[]{:S(2)}) collective-permute-start(bf16[128,512]{1,0:T(8,128)(2,1)} %param.9), channel_id=1, source_target_pairs={{0,2},{1,3},{2,4},{3,5},{4,6},{5,7},{6,8},{7,9},{8,10},{9,11},{10,... | collective-permute-start | bytes 393224 | tf_op jit(solution)/shard_map/ppermute | solution.py:38
  13.9 3.5 %collective-permute-start.3 = (bf16[128,512]{1,0:T(8,128)(2,1)}, bf16[128,512]{1,0:T(8,128)(2,1)S(1)}, u32[]{:S(2)}, u32[]{:S(2)}) collective-permute-start(bf16[128,512]{1,0:T(8,128)(2,1)} %param.9), channel_id=1, source_target_pairs={{0,1},{1,2},{2,3},{3,4},{4,5},{5,6},{6,7},{7,8},{8,9},{9,10},{10,1... | collective-permute-start | bytes 393224 | tf_op jit(solution)/shard_map/ppermute | solution.py:38
  18.9 11.2 %all-to-all-start = ((bf16[32,16,128]{2,1,0:T(8,128)(2,1)}), bf16[32,16,128]{2,1,0:T(8,128)(2,1)S(1)}, u32[]{:S(2)}, u32[]{:S(2)}) async-start(bf16[32,16,128]{2,1,0:T(8,128)(2,1)} %broadcast_in_dim.28), calls=%async_computation | async-start | bytes 262144 | tf_op jit(solution)/shard_map/all_to_all | solution.py:42
  33.5 4.0 %collective-permute-start.2 = (bf16[256,512]{1,0:T(8,128)(2,1)S(1)}, bf16[256,512]{1,0:T(8,128)(2,1)S(1)}, u32[]{:S(2)}, u32[]{:S(2)}) collective-permute-start(bf16[256,512]{1,0:T(8,128)(2,1)S(1)} %constant_dynamic-update-slice_fusion.keys1_ref), channel_id=1, source_target_pairs={{0,2},{1,3},{2,4},{3,5},{4,6},{5,7},{6,8},{7,9},{8,10},{9,11},{10,... | collective-permute-start | bytes 786440 | tf_op jit(solution)/shard_map/ppermute | solution.py:38
  38.3 7.6 %all-to-all-done = bf16[32,16,128]{2,1,0:T(8,128)(2,1)S(1)} async-done(((bf16[32,16,128]{2,1,0:T(8,128)(2,1)}), bf16[32,16,128]{2,1,0:T(8,128)(2,1)S(1)}, u32[]{:S(2)}, u32[]{:S(2)}) %all-to-all-start) | async-done | bytes 131104 | tf_op jit(solution)/shard_map/all_to_all | solution.py:42
  47.0 7.9 %all-to-all-start.1 = ((bf16[16,8,4096]{2,1,0:T(8,128)(2,1)}), bf16[16,8,4096]{2,1,0:T(8,128)(2,1)S(1)}, u32[]{:S(2)}, u32[]{:S(2)}) async-start(bf16[16,8,4096]{2,1,0:T(8,128)(2,1)} %broadcast_in_dim.30), calls=%async_computation.1 | async-start | bytes 2097152 | tf_op jit(solution)/shard_map/all_to_all | solution.py:42
  55.0 1.9 %collective-permute-start.4 = (bf16[256,512]{1,0:T(8,128)(2,1)S(1)}, bf16[256,512]{1,0:T(8,128)(2,1)S(1)}, u32[]{:S(2)}, u32[]{:S(2)}) collective-permute-start(bf16[256,512]{1,0:T(8,128)(2,1)S(1)} %collective-permute-done.2.keys2_ref), channel_id=1, source_target_pairs={{0,2},{1,3},{2,4},{3,5},{4,6},{5,7},{6,8},{7,9},{8,10},{9,11},{10,... | collective-permute-start | bytes 786440 | tf_op jit(solution)/shard_map/ppermute | solution.py:38
  58.1 7.5 %score.1 = (bf16[256,4096]{1,0:T(8,128)(2,1)}, bf16[256,4096]{1,0:T(8,128)(2,1)}, bf16[256,4096]{1,0:T(8,128)(2,1)}, f32[8,4096]{1,0:T(8,128)}) custom-call(bf16[128,4096]{1,0:T(8,128)(2,1)} %query_ref.3, bf16[256,512]{1,0:T(8,128)(2,1)} %copy-done.16, bf16[256,512]{1,0:T(8,128)(2,1)} %copy-done.14, bf16[256,512]{1,0:T(8,128)(2,1)} %pad_maximum_fusion.keys0_ref, ...), custom_call_target="tpu_custom_call" | custom-call | flops 10000000000 | bytes 134217728 | tf_op jit(solution)/shard_map/score/pallas_call | solution.py:235
  65.6 6.8 %all-to-all-done.1 = bf16[16,8,4096]{2,1,0:T(8,128)(2,1)S(1)} async-done(((bf16[16,8,4096]{2,1,0:T(8,128)(2,1)}), bf16[16,8,4096]{2,1,0:T(8,128)(2,1)S(1)}, u32[]{:S(2)}, u32[]{:S(2)}) %all-to-all-start.1) | async-done | bytes 1048608 | tf_op jit(solution)/shard_map/all_to_all | solution.py:42
  73.4 3.3 %lowrank.1 = bf16[64,128]{1,0:T(8,128)(2,1)} custom-call(bf16[2,64,4096]{2,1,0:T(8,128)(2,1)} %bitcast.16, bf16[128,8192]{1,0:T(8,128)(2,1)} %hidden_ref.1), custom_call_target="tpu_custom_call" | custom-call | flops 10000000000 | bytes 134217728 | tf_op jit(solution)/shard_map/lowrank/pallas_call | solution.py:313
  76.7 2.5 %collective-permute-start.8 = (bf16[64,128]{1,0:T(8,128)(2,1)}, bf16[64,128]{1,0:T(8,128)(2,1)S(1)}, u32[]{:S(2)}, u32[]{:S(2)}) collective-permute-start(bf16[64,128]{1,0:T(8,128)(2,1)} %lowrank.1), channel_id=1, source_target_pairs={{0,1},{1,2},{2,3},{3,4},{4,5},{5,6},{6,7},{7,8},{8,9},{9,10},{10,1... | collective-permute-start | bytes 49160 | tf_op jit(solution)/shard_map/ppermute | solution.py:38
  79.3 2.1 %last_score.1 = (bf16[256,4096]{1,0:T(8,128)(2,1)S(1)}, f32[2,4096]{1,0:T(2,128)S(1)}) custom-call(bf16[128,4096]{1,0:T(8,128)(2,1)S(1)} %copy-done.2, bf16[256,512]{1,0:T(8,128)(2,1)S(1)} %collective-permute-done.4.keys_ref, f32[256,128]{1,0:T(8,128)S(1)} %slice.30.bias_ref), custom_call_target="tpu_custom_call" | custom-call | flops 10000000000 | bytes 134217728 | tf_op jit(solution)/shard_map/last_score/pallas_call | solution.py:223
  81.4 1.3 far.1
  82.8 1.3 collective-permute-start.5
  85.4 1.3 near.1
  86.8 12.0 %collective-permute-start.10 = (bf16[64,512]{1,0:T(8,128)(2,1)S(1)}, bf16[64,512]{1,0:T(8,128)(2,1)S(1)}, u32[]{:S(2)}, u32[]{:S(2)}) collective-permute-start(bf16[64,512]{1,0:T(8,128)(2,1)S(1)} %pad_maximum_fusion.2), channel_id=1, source_target_pairs={{0,4},{1,5},{2,6},{3,7},{4,8},{5,9},{6,10},{7,11},{8,12},{9,13},{1... | collective-permute-start | bytes 196616 | tf_op jit(solution)/shard_map/ppermute | solution.py:38
  100.5 2.4 %mixed.2.up0_ref = f32[64,256]{1,0:T(8,128)S(1)} custom-call(bf16[256,4096]{1,0:T(8,128)(2,1)S(1)} %get-tuple-element.20.w3_ref, bf16[256,4096]{1,0:T(8,128)(2,1)S(1)} %copy-done.6, bf16[256,4096]{1,0:T(8,128)(2,1)S(1)} %copy-done.7, bf16[256,4096]{1,0:T(8,128)(2,1)S(1)} %copy-done.8, f32[4,4096]{1,0:T(4,128)S(1)} %get-tuple-element.24.scale_ref, ...), custom_call_target="tpu_custom_call" | custom-call | flops 10000000000 | bytes 134217728 | tf_op jit(solution)/shard_map/mixed/pallas_call | solution.py:223
  102.9 2.4 %collective-permute-done.6 = f32[64,256]{1,0:T(8,128)S(1)} collective-permute-done((f32[64,256]{1,0:T(8,128)S(1)}, f32[64,256]{1,0:T(8,128)S(1)}, u32[]{:S(2)}, u32[]{:S(2)}) %collective-permute-start.6) | collective-permute-done | bytes 65568 | tf_op jit(solution)/shard_map/ppermute | solution.py:38
  105.4 1.4 collective-permute-start.7
  106.8 2.4 %mixed.3.up1_ref = f32[64,256]{1,0:T(8,128)S(1)} custom-call(bf16[256,4096]{1,0:T(8,128)(2,1)S(1)} %get-tuple-element.20.w3_ref, bf16[256,4096]{1,0:T(8,128)(2,1)S(1)} %copy-done.6, bf16[256,4096]{1,0:T(8,128)(2,1)S(1)} %copy-done.7, bf16[256,4096]{1,0:T(8,128)(2,1)S(1)} %copy-done.8, f32[4,4096]{1,0:T(4,128)S(1)} %get-tuple-element.24.scale_ref, ...), custom_call_target="tpu_custom_call" | custom-call | flops 10000000000 | bytes 134217728 | tf_op jit(solution)/shard_map/mixed/pallas_call | solution.py:223
  110.6 27.6 %all_to_all.25.in_ref = bf16[16,8,4352]{2,1,0:T(8,128)(2,1)S(1)} all-to-all(bf16[16,8,4352]{2,1,0:T(8,128)(2,1)S(1)} %bitcast.15), channel_id=1, replica_groups=mesh['dp'=16,'fsdp'=32] {'dp'}, dimensions={0} | all-to-all | bytes 2228224 | tf_op jit(solution)/shard_map/all_to_all | solution.py:42
  138.4 26.7 %all_to_all.26.in_ref = bf16[32,8,384]{2,1,0:T(8,128)(2,1)S(1)} all-to-all(bf16[32,8,384]{2,1,0:T(8,128)(2,1)S(1)} %fold_dp.1), channel_id=1, replica_groups=mesh['dp'=16,'fsdp'=32] {'fsdp'}, dimensions={0} | all-to-all | bytes 393216 | tf_op jit(solution)/shard_map/all_to_all | solution.py:42
  165.2 12.0 %all_to_all.27.in_ref = f32[16,8,384]{2,1,0:T(8,128)S(1)} all-to-all(f32[16,8,384]{2,1,0:T(8,128)S(1)} %fold_fsdp.1), channel_id=1, replica_groups=mesh['dp'=16,'fsdp'=32] {'dp'}, dimensions={0} | all-to-all | bytes 393216 | tf_op jit(solution)/shard_map/all_to_all | solution.py:42
  (76 shorter events, 14.0 us)
Async XLA Ops:
  0.6 17.6 %copy-start = (bf16[256,64]{0,1:T(8,128)(2,1)S(1)}, bf16[256,64]{0,1:T(8,128)(2,1)}, u32[]{:S(2)}) copy-start(bf16[256,64]{0,1:T(8,128)(2,1)} %param.11) | copy-start | bytes 98308
  0.6 32.8 %collective-permute-start = (bf16[128,512]{1,0:T(8,128)(2,1)}, bf16[128,512]{1,0:T(8,128)(2,1)S(1)}, u32[]{:S(2)}, u32[]{:S(2)}) collective-permute-start(bf16[128,512]{1,0:T(8,128)(2,1)} %param.9), channel_id=1, source_target_pairs={{0,3},{1,4},{2,5},{3,6},{4,7},{5,8},{6,9},{7,10},{8,11},{9,12},{10... | collective-permute-start | bytes 393224 | tf_op jit(solution)/shard_map/ppermute | solution.py:38
  7.7 25.7 %collective-permute-start.1 = (bf16[128,512]{1,0:T(8,128)(2,1)}, bf16[128,512]{1,0:T(8,128)(2,1)S(1)}, u32[]{:S(2)}, u32[]{:S(2)}) collective-permute-start(bf16[128,512]{1,0:T(8,128)(2,1)} %param.9), channel_id=1, source_target_pairs={{0,2},{1,3},{2,4},{3,5},{4,6},{5,7},{6,8},{7,9},{8,10},{9,11},{10,... | collective-permute-start | bytes 393224 | tf_op jit(solution)/shard_map/ppermute | solution.py:38
  13.9 23.7 %collective-permute-start.3 = (bf16[128,512]{1,0:T(8,128)(2,1)}, bf16[128,512]{1,0:T(8,128)(2,1)S(1)}, u32[]{:S(2)}, u32[]{:S(2)}) collective-permute-start(bf16[128,512]{1,0:T(8,128)(2,1)} %param.9), channel_id=1, source_target_pairs={{0,1},{1,2},{2,3},{3,4},{4,5},{5,6},{6,7},{7,8},{8,9},{9,10},{10,1... | collective-permute-start | bytes 393224 | tf_op jit(solution)/shard_map/ppermute | solution.py:38
  18.9 27.0 %all-to-all-start = ((bf16[32,16,128]{2,1,0:T(8,128)(2,1)}), bf16[32,16,128]{2,1,0:T(8,128)(2,1)S(1)}, u32[]{:S(2)}, u32[]{:S(2)}) async-start(bf16[32,16,128]{2,1,0:T(8,128)(2,1)} %broadcast_in_dim.28), calls=%async_computation | async-start | bytes 262144 | tf_op jit(solution)/shard_map/all_to_all | solution.py:42
  32.2 5.3 %copy-start.13 = (bf16[128,512]{1,0:T(8,128)(2,1)S(1)}, bf16[128,512]{1,0:T(8,128)(2,1)}, u32[]{:S(2)}) copy-start(bf16[128,512]{1,0:T(8,128)(2,1)} %param.9) | copy-start | bytes 393220
  33.4 23.5 %copy-start.15 = (s32[1,128]{1,0:T(1,128)S(1)}, s32[1,128]{1,0:T(1,128)}, u32[]{:S(2)}) copy-start(s32[1,128]{1,0:T(1,128)} %param.10) | copy-start | bytes 1540
  33.5 23.8 %copy-start.14 = (bf16[256,512]{1,0:T(8,128)(2,1)}, bf16[256,512]{1,0:T(8,128)(2,1)S(1)}, u32[]{:S(2)}) copy-start(bf16[256,512]{1,0:T(8,128)(2,1)S(1)} %constant_dynamic-update-slice_fusion.keys1_ref) | copy-start | bytes 786436
  33.5 21.5 %collective-permute-start.2 = (bf16[256,512]{1,0:T(8,128)(2,1)S(1)}, bf16[256,512]{1,0:T(8,128)(2,1)S(1)}, u32[]{:S(2)}, u32[]{:S(2)}) collective-permute-start(bf16[256,512]{1,0:T(8,128)(2,1)S(1)} %constant_dynamic-update-slice_fusion.keys1_ref), channel_id=1, source_target_pairs={{0,2},{1,3},{2,4},{3,5},{4,6},{5,7},{6,8},{7,9},{8,10},{9,11},{10,... | collective-permute-start | bytes 786440 | tf_op jit(solution)/shard_map/ppermute | solution.py:38
  47.0 25.5 %all-to-all-start.1 = ((bf16[16,8,4096]{2,1,0:T(8,128)(2,1)}), bf16[16,8,4096]{2,1,0:T(8,128)(2,1)S(1)}, u32[]{:S(2)}, u32[]{:S(2)}) async-start(bf16[16,8,4096]{2,1,0:T(8,128)(2,1)} %broadcast_in_dim.30), calls=%async_computation.1 | async-start | bytes 2097152 | tf_op jit(solution)/shard_map/all_to_all | solution.py:42
  54.9 2.4 %copy-start.16 = (bf16[256,512]{1,0:T(8,128)(2,1)}, bf16[256,512]{1,0:T(8,128)(2,1)S(1)}, u32[]{:S(2)}) copy-start(bf16[256,512]{1,0:T(8,128)(2,1)S(1)} %collective-permute-done.2.keys2_ref) | copy-start | bytes 786436
  55.0 24.2 %collective-permute-start.4 = (bf16[256,512]{1,0:T(8,128)(2,1)S(1)}, bf16[256,512]{1,0:T(8,128)(2,1)S(1)}, u32[]{:S(2)}, u32[]{:S(2)}) collective-permute-start(bf16[256,512]{1,0:T(8,128)(2,1)S(1)} %collective-permute-done.2.keys2_ref), channel_id=1, source_target_pairs={{0,2},{1,3},{2,4},{3,5},{4,6},{5,7},{6,8},{7,9},{8,10},{9,11},{10,... | collective-permute-start | bytes 786440 | tf_op jit(solution)/shard_map/ppermute | solution.py:38
  73.4 5.8 %copy-start.2 = (bf16[128,4096]{1,0:T(8,128)(2,1)S(1)}, bf16[128,4096]{1,0:T(8,128)(2,1)}, u32[]{:S(2)}) copy-start(bf16[128,4096]{1,0:T(8,128)(2,1)} %query_ref.3) | copy-start | bytes 3145732
  76.7 7.4 %collective-permute-start.8 = (bf16[64,128]{1,0:T(8,128)(2,1)}, bf16[64,128]{1,0:T(8,128)(2,1)S(1)}, u32[]{:S(2)}, u32[]{:S(2)}) collective-permute-start(bf16[64,128]{1,0:T(8,128)(2,1)} %lowrank.1), channel_id=1, source_target_pairs={{0,1},{1,2},{2,3},{3,4},{4,5},{5,6},{6,7},{7,8},{8,9},{9,10},{10,1... | collective-permute-start | bytes 49160 | tf_op jit(solution)/shard_map/ppermute | solution.py:38
  81.4 2.7 %copy-start.12 = (bf16[64,128]{1,0:T(8,128)(2,1)S(1)}, bf16[64,128]{1,0:T(8,128)(2,1)}, u32[]{:S(2)}) copy-start(bf16[64,128]{1,0:T(8,128)(2,1)} %lowrank.1) | copy-start | bytes 49156
  81.4 4.0 %copy-start.7 = (bf16[256,4096]{1,0:T(8,128)(2,1)S(1)}, bf16[256,4096]{1,0:T(8,128)(2,1)}, u32[]{:S(2)}) copy-start(bf16[256,4096]{1,0:T(8,128)(2,1)} %get-tuple-element.16.w1_ref) | copy-start | bytes 6291460
  81.4 4.0 %copy-start.8 = (bf16[256,4096]{1,0:T(8,128)(2,1)S(1)}, bf16[256,4096]{1,0:T(8,128)(2,1)}, u32[]{:S(2)}) copy-start(bf16[256,4096]{1,0:T(8,128)(2,1)} %get-tuple-element.17.w0_ref) | copy-start | bytes 6291460
  82.8 16.0 %collective-permute-start.5 = (bf16[64,512]{1,0:T(8,128)(2,1)S(1)}, bf16[64,512]{1,0:T(8,128)(2,1)S(1)}, u32[]{:S(2)}, u32[]{:S(2)}) collective-permute-start(bf16[64,512]{1,0:T(8,128)(2,1)S(1)} %get-tuple-element.25), channel_id=1, source_target_pairs={{4,0},{5,1},{6,2},{7,3},{8,4},{9,5},{10,6},{11,7},{12,8},{13,9},{1... | collective-permute-start | bytes 196616 | tf_op jit(solution)/shard_map/ppermute | solution.py:38
  84.1 2.6 %collective-permute-start.9 = (bf16[64,256]{1,0:T(8,128)(2,1)S(1)}, bf16[64,256]{1,0:T(8,128)(2,1)S(1)}, u32[]{:S(2)}, u32[]{:S(2)}) collective-permute-start(bf16[64,256]{1,0:T(8,128)(2,1)S(1)} %pad_maximum_fusion.3), channel_id=1, source_target_pairs={{0,2},{1,3},{2,4},{3,5},{4,6},{5,7},{6,8},{7,9},{8,10},{9,11},{10,... | collective-permute-start | bytes 98312 | tf_op jit(solution)/shard_map/ppermute | solution.py:38
  85.4 15.1 %copy-start.4 = (bf16[128,4096]{1,0:T(8,128)(2,1)S(1)}, bf16[128,4096]{1,0:T(8,128)(2,1)}, u32[]{:S(2)}) copy-start(bf16[128,4096]{1,0:T(8,128)(2,1)} %gradient_ref.5) | copy-start | bytes 3145732
  86.8 13.7 %collective-permute-start.10 = (bf16[64,512]{1,0:T(8,128)(2,1)S(1)}, bf16[64,512]{1,0:T(8,128)(2,1)S(1)}, u32[]{:S(2)}, u32[]{:S(2)}) collective-permute-start(bf16[64,512]{1,0:T(8,128)(2,1)S(1)} %pad_maximum_fusion.2), channel_id=1, source_target_pairs={{0,4},{1,5},{2,6},{3,7},{4,8},{5,9},{6,10},{7,11},{8,12},{9,13},{1... | collective-permute-start | bytes 196616 | tf_op jit(solution)/shard_map/ppermute | solution.py:38
  98.8 6.5 %collective-permute-start.6 = (f32[64,256]{1,0:T(8,128)S(1)}, f32[64,256]{1,0:T(8,128)S(1)}, u32[]{:S(2)}, u32[]{:S(2)}) collective-permute-start(f32[64,256]{1,0:T(8,128)S(1)} %slice.32), channel_id=1, source_target_pairs={{2,0},{3,1},{4,2},{5,3},{6,4},{7,5},{8,6},{9,7},{10,8},{11,9},{12,... | collective-permute-start | bytes 196616 | tf_op jit(solution)/shard_map/ppermute | solution.py:38
  105.3 4.8 %copy-start.1 = (bf16[128,8192]{1,0:T(8,128)(2,1)S(1)}, bf16[128,8192]{1,0:T(8,128)(2,1)}, u32[]{:S(2)}) copy-start(bf16[128,8192]{1,0:T(8,128)(2,1)} %hidden_ref.1) | copy-start | bytes 6291460
  105.4 4.8 %collective-permute-start.7 = (f32[64,128]{1,0:T(8,128)S(1)}, f32[64,128]{1,0:T(8,128)S(1)}, u32[]{:S(2)}, u32[]{:S(2)}) collective-permute-start(f32[64,128]{1,0:T(8,128)S(1)} %slice.34), channel_id=1, source_target_pairs={{1,0},{2,1},{3,2},{4,3},{5,4},{6,5},{7,6},{8,7},{9,8},{10,9},{11,1... | collective-permute-start | bytes 98312 | tf_op jit(solution)/shard_map/ppermute | solution.py:38
  (6 other events, 8.2 us)

commit v5 on v4

--- a/solution.py
+++ b/solution.py
@@ -42,35 +42,15 @@
     return lax.all_to_all(slots, axis, 0, 0, tiled=True)
 
 
-def lowrank_kernel(weight_hbm, hidden_hbm, out_ref, weight_ref, hidden_ref, arrived):
-    copies = []
-    for j in range(4):
-        lanes = pl.ds(j * 1024, 1024)
-        wide = pl.ds(j * 2048, 2048)
-        copies.append(
-            (
-                pltpu.make_async_copy(
-                    weight_hbm.at[:, :, lanes], weight_ref.at[:, :, lanes], arrived.at[0, j]
-                ),
-                pltpu.make_async_copy(
-                    hidden_hbm.at[:, wide], hidden_ref.at[:, wide], arrived.at[1, j]
-                ),
-            )
+def lowrank_kernel(weight_ref, hidden_ref, out_ref):
+    total = jnp.zeros((ADAPTER_RANK, TOKENS), F32)
+    for f in range(N_FSDP):
+        rows = jnp.concatenate(
+            [weight_ref[half, :, f * 128 : f * 128 + 128] for half in range(2)], axis=1
         )
-    for pair in copies:
-        for copy in pair:
-            copy.start()
-    total = jnp.zeros((ADAPTER_RANK, TOKENS), F32)
-    for j, pair in enumerate(copies):
-        for copy in pair:
-            copy.wait()
-        for f in range(8 * j, 8 * j + 8):
-            rows = jnp.concatenate(
-                [weight_ref[half, :, f * 128 : f * 128 + 128] for half in range(2)], axis=1
-            )
-            total += lax.dot_general(
-                rows, hidden_ref[:, f * 256 : f * 256 + 256], NT, preferred_element_type=F32
-            )
+        total += lax.dot_general(
+            rows, hidden_ref[:, f * 256 : f * 256 + 256], NT, preferred_element_type=F32
+        )
     out_ref[...] = total.astype(BF16)
 
 
@@ -183,20 +163,31 @@
 LANES = DOWN + 256
 
 
-def shares_kernel(key_ref, hidden_ref, up0_ref, up1_ref, out_ref):
-    for f in range(N_FSDP):
-        product = jnp.dot(
-            key_ref[...], hidden_ref[:, f * 256 : f * 256 + 256], preferred_element_type=F32
-        ).astype(BF16)
-        for half in range(2):
-            out_ref[half, :, f * 128 : f * 128 + 128] = product[:, half * 128 : half * 128 + 128]
-    for half, up_ref in enumerate((up0_ref, up1_ref)):
-        out_ref[half, :, DOWN:] = up_ref[...].astype(BF16)
+def shares_kernel(core_ref, key_ref, hidden_ref, up0_ref, up1_ref, own_ref, other_ref):
+    for core in range(2):
+
+        @pl.when(core_ref[0] == core)
+        def _(core=core):
+            halves = (own_ref, other_ref) if core == 0 else (other_ref, own_ref)
+            for f in range(N_FSDP):
+                product = jnp.dot(
+                    key_ref[...], hidden_ref[:, f * 256 : f * 256 + 256], preferred_element_type=F32
+                )
+                for half, ref in enumerate(halves):
+                    ref[:, f * 128 : f * 128 + 128] = product[:, half * 128 : half * 128 + 128]
+            halves[0][:, DOWN:] = up0_ref[...]
+            halves[1][:, DOWN:] = up1_ref[...]
+
+
+def add_kernel(own_ref, other_ref, out_ref):
+    for part in range(8):
+        rows = slice(part * 8, part * 8 + 8)
+        out_ref[part] = (own_ref[rows, :] + other_ref[rows, :]).astype(BF16)
 
 
 def fold_dp_kernel(in_ref, out_ref):
     def total(columns):
-        return sum(in_ref[d, :, columns].astype(F32) for d in range(N_DP))
+        return sum(in_ref[d, :, columns].astype(F32) for d in range(N_DP // 2))
 
     up = total(slice(DOWN, LANES)).astype(BF16)
     for f in range(N_FSDP):
@@ -214,7 +205,7 @@
     for half in range(2):
         for part in range(8):
             rows = slice(part * 8, part * 8 + 8)
-            block = in_ref[half * 8 + part]
+            block = in_ref[part * 2 + half]
             down_ref[rows, half * 128 : half * 128 + 128] = block[:, :128]
             up_ref[rows, half * 256 : half * 256 + 256] = block[:, 128:]
 
@@ -307,25 +298,14 @@
         "reached",
         jax.ShapeDtypeStruct((ADAPTER_RANK, columns_of), BF16),
         output_gradient,
-        adapter_up_weight,
-    )
-    anywhere = pl.BlockSpec(memory_space=pl.ANY)
-    rank = pl.pallas_call(
-        lowrank_kernel,
-        in_specs=[anywhere, anywhere],
-        out_specs=pl.BlockSpec(memory_space=pltpu.VMEM),
-        out_shape=jax.ShapeDtypeStruct((ADAPTER_RANK, TOKENS), BF16),
-        scratch_shapes=[
-            pltpu.VMEM((2, ADAPTER_RANK, DOWN), BF16),
-            pltpu.VMEM((TOKENS, MODEL_WIDTH), BF16),
-            pltpu.SemaphoreType.DMA((2, 4)),
-        ],
-        compiler_params=params(60),
-        cost_estimate=COST,
-        name="lowrank",
-    )(weight, hidden)
+        lax.optimization_barrier((adapter_up_weight, stats))[0],
+    )
+    rank = plain(
+        lowrank_kernel, "lowrank", jax.ShapeDtypeStruct((ADAPTER_RANK, TOKENS), BF16), weight, hidden
+    )
     rank1 = jnp.concatenate([from_behind(rank, 1), rank], axis=1)
-    pair3, rank, stats = lax.optimization_barrier((pair3, rank, stats))
+    pair3, rank1, stats = lax.optimization_barrier((pair3, rank1, stats))
+    rank2 = jnp.concatenate([from_behind(rank1, 2), rank1], axis=1)
     w3, last = plain(
         last_score_kernel,
         "last_score",
@@ -334,6 +314,7 @@
         pair3,
         bias[:256],
     )
+    w3, rank2 = lax.optimization_barrier((w3, rank2))
     far, scale = plain(
         far_kernel,
         "far",
@@ -357,7 +338,6 @@
         reached,
     )
     came = from_behind(far, -4)
-    rank2 = jnp.concatenate([from_behind(rank1, 2), rank1], axis=1)
     near = near + came.astype(F32)
     rank3 = jnp.concatenate([from_behind(rank2, 4), rank2], axis=1)
     came = from_behind(near[:, :256], -2)
@@ -380,15 +360,22 @@
     ]
     key_grad = (near[:, 128:] + came).astype(BF16)
 
+    share = jax.ShapeDtypeStruct((ADAPTER_RANK, LANES), F32)
+    own, other = pl.pallas_call(
+        shares_kernel,
+        in_specs=[pl.BlockSpec(memory_space=pltpu.SMEM)] + whole(key_grad, hidden, *ups),
+        out_specs=whole(share, share),
+        out_shape=(share, share),
+        compiler_params=params(20),
+        cost_estimate=COST,
+        name="shares",
+    )((member % 2).astype(jnp.int32).reshape(1), key_grad, hidden, *ups)
+    other = lax.ppermute(other, "dp", [(d, d ^ 1) for d in range(N_DP)])
     shares = plain(
-        shares_kernel,
-        "shares",
-        jax.ShapeDtypeStruct((2, ADAPTER_RANK, LANES), BF16),
-        key_grad,
-        hidden,
-        *ups,
-    )
-    shares = exchange(shares.reshape(N_DP, 8, LANES), "dp")
+        add_kernel, "add", jax.ShapeDtypeStruct((N_DP // 2, 8, LANES), BF16), own, other
+    )
+    groups = [list(range(core, N_DP, 2)) for core in range(2)]
+    shares = lax.all_to_all(shares, "dp", 0, 0, axis_index_groups=groups, tiled=True)
     shares = plain(
         fold_dp_kernel, "fold_dp", jax.ShapeDtypeStruct((N_FSDP, 8, 384), BF16), shares
     )

time: 179 us -> 189 us (1.056)
  starting transfers between devices: 61.7 us -> 79.3 us
  local copies, waits for them, and re-layouts: 5.78 us -> 2.86 us
  waiting for transfers between devices: 18.2 us -> 15.5 us
  Pallas kernels: 22.8 us -> 20.6 us
    all_to_all x3 -> x2, blocking collectives: 66.4 us -> 49.9 us  [exchange(): return lax.all_to_all(slots, axis, 0, 0, tiled=True)]
    all_to_all x0 -> x1, blocking collectives: none -> 15.1 us  [local(): lax.all_to_all(shares, 'dp', 0, 0, axis_index_groups=groups, tiled=True)]
    all_to_all x2, waiting for transfers between devices: 14.4 us -> 5.79 us  [exchange(): return lax.all_to_all(slots, axis, 0, 0, tiled=True)]
    ppermute x0 -> x1, starting transfers between devices: none -> 6.55 us  [local(): other = lax.ppermute(other, 'dp', [(d, d ^ 1) for d in range(N_DP)])]
    all_to_all x2, starting transfers between devices: 19.2 us -> 24.9 us  [exchange(): return lax.all_to_all(slots, axis, 0, 0, tiled=True)]
    ppermute x11, starting transfers between devices: 42.5 us -> 47.8 us  [from_behind(): return lax.ppermute(block, 'fsdp', route)]
    unnamed x36 -> x25, local copies, waits for them, and re-layouts: 3.9 us -> 0.08 us
    ppermute x11, waiting for transfers between devices: 3.72 us -> 7.31 us  [from_behind(): return lax.ppermute(block, 'fsdp', route)]
  transfers between devices with their start and end apart: 13 -> 14, of which waited for: 5 -> 5; matrix products, arithmetic and copies ran while one was open for 2% -> 3% of each run, Pallas kernels for 12% -> 10%
where the time goes in v5:
time: 189 us; the launch traced here: 188 us
  starting transfers between devices  79.3 us (42%)
  blocking collectives  65 us (34%)
  Pallas kernels  20.6 us (11%)
  waiting for transfers between devices  15.5 us (8%)
  other arithmetic  3.61 us (2%)
  local copies, waits for them, and re-layouts  2.86 us (2%)
    all_to_all x2, blocking collectives, exchange(): return lax.all_to_all(slots, axis, 0, 0, tiled=True)  49.9 us
    ppermute x11, starting transfers between devices, from_behind(): return lax.ppermute(block, 'fsdp', route)  47.8 us
    all_to_all x2, starting transfers between devices, exchange(): return lax.all_to_all(slots, axis, 0, 0, tiled=True)  24.9 us
    all_to_all x1, blocking collectives, local(): lax.all_to_all(shares, 'dp', 0, 0, axis_index_groups=groups, tiled=True)  15.1 us
    pallas_call x11, Pallas kernels, plain(): pl.pallas_call(kernel, in_specs=whole(*arrays), out_specs=jax.tree.map(la...  12.4 us
    pallas_call x1, Pallas kernels, by_steps(): pl.pallas_call(kernel, grid=(steps,), in_specs=[spec for spec, _ in given...  7.66 us
    ppermute x11, waiting for transfers between devices, from_behind(): return lax.ppermute(block, 'fsdp', route)  7.31 us
    ppermute x1, starting transfers between devices, local(): other = lax.ppermute(other, 'dp', [(d, d ^ 1) for d in range(N_DP)])  6.55 us
  transfers between devices with their start and end apart: 14, of which 5 were waited for; matrix products, arithmetic and copies ran while one was open for 3% of the time, Pallas kernels for 10%

profile of v5, /device:TPU:1, one launch (start us, length us, event | category | flops | bytes accessed | tf_op | source)
XLA Modules:
  0.0 187.9 jit_solution(5044706042954378512)
XLA Ops:
  2.2 18.7 %all-to-all-start = ((bf16[32,16,128]{2,1,0:T(8,128)(2,1)}), bf16[32,16,128]{2,1,0:T(8,128)(2,1)S(1)}, u32[]{:S(2)}, u32[]{:S(2)}) async-start(bf16[32,16,128]{2,1,0:T(8,128)(2,1)} %broadcast_in_dim.28), calls=%async_computation | async-start | bytes 262144 | tf_op jit(solution)/shard_map/all_to_all | solution.py:42
  20.8 4.9 %collective-permute-start = (bf16[128,512]{1,0:T(8,128)(2,1)}, bf16[128,512]{1,0:T(8,128)(2,1)S(1)}, u32[]{:S(2)}, u32[]{:S(2)}) collective-permute-start(bf16[128,512]{1,0:T(8,128)(2,1)} %param.9), channel_id=1, source_target_pairs={{0,3},{1,4},{2,5},{3,6},{4,7},{5,8},{6,9},{7,10},{8,11},{9,12},{10... | collective-permute-start | bytes 393224 | tf_op jit(solution)/shard_map/ppermute | solution.py:38
  25.8 5.2 %collective-permute-start.1 = (bf16[128,512]{1,0:T(8,128)(2,1)}, bf16[128,512]{1,0:T(8,128)(2,1)S(1)}, u32[]{:S(2)}, u32[]{:S(2)}) collective-permute-start(bf16[128,512]{1,0:T(8,128)(2,1)} %param.9), channel_id=1, source_target_pairs={{0,2},{1,3},{2,4},{3,5},{4,6},{5,7},{6,8},{7,9},{8,10},{9,11},{10,... | collective-permute-start | bytes 393224 | tf_op jit(solution)/shard_map/ppermute | solution.py:38
  31.0 3.1 %collective-permute-start.3 = (bf16[128,512]{1,0:T(8,128)(2,1)}, bf16[128,512]{1,0:T(8,128)(2,1)S(1)}, u32[]{:S(2)}, u32[]{:S(2)}) collective-permute-start(bf16[128,512]{1,0:T(8,128)(2,1)} %param.9), channel_id=1, source_target_pairs={{0,1},{1,2},{2,3},{3,4},{4,5},{5,6},{6,7},{7,8},{8,9},{9,10},{10,1... | collective-permute-start | bytes 393224 | tf_op jit(solution)/shard_map/ppermute | solution.py:38
  34.2 4.1 %collective-permute-done.1 = bf16[128,512]{1,0:T(8,128)(2,1)S(1)} collective-permute-done((bf16[128,512]{1,0:T(8,128)(2,1)}, bf16[128,512]{1,0:T(8,128)(2,1)S(1)}, u32[]{:S(2)}, u32[]{:S(2)}) %collective-permute-start.1) | collective-permute-done | bytes 131104 | tf_op jit(solution)/shard_map/ppermute | solution.py:38
  38.3 6.7 %collective-permute-start.2 = (bf16[256,512]{1,0:T(8,128)(2,1)S(1)}, bf16[256,512]{1,0:T(8,128)(2,1)}, u32[]{:S(2)}, u32[]{:S(2)}) collective-permute-start(bf16[256,512]{1,0:T(8,128)(2,1)S(1)} %constant_dynamic-update-slice_fusion.keys1_ref), channel_id=1, source_target_pairs={{0,2},{1,3},{2,4},{3,5},{4,6},{5,7},{6,8},{7,9},{8,10},{9,11},{10,... | collective-permute-start | bytes 786440 | tf_op jit(solution)/shard_map/ppermute | solution.py:38
  45.0 1.6 pad_maximum_fusion.keys0_ref
  47.7 6.3 %all-to-all-start.1 = ((bf16[16,8,4096]{2,1,0:T(8,128)(2,1)}), bf16[16,8,4096]{2,1,0:T(8,128)(2,1)S(1)}, u32[]{:S(2)}, u32[]{:S(2)}) async-start(bf16[16,8,4096]{2,1,0:T(8,128)(2,1)} %broadcast_in_dim.30), calls=%async_computation.1 | async-start | bytes 2097152 | tf_op jit(solution)/shard_map/all_to_all | solution.py:42
  54.1 4.4 %collective-permute-start.4 = (bf16[256,512]{1,0:T(8,128)(2,1)}, bf16[256,512]{1,0:T(8,128)(2,1)S(1)}, u32[]{:S(2)}, u32[]{:S(2)}) collective-permute-start(bf16[256,512]{1,0:T(8,128)(2,1)} %collective-permute-done.2.keys2_ref), channel_id=1, source_target_pairs={{0,2},{1,3},{2,4},{3,5},{4,6},{5,7},{6,8},{7,9},{8,10},{9,11},{10,... | collective-permute-start | bytes 786440 | tf_op jit(solution)/shard_map/ppermute | solution.py:38
  59.7 7.7 %score.1 = (bf16[256,4096]{1,0:T(8,128)(2,1)}, bf16[256,4096]{1,0:T(8,128)(2,1)}, bf16[256,4096]{1,0:T(8,128)(2,1)}, f32[8,4096]{1,0:T(8,128)}) custom-call(bf16[128,4096]{1,0:T(8,128)(2,1)} %query_ref.3, bf16[256,512]{1,0:T(8,128)(2,1)} %collective-permute-done.2.keys2_ref, bf16[256,512]{1,0:T(8,128)(2,1)} %copy-done.9, ...), custom_call_target="tpu_custom_call" | custom-call | flops 10000000000 | bytes 134217728 | tf_op jit(solution)/shard_map/score/pallas_call | solution.py:226
  67.3 5.8 %all-to-all-done.1 = bf16[16,8,4096]{2,1,0:T(8,128)(2,1)S(1)} async-done(((bf16[16,8,4096]{2,1,0:T(8,128)(2,1)}), bf16[16,8,4096]{2,1,0:T(8,128)(2,1)S(1)}, u32[]{:S(2)}, u32[]{:S(2)}) %all-to-all-start.1) | async-done | bytes 1048608 | tf_op jit(solution)/shard_map/all_to_all | solution.py:42
  74.0 9.5 %collective-permute-start.5 = (bf16[64,128]{1,0:T(8,128)(2,1)S(1)}, bf16[64,128]{1,0:T(8,128)(2,1)S(1)}, u32[]{:S(2)}, u32[]{:S(2)}) collective-permute-start(bf16[64,128]{1,0:T(8,128)(2,1)S(1)} %lowrank.1), channel_id=1, source_target_pairs={{0,1},{1,2},{2,3},{3,4},{4,5},{5,6},{6,7},{7,8},{8,9},{9,10},{10,1... | collective-permute-start | bytes 49160 | tf_op jit(solution)/shard_map/ppermute | solution.py:38
  85.6 2.2 %collective-permute-start.6 = (bf16[64,256]{1,0:T(8,128)(2,1)S(1)}, bf16[64,256]{1,0:T(8,128)(2,1)S(1)}, u32[]{:S(2)}, u32[]{:S(2)}) collective-permute-start(bf16[64,256]{1,0:T(8,128)(2,1)S(1)} %pad_maximum_fusion.2), channel_id=1, source_target_pairs={{0,2},{1,3},{2,4},{3,5},{4,6},{5,7},{6,8},{7,9},{8,10},{9,11},{10,... | collective-permute-start | bytes 98312 | tf_op jit(solution)/shard_map/ppermute | solution.py:38
  87.9 2.1 %last_score.1 = (bf16[256,4096]{1,0:T(8,128)(2,1)S(1)}, f32[2,4096]{1,0:T(2,128)S(1)}) custom-call(bf16[128,4096]{1,0:T(8,128)(2,1)S(1)} %copy-done.2, bf16[256,512]{1,0:T(8,128)(2,1)S(1)} %collective-permute-done.4.keys_ref, f32[256,128]{1,0:T(8,128)S(1)} %slice.30.bias_ref), custom_call_target="tpu_custom_call" | custom-call | flops 10000000000 | bytes 134217728 | tf_op jit(solution)/shard_map/last_score/pallas_call | solution.py:214
  90.0 1.3 far.1
  92.7 7.9 %collective-permute-start.10 = (bf16[64,512]{1,0:T(8,128)(2,1)S(1)}, bf16[64,512]{1,0:T(8,128)(2,1)S(1)}, u32[]{:S(2)}, u32[]{:S(2)}) collective-permute-start(bf16[64,512]{1,0:T(8,128)(2,1)S(1)} %pad_maximum_fusion.1), channel_id=1, source_target_pairs={{0,4},{1,5},{2,6},{3,7},{4,8},{5,9},{6,10},{7,11},{8,12},{9,13},{1... | collective-permute-start | bytes 196616 | tf_op jit(solution)/shard_map/ppermute | solution.py:38
  103.3 2.4 %mixed.2.up0_ref = f32[64,256]{1,0:T(8,128)S(1)} custom-call(bf16[256,4096]{1,0:T(8,128)(2,1)S(1)} %get-tuple-element.28.w3_ref, bf16[256,4096]{1,0:T(8,128)(2,1)S(1)} %copy-done.5, bf16[256,4096]{1,0:T(8,128)(2,1)S(1)} %copy-done.6, bf16[256,4096]{1,0:T(8,128)(2,1)S(1)} %copy-done.7, f32[4,4096]{1,0:T(4,128)S(1)} %get-tuple-element.33.scale_ref, ...), custom_call_target="tpu_custom_call" | custom-call | flops 10000000000 | bytes 134217728 | tf_op jit(solution)/shard_map/mixed/pallas_call | solution.py:214
  105.7 2.2 %collective-permute-done.8 = f32[64,256]{1,0:T(8,128)S(1)} collective-permute-done((f32[64,256]{1,0:T(8,128)S(1)}, f32[64,256]{1,0:T(8,128)S(1)}, u32[]{:S(2)}, u32[]{:S(2)}) %collective-permute-start.8) | collective-permute-done | bytes 65568 | tf_op jit(solution)/shard_map/ppermute | solution.py:38
  109.3 2.4 %mixed.3.up1_ref = f32[64,256]{1,0:T(8,128)S(1)} custom-call(bf16[256,4096]{1,0:T(8,128)(2,1)S(1)} %get-tuple-element.28.w3_ref, bf16[256,4096]{1,0:T(8,128)(2,1)S(1)} %copy-done.5, bf16[256,4096]{1,0:T(8,128)(2,1)S(1)} %copy-done.6, bf16[256,4096]{1,0:T(8,128)(2,1)S(1)} %copy-done.7, f32[4,4096]{1,0:T(4,128)S(1)} %get-tuple-element.33.scale_ref, ...), custom_call_target="tpu_custom_call" | custom-call | flops 10000000000 | bytes 134217728 | tf_op jit(solution)/shard_map/mixed/pallas_call | solution.py:214
  113.1 6.5 %collective-permute-start.11 = (f32[64,4352]{1,0:T(8,128)S(1)}, f32[64,4352]{1,0:T(8,128)S(1)}, u32[]{:S(2)}, u32[]{:S(2)}) collective-permute-start(f32[64,4352]{1,0:T(8,128)S(1)} %get-tuple-element.37), channel_id=1, source_target_pairs={{0,32},{32,0},{64,96},{96,64},{128,160},{160,128},{192,224},{224,1... | collective-permute-start | bytes 3342344 | tf_op jit(solution)/shard_map/ppermute | solution.py:373
  119.6 2.4 %collective-permute-done.11.other_ref = f32[64,4352]{1,0:T(8,128)S(1)} collective-permute-done((f32[64,4352]{1,0:T(8,128)S(1)}, f32[64,4352]{1,0:T(8,128)S(1)}, u32[]{:S(2)}, u32[]{:S(2)}) %collective-permute-start.11) | collective-permute-done | bytes 1114144 | tf_op jit(solution)/shard_map/ppermute | solution.py:373
  122.1 15.1 %all_to_all.25.in_ref = bf16[8,8,4352]{2,1,0:T(8,128)(2,1)S(1)} all-to-all(bf16[8,8,4352]{2,1,0:T(8,128)(2,1)S(1)} %add.47), channel_id=1, replica_groups={{0,64,128,192,256,320,384,448},{32,96,160,224,288,352,416,480},{1,65,12..., dimensions={0} | all-to-all | bytes 1114112 | tf_op jit(solution)/shard_map/all_to_all | solution.py:378
  137.2 36.1 %all_to_all.26.in_ref = bf16[32,8,384]{2,1,0:T(8,128)(2,1)S(1)} all-to-all(bf16[32,8,384]{2,1,0:T(8,128)(2,1)S(1)} %fold_dp.1), channel_id=1, replica_groups=mesh['dp'=16,'fsdp'=32] {'fsdp'}, dimensions={0} | all-to-all | bytes 393216 | tf_op jit(solution)/shard_map/all_to_all | solution.py:42
  173.4 13.7 %all_to_all.27.in_ref = f32[16,8,384]{2,1,0:T(8,128)S(1)} all-to-all(f32[16,8,384]{2,1,0:T(8,128)S(1)} %fold_fsdp.1), channel_id=1, replica_groups=mesh['dp'=16,'fsdp'=32] {'dp'}, dimensions={0} | all-to-all | bytes 393216 | tf_op jit(solution)/shard_map/all_to_all | solution.py:42
  (68 shorter events, 14.3 us)
Async XLA Ops:
  2.2 44.5 %all-to-all-start = ((bf16[32,16,128]{2,1,0:T(8,128)(2,1)}), bf16[32,16,128]{2,1,0:T(8,128)(2,1)S(1)}, u32[]{:S(2)}, u32[]{:S(2)}) async-start(bf16[32,16,128]{2,1,0:T(8,128)(2,1)} %broadcast_in_dim.28), calls=%async_computation | async-start | bytes 262144 | tf_op jit(solution)/shard_map/all_to_all | solution.py:42
  20.8 13.3 %collective-permute-start = (bf16[128,512]{1,0:T(8,128)(2,1)}, bf16[128,512]{1,0:T(8,128)(2,1)S(1)}, u32[]{:S(2)}, u32[]{:S(2)}) collective-permute-start(bf16[128,512]{1,0:T(8,128)(2,1)} %param.9), channel_id=1, source_target_pairs={{0,3},{1,4},{2,5},{3,6},{4,7},{5,8},{6,9},{7,10},{8,11},{9,12},{10... | collective-permute-start | bytes 393224 | tf_op jit(solution)/shard_map/ppermute | solution.py:38
  25.8 12.5 %collective-permute-start.1 = (bf16[128,512]{1,0:T(8,128)(2,1)}, bf16[128,512]{1,0:T(8,128)(2,1)S(1)}, u32[]{:S(2)}, u32[]{:S(2)}) collective-permute-start(bf16[128,512]{1,0:T(8,128)(2,1)} %param.9), channel_id=1, source_target_pairs={{0,2},{1,3},{2,4},{3,5},{4,6},{5,7},{6,8},{7,9},{8,10},{9,11},{10,... | collective-permute-start | bytes 393224 | tf_op jit(solution)/shard_map/ppermute | solution.py:38
  31.0 14.0 %collective-permute-start.3 = (bf16[128,512]{1,0:T(8,128)(2,1)}, bf16[128,512]{1,0:T(8,128)(2,1)S(1)}, u32[]{:S(2)}, u32[]{:S(2)}) collective-permute-start(bf16[128,512]{1,0:T(8,128)(2,1)} %param.9), channel_id=1, source_target_pairs={{0,1},{1,2},{2,3},{3,4},{4,5},{5,6},{6,7},{7,8},{8,9},{9,10},{10,1... | collective-permute-start | bytes 393224 | tf_op jit(solution)/shard_map/ppermute | solution.py:38
  34.1 24.4 %copy-start.10 = (s32[1,128]{1,0:T(1,128)S(1)}, s32[1,128]{1,0:T(1,128)}, u32[]{:S(2)}) copy-start(s32[1,128]{1,0:T(1,128)} %param.10) | copy-start | bytes 1540
  38.3 20.2 %copy-start.9 = (bf16[256,512]{1,0:T(8,128)(2,1)}, bf16[256,512]{1,0:T(8,128)(2,1)S(1)}, u32[]{:S(2)}) copy-start(bf16[256,512]{1,0:T(8,128)(2,1)S(1)} %constant_dynamic-update-slice_fusion.keys1_ref) | copy-start | bytes 786436
  38.3 15.8 %collective-permute-start.2 = (bf16[256,512]{1,0:T(8,128)(2,1)S(1)}, bf16[256,512]{1,0:T(8,128)(2,1)}, u32[]{:S(2)}, u32[]{:S(2)}) collective-permute-start(bf16[256,512]{1,0:T(8,128)(2,1)S(1)} %constant_dynamic-update-slice_fusion.keys1_ref), channel_id=1, source_target_pairs={{0,2},{1,3},{2,4},{3,5},{4,6},{5,7},{6,8},{7,9},{8,10},{9,11},{10,... | collective-permute-start | bytes 786440 | tf_op jit(solution)/shard_map/ppermute | solution.py:38
  47.7 25.4 %all-to-all-start.1 = ((bf16[16,8,4096]{2,1,0:T(8,128)(2,1)}), bf16[16,8,4096]{2,1,0:T(8,128)(2,1)S(1)}, u32[]{:S(2)}, u32[]{:S(2)}) async-start(bf16[16,8,4096]{2,1,0:T(8,128)(2,1)} %broadcast_in_dim.30), calls=%async_computation.1 | async-start | bytes 2097152 | tf_op jit(solution)/shard_map/all_to_all | solution.py:42
  54.1 31.5 %collective-permute-start.4 = (bf16[256,512]{1,0:T(8,128)(2,1)}, bf16[256,512]{1,0:T(8,128)(2,1)S(1)}, u32[]{:S(2)}, u32[]{:S(2)}) collective-permute-start(bf16[256,512]{1,0:T(8,128)(2,1)} %collective-permute-done.2.keys2_ref), channel_id=1, source_target_pairs={{0,2},{1,3},{2,4},{3,5},{4,6},{5,7},{6,8},{7,9},{8,10},{9,11},{10,... | collective-permute-start | bytes 786440 | tf_op jit(solution)/shard_map/ppermute | solution.py:38
  59.7 13.5 %copy-start.1 = (bf16[128,8192]{1,0:T(8,128)(2,1)S(1)}, bf16[128,8192]{1,0:T(8,128)(2,1)}, u32[]{:S(2)}) copy-start(bf16[128,8192]{1,0:T(8,128)(2,1)} %hidden_ref.3) | copy-start | bytes 6291460
  73.1 10.4 %copy-start.3 = (bf16[128,4096]{1,0:T(8,128)(2,1)S(1)}, bf16[128,4096]{1,0:T(8,128)(2,1)}, u32[]{:S(2)}) copy-start(bf16[128,4096]{1,0:T(8,128)(2,1)} %gradient_ref.5) | copy-start | bytes 3145732
  73.1 10.4 %copy-start.4 = (bf16[64,512]{1,0:T(8,128)(2,1)S(1)}, bf16[64,512]{1,0:T(8,128)(2,1)}, u32[]{:S(2)}) copy-start(bf16[64,512]{1,0:T(8,128)(2,1)} %up_ref) | copy-start | bytes 196612
  74.0 13.9 %copy-start.2 = (bf16[128,4096]{1,0:T(8,128)(2,1)S(1)}, bf16[128,4096]{1,0:T(8,128)(2,1)}, u32[]{:S(2)}) copy-start(bf16[128,4096]{1,0:T(8,128)(2,1)} %query_ref.3) | copy-start | bytes 3145732
  74.0 11.6 %collective-permute-start.5 = (bf16[64,128]{1,0:T(8,128)(2,1)S(1)}, bf16[64,128]{1,0:T(8,128)(2,1)S(1)}, u32[]{:S(2)}, u32[]{:S(2)}) collective-permute-start(bf16[64,128]{1,0:T(8,128)(2,1)S(1)} %lowrank.1), channel_id=1, source_target_pairs={{0,1},{1,2},{2,3},{3,4},{4,5},{5,6},{6,7},{7,8},{8,9},{9,10},{10,1... | collective-permute-start | bytes 49160 | tf_op jit(solution)/shard_map/ppermute | solution.py:38
  85.6 4.4 %copy-start.5 = (bf16[256,4096]{1,0:T(8,128)(2,1)S(1)}, bf16[256,4096]{1,0:T(8,128)(2,1)}, u32[]{:S(2)}) copy-start(bf16[256,4096]{1,0:T(8,128)(2,1)} %get-tuple-element.29.w2_ref) | copy-start | bytes 6291460
  85.6 4.4 %copy-start.8 = (f32[8,4096]{1,0:T(8,128)S(1)}, f32[8,4096]{1,0:T(8,128)}, u32[]{:S(2)}) copy-start(f32[8,4096]{1,0:T(8,128)} %get-tuple-element.31.stats_ref) | copy-start | bytes 393220
  85.6 4.4 %collective-permute-start.6 = (bf16[64,256]{1,0:T(8,128)(2,1)S(1)}, bf16[64,256]{1,0:T(8,128)(2,1)S(1)}, u32[]{:S(2)}, u32[]{:S(2)}) collective-permute-start(bf16[64,256]{1,0:T(8,128)(2,1)S(1)} %pad_maximum_fusion.2), channel_id=1, source_target_pairs={{0,2},{1,3},{2,4},{3,5},{4,6},{5,7},{6,8},{7,9},{8,10},{9,11},{10,... | collective-permute-start | bytes 98312 | tf_op jit(solution)/shard_map/ppermute | solution.py:38
  90.0 10.6 %copy-start.6 = (bf16[256,4096]{1,0:T(8,128)(2,1)S(1)}, bf16[256,4096]{1,0:T(8,128)(2,1)}, u32[]{:S(2)}) copy-start(bf16[256,4096]{1,0:T(8,128)(2,1)} %get-tuple-element.22.w1_ref) | copy-start | bytes 6291460
  90.0 10.6 %copy-start.7 = (bf16[256,4096]{1,0:T(8,128)(2,1)S(1)}, bf16[256,4096]{1,0:T(8,128)(2,1)}, u32[]{:S(2)}) copy-start(bf16[256,4096]{1,0:T(8,128)(2,1)} %get-tuple-element.23.w0_ref) | copy-start | bytes 6291460
  91.4 10.5 %collective-permute-start.7 = (bf16[64,512]{1,0:T(8,128)(2,1)S(1)}, bf16[64,512]{1,0:T(8,128)(2,1)S(1)}, u32[]{:S(2)}, u32[]{:S(2)}) collective-permute-start(bf16[64,512]{1,0:T(8,128)(2,1)S(1)} %get-tuple-element.34), channel_id=1, source_target_pairs={{4,0},{5,1},{6,2},{7,3},{8,4},{9,5},{10,6},{11,7},{12,8},{13,9},{1... | collective-permute-start | bytes 196616 | tf_op jit(solution)/shard_map/ppermute | solution.py:38
  92.7 10.6 %collective-permute-start.10 = (bf16[64,512]{1,0:T(8,128)(2,1)S(1)}, bf16[64,512]{1,0:T(8,128)(2,1)S(1)}, u32[]{:S(2)}, u32[]{:S(2)}) collective-permute-start(bf16[64,512]{1,0:T(8,128)(2,1)S(1)} %pad_maximum_fusion.1), channel_id=1, source_target_pairs={{0,4},{1,5},{2,6},{3,7},{4,8},{5,9},{6,10},{7,11},{8,12},{9,13},{1... | collective-permute-start | bytes 196616 | tf_op jit(solution)/shard_map/ppermute | solution.py:38
  102.0 6.0 %collective-permute-start.8 = (f32[64,256]{1,0:T(8,128)S(1)}, f32[64,256]{1,0:T(8,128)S(1)}, u32[]{:S(2)}, u32[]{:S(2)}) collective-permute-start(f32[64,256]{1,0:T(8,128)S(1)} %slice.32), channel_id=1, source_target_pairs={{2,0},{3,1},{4,2},{5,3},{6,4},{7,5},{8,6},{9,7},{10,8},{11,9},{12,... | collective-permute-start | bytes 196616 | tf_op jit(solution)/shard_map/ppermute | solution.py:38
  108.0 4.7 %collective-permute-start.9 = (f32[64,128]{1,0:T(8,128)S(1)}, f32[64,128]{1,0:T(8,128)S(1)}, u32[]{:S(2)}, u32[]{:S(2)}) collective-permute-start(f32[64,128]{1,0:T(8,128)S(1)} %slice.34), channel_id=1, source_target_pairs={{1,0},{2,1},{3,2},{4,3},{5,4},{6,5},{7,6},{8,7},{9,8},{10,9},{11,1... | collective-permute-start | bytes 98312 | tf_op jit(solution)/shard_map/ppermute | solution.py:38
  113.1 8.9 %collective-permute-start.11 = (f32[64,4352]{1,0:T(8,128)S(1)}, f32[64,4352]{1,0:T(8,128)S(1)}, u32[]{:S(2)}, u32[]{:S(2)}) collective-permute-start(f32[64,4352]{1,0:T(8,128)S(1)} %get-tuple-element.37), channel_id=1, source_target_pairs={{0,32},{32,0},{64,96},{96,64},{128,160},{160,128},{192,224},{224,1... | collective-permute-start | bytes 3342344 | tf_op jit(solution)/shard_map/ppermute | solution.py:373
  (1 other events, 0.8 us)

commit v6 on v5

--- a/solution.py
+++ b/solution.py
@@ -40,6 +40,10 @@
 
 def exchange(slots, axis):
     return lax.all_to_all(slots, axis, 0, 0, tiled=True)
+
+
+def docs_kernel(in_ref, out_ref):
+    out_ref[...] = in_ref[...]
 
 
 def lowrank_kernel(weight_ref, hidden_ref, out_ref):
@@ -163,31 +167,20 @@
 LANES = DOWN + 256
 
 
-def shares_kernel(core_ref, key_ref, hidden_ref, up0_ref, up1_ref, own_ref, other_ref):
-    for core in range(2):
-
-        @pl.when(core_ref[0] == core)
-        def _(core=core):
-            halves = (own_ref, other_ref) if core == 0 else (other_ref, own_ref)
-            for f in range(N_FSDP):
-                product = jnp.dot(
-                    key_ref[...], hidden_ref[:, f * 256 : f * 256 + 256], preferred_element_type=F32
-                )
-                for half, ref in enumerate(halves):
-                    ref[:, f * 128 : f * 128 + 128] = product[:, half * 128 : half * 128 + 128]
-            halves[0][:, DOWN:] = up0_ref[...]
-            halves[1][:, DOWN:] = up1_ref[...]
-
-
-def add_kernel(own_ref, other_ref, out_ref):
-    for part in range(8):
-        rows = slice(part * 8, part * 8 + 8)
-        out_ref[part] = (own_ref[rows, :] + other_ref[rows, :]).astype(BF16)
+def shares_kernel(key_ref, hidden_ref, up0_ref, up1_ref, out_ref):
+    for f in range(N_FSDP):
+        product = jnp.dot(
+            key_ref[...], hidden_ref[:, f * 256 : f * 256 + 256], preferred_element_type=F32
+        ).astype(BF16)
+        for half in range(2):
+            out_ref[half, :, f * 128 : f * 128 + 128] = product[:, half * 128 : half * 128 + 128]
+    for half, up_ref in enumerate((up0_ref, up1_ref)):
+        out_ref[half, :, DOWN:] = up_ref[...].astype(BF16)
 
 
 def fold_dp_kernel(in_ref, out_ref):
     def total(columns):
-        return sum(in_ref[d, :, columns].astype(F32) for d in range(N_DP // 2))
+        return sum(in_ref[d, :, columns].astype(F32) for d in range(N_DP))
 
     up = total(slice(DOWN, LANES)).astype(BF16)
     for f in range(N_FSDP):
@@ -205,7 +198,7 @@
     for half in range(2):
         for part in range(8):
             rows = slice(part * 8, part * 8 + 8)
-            block = in_ref[part * 2 + half]
+            block = in_ref[half * 8 + part]
             down_ref[rows, half * 128 : half * 128 + 128] = block[:, :128]
             up_ref[rows, half * 256 : half * 256 + 256] = block[:, 128:]
 
@@ -253,8 +246,17 @@
 
     keys1, keys2, keys3 = [from_behind(keys, distance) for distance in (1, 2, 3)]
     weight_slice = lax.dynamic_slice(adapter_down_weight.T, (part * 8, half * 128), (8, 128))
-    docs_row = document_numbers.reshape(1, TOKENS).astype(BF16)
-    slot = jnp.concatenate([weight_slice, docs_row, jnp.zeros((7, 128), BF16)], axis=0)
+    slot = jnp.concatenate(
+        [
+            weight_slice,
+            document_numbers.reshape(1, TOKENS).astype(BF16),
+            jnp.zeros((7, 128), BF16),
+        ],
+        axis=0,
+    )
+    docs_row = plain(
+        docs_kernel, "docs", jax.ShapeDtypeStruct((1, TOKENS), jnp.int32), document_numbers
+    )
     slots = jnp.broadcast_to(slot[None], (N_FSDP, 16, 128))
     row_parts = exchange(slots, "fsdp")
     pair0 = jnp.concatenate([keys1, keys], axis=0)
@@ -269,7 +271,7 @@
 
     padded = jnp.concatenate([jnp.full((SPAN - 1, TOKENS), -1, jnp.int32), docs], axis=0)
     window_docs = lax.dynamic_slice(padded, (position, 0), (SPAN, TOKENS)).reshape(WINDOW)
-    own_docs = document_numbers.reshape(TOKENS)
+    own_docs = docs_row[0]
     key_pos = jnp.arange(WINDOW, dtype=jnp.int32) - (SPAN - 1) * TOKENS
     visible = (window_docs[:, None] == own_docs[None, :]) & (
         key_pos[:, None] <= jnp.arange(TOKENS, dtype=jnp.int32)[None, :]
@@ -312,7 +314,7 @@
         (weights_shape, jax.ShapeDtypeStruct((2, columns_of), F32)),
         queries,
         pair3,
-        bias[:256],
+        bias,
     )
     w3, rank2 = lax.optimization_barrier((w3, rank2))
     far, scale = plain(
@@ -360,22 +362,15 @@
     ]
     key_grad = (near[:, 128:] + came).astype(BF16)
 
-    share = jax.ShapeDtypeStruct((ADAPTER_RANK, LANES), F32)
-    own, other = pl.pallas_call(
+    shares = plain(
         shares_kernel,
-        in_specs=[pl.BlockSpec(memory_space=pltpu.SMEM)] + whole(key_grad, hidden, *ups),
-        out_specs=whole(share, share),
-        out_shape=(share, share),
-        compiler_params=params(20),
-        cost_estimate=COST,
-        name="shares",
-    )((member % 2).astype(jnp.int32).reshape(1), key_grad, hidden, *ups)
-    other = lax.ppermute(other, "dp", [(d, d ^ 1) for d in range(N_DP)])
-    shares = plain(
-        add_kernel, "add", jax.ShapeDtypeStruct((N_DP // 2, 8, LANES), BF16), own, other
-    )
-    groups = [list(range(core, N_DP, 2)) for core in range(2)]
-    shares = lax.all_to_all(shares, "dp", 0, 0, axis_index_groups=groups, tiled=True)
+        "shares",
+        jax.ShapeDtypeStruct((2, ADAPTER_RANK, LANES), BF16),
+        key_grad,
+        hidden,
+        *ups,
+    )
+    shares = exchange(shares.reshape(N_DP, 8, LANES), "dp")
     shares = plain(
         fold_dp_kernel, "fold_dp", jax.ShapeDtypeStruct((N_FSDP, 8, 384), BF16), shares
     )

time: 189 us -> 178 us (0.942)
  starting transfers between devices: 79.3 us -> 60.1 us
  blocking collectives: 65 us -> 70.4 us
  waiting for transfers between devices: 15.5 us -> 19.8 us
    all_to_all x2 -> x3, blocking collectives: 49.9 us -> 70.4 us  [exchange(): return lax.all_to_all(slots, axis, 0, 0, tiled=True)]
    all_to_all x1 -> x0, blocking collectives: 15.1 us -> none  [local(): lax.all_to_all(shares, 'dp', 0, 0, axis_index_groups=groups, tiled=True)]
    all_to_all x2, waiting for transfers between devices: 5.79 us -> 16.4 us  [exchange(): return lax.all_to_all(slots, axis, 0, 0, tiled=True)]
    ppermute x11, starting transfers between devices: 47.8 us -> 39.3 us  [from_behind(): return lax.ppermute(block, 'fsdp', route)]
    ppermute x1 -> x0, starting transfers between devices: 6.55 us -> none  [local(): other = lax.ppermute(other, 'dp', [(d, d ^ 1) for d in range(N_DP)])]
    all_to_all x2, starting transfers between devices: 24.9 us -> 20.8 us  [exchange(): return lax.all_to_all(slots, axis, 0, 0, tiled=True)]
    ppermute x11, waiting for transfers between devices: 7.31 us -> 3.42 us  [from_behind(): return lax.ppermute(block, 'fsdp', route)]
    ppermute x1 -> x0, waiting for transfers between devices: 2.36 us -> none  [local(): other = lax.ppermute(other, 'dp', [(d, d ^ 1) for d in range(N_DP)])]
  transfers between devices with their start and end apart: 14 -> 13, of which waited for: 5 -> 4; matrix products, arithmetic and copies ran while one was open for 3% -> 3% of each run, Pallas kernels for 10% -> 10%
where the time goes in v6:
time: 178 us; the launch traced here: 177 us
  blocking collectives  70.4 us (40%)
  starting transfers between devices  60.1 us (34%)
  Pallas kernels  20.5 us (12%)
  waiting for transfers between devices  19.8 us (11%)
  other arithmetic  2.71 us (2%)
  local copies, waits for them, and re-layouts  2.6 us (1%)
    all_to_all x3, blocking collectives, exchange(): return lax.all_to_all(slots, axis, 0, 0, tiled=True)  70.4 us
    ppermute x11, starting transfers between devices, from_behind(): return lax.ppermute(block, 'fsdp', route)  39.3 us
    all_to_all x2, starting transfers between devices, exchange(): return lax.all_to_all(slots, axis, 0, 0, tiled=True)  20.8 us
    all_to_all x2, waiting for transfers between devices, exchange(): return lax.all_to_all(slots, axis, 0, 0, tiled=True)  16.4 us
    pallas_call x12, Pallas kernels, plain(): pl.pallas_call(kernel, in_specs=whole(*arrays), out_specs=jax.tree.map(la...  12.9 us
    pallas_call x1, Pallas kernels, by_steps(): pl.pallas_call(kernel, grid=(steps,), in_specs=[spec for spec, _ in given...  7.66 us
  transfers between devices with their start and end apart: 13, of which 4 were waited for; matrix products, arithmetic and copies ran while one was open for 3% of the time, Pallas kernels for 10%

profile of v6, /device:TPU:1, one launch (start us, length us, event | category | flops | bytes accessed | tf_op | source)
XLA Modules:
  0.0 177.2 jit_solution(14895746329054635409)
XLA Ops:
  0.6 7.1 %collective-permute-start = (bf16[128,512]{1,0:T(8,128)(2,1)}, bf16[128,512]{1,0:T(8,128)(2,1)S(1)}, u32[]{:S(2)}, u32[]{:S(2)}) collective-permute-start(bf16[128,512]{1,0:T(8,128)(2,1)} %param.9), channel_id=1, source_target_pairs={{0,3},{1,4},{2,5},{3,6},{4,7},{5,8},{6,9},{7,10},{8,11},{9,12},{10... | collective-permute-start | bytes 393224 | tf_op jit(solution)/shard_map/ppermute | solution.py:38
  7.7 6.1 %collective-permute-start.1 = (bf16[128,512]{1,0:T(8,128)(2,1)}, bf16[128,512]{1,0:T(8,128)(2,1)S(1)}, u32[]{:S(2)}, u32[]{:S(2)}) collective-permute-start(bf16[128,512]{1,0:T(8,128)(2,1)} %param.9), channel_id=1, source_target_pairs={{0,2},{1,3},{2,4},{3,5},{4,6},{5,7},{6,8},{7,9},{8,10},{9,11},{10,... | collective-permute-start | bytes 393224 | tf_op jit(solution)/shard_map/ppermute | solution.py:38
  13.9 3.5 %collective-permute-start.3 = (bf16[128,512]{1,0:T(8,128)(2,1)}, bf16[128,512]{1,0:T(8,128)(2,1)S(1)}, u32[]{:S(2)}, u32[]{:S(2)}) collective-permute-start(bf16[128,512]{1,0:T(8,128)(2,1)} %param.9), channel_id=1, source_target_pairs={{0,1},{1,2},{2,3},{3,4},{4,5},{5,6},{6,7},{7,8},{8,9},{9,10},{10,1... | collective-permute-start | bytes 393224 | tf_op jit(solution)/shard_map/ppermute | solution.py:38
  18.9 11.2 %all-to-all-start = ((bf16[32,16,128]{2,1,0:T(8,128)(2,1)}), bf16[32,16,128]{2,1,0:T(8,128)(2,1)S(1)}, u32[]{:S(2)}, u32[]{:S(2)}) async-start(bf16[32,16,128]{2,1,0:T(8,128)(2,1)} %broadcast_in_dim.28), calls=%async_computation | async-start | bytes 262144 | tf_op jit(solution)/shard_map/all_to_all | solution.py:42
  30.9 4.8 %collective-permute-start.2 = (bf16[256,512]{1,0:T(8,128)(2,1)S(1)}, bf16[256,512]{1,0:T(8,128)(2,1)}, u32[]{:S(2)}, u32[]{:S(2)}) collective-permute-start(bf16[256,512]{1,0:T(8,128)(2,1)S(1)} %constant_dynamic-update-slice_fusion.keys1_ref), channel_id=1, source_target_pairs={{0,2},{1,3},{2,4},{3,5},{4,6},{5,7},{6,8},{7,9},{8,10},{9,11},{10,... | collective-permute-start | bytes 786440 | tf_op jit(solution)/shard_map/ppermute | solution.py:38
  36.4 9.5 %all-to-all-done = bf16[32,16,128]{2,1,0:T(8,128)(2,1)S(1)} async-done(((bf16[32,16,128]{2,1,0:T(8,128)(2,1)}), bf16[32,16,128]{2,1,0:T(8,128)(2,1)S(1)}, u32[]{:S(2)}, u32[]{:S(2)}) %all-to-all-start) | async-done | bytes 131104 | tf_op jit(solution)/shard_map/all_to_all | solution.py:42
  47.0 9.5 %all-to-all-start.1 = ((bf16[16,8,4096]{2,1,0:T(8,128)(2,1)}), bf16[16,8,4096]{2,1,0:T(8,128)(2,1)S(1)}, u32[]{:S(2)}, u32[]{:S(2)}) async-start(bf16[16,8,4096]{2,1,0:T(8,128)(2,1)} %broadcast_in_dim.30), calls=%async_computation.1 | async-start | bytes 2097152 | tf_op jit(solution)/shard_map/all_to_all | solution.py:42
  56.6 1.3 collective-permute-start.4
  59.1 7.7 %score.1 = (bf16[256,4096]{1,0:T(8,128)(2,1)}, bf16[256,4096]{1,0:T(8,128)(2,1)}, bf16[256,4096]{1,0:T(8,128)(2,1)}, f32[8,4096]{1,0:T(8,128)}) custom-call(bf16[128,4096]{1,0:T(8,128)(2,1)} %query_ref.3, bf16[256,512]{1,0:T(8,128)(2,1)} %collective-permute-done.2.keys2_ref, bf16[256,512]{1,0:T(8,128)(2,1)} %copy-done.12, ...), custom_call_target="tpu_custom_call" | custom-call | flops 10000000000 | bytes 134217728 | tf_op jit(solution)/shard_map/score/pallas_call | solution.py:219
  66.7 6.8 %all-to-all-done.1 = bf16[16,8,4096]{2,1,0:T(8,128)(2,1)S(1)} async-done(((bf16[16,8,4096]{2,1,0:T(8,128)(2,1)}), bf16[16,8,4096]{2,1,0:T(8,128)(2,1)S(1)}, u32[]{:S(2)}, u32[]{:S(2)}) %all-to-all-start.1) | async-done | bytes 1048608 | tf_op jit(solution)/shard_map/all_to_all | solution.py:42
  74.4 1.6 collective-permute-start.5
  77.3 3.1 %collective-permute-start.6 = (bf16[64,256]{1,0:T(8,128)(2,1)S(1)}, bf16[64,256]{1,0:T(8,128)(2,1)S(1)}, u32[]{:S(2)}, u32[]{:S(2)}) collective-permute-start(bf16[64,256]{1,0:T(8,128)(2,1)S(1)} %pad_maximum_fusion.2), channel_id=1, source_target_pairs={{0,2},{1,3},{2,4},{3,5},{4,6},{5,7},{6,8},{7,9},{8,10},{9,11},{10,... | collective-permute-start | bytes 98312 | tf_op jit(solution)/shard_map/ppermute | solution.py:38
  80.4 2.1 %last_score.1 = (bf16[256,4096]{1,0:T(8,128)(2,1)S(1)}, f32[2,4096]{1,0:T(2,128)S(1)}) custom-call(bf16[128,4096]{1,0:T(8,128)(2,1)S(1)} %copy-done.3, bf16[256,512]{1,0:T(8,128)(2,1)S(1)} %collective-permute-done.4.keys_ref, f32[1024,128]{1,0:T(8,128)S(1)} %copy-done.1), custom_call_target="tpu_custom_call" | custom-call | flops 10000000000 | bytes 134217728 | tf_op jit(solution)/shard_map/last_score/pallas_call | solution.py:207
  82.6 1.3 far.1
  84.0 1.3 collective-permute-start.7
  85.3 7.9 %collective-permute-start.10 = (bf16[64,512]{1,0:T(8,128)(2,1)S(1)}, bf16[64,512]{1,0:T(8,128)(2,1)S(1)}, u32[]{:S(2)}, u32[]{:S(2)}) collective-permute-start(bf16[64,512]{1,0:T(8,128)(2,1)S(1)} %pad_maximum_fusion.1), channel_id=1, source_target_pairs={{0,4},{1,5},{2,6},{3,7},{4,8},{5,9},{6,10},{7,11},{8,12},{9,13},{1... | collective-permute-start | bytes 196616 | tf_op jit(solution)/shard_map/ppermute | solution.py:38
  93.2 1.3 near.1
  94.6 1.3 collective-permute-start.8
  95.9 2.4 %mixed.2.up0_ref = f32[64,256]{1,0:T(8,128)S(1)} custom-call(bf16[256,4096]{1,0:T(8,128)(2,1)S(1)} %get-tuple-element.26.w3_ref, bf16[256,4096]{1,0:T(8,128)(2,1)S(1)} %copy-done.7, bf16[256,4096]{1,0:T(8,128)(2,1)S(1)} %copy-done.8, bf16[256,4096]{1,0:T(8,128)(2,1)S(1)} %copy-done.9, f32[4,4096]{1,0:T(4,128)S(1)} %get-tuple-element.31.scale_ref, ...), custom_call_target="tpu_custom_call" | custom-call | flops 10000000000 | bytes 134217728 | tf_op jit(solution)/shard_map/mixed/pallas_call | solution.py:207
  98.3 2.4 %collective-permute-done.8 = f32[64,256]{1,0:T(8,128)S(1)} collective-permute-done((f32[64,256]{1,0:T(8,128)S(1)}, f32[64,256]{1,0:T(8,128)S(1)}, u32[]{:S(2)}, u32[]{:S(2)}) %collective-permute-start.8) | collective-permute-done | bytes 65568 | tf_op jit(solution)/shard_map/ppermute | solution.py:38
  102.1 2.4 %mixed.3.up1_ref = f32[64,256]{1,0:T(8,128)S(1)} custom-call(bf16[256,4096]{1,0:T(8,128)(2,1)S(1)} %get-tuple-element.26.w3_ref, bf16[256,4096]{1,0:T(8,128)(2,1)S(1)} %copy-done.7, bf16[256,4096]{1,0:T(8,128)(2,1)S(1)} %copy-done.8, bf16[256,4096]{1,0:T(8,128)(2,1)S(1)} %copy-done.9, f32[4,4096]{1,0:T(4,128)S(1)} %get-tuple-element.31.scale_ref, ...), custom_call_target="tpu_custom_call" | custom-call | flops 10000000000 | bytes 134217728 | tf_op jit(solution)/shard_map/mixed/pallas_call | solution.py:207
  105.9 28.1 %all_to_all.25.in_ref = bf16[16,8,4352]{2,1,0:T(8,128)(2,1)S(1)} all-to-all(bf16[16,8,4352]{2,1,0:T(8,128)(2,1)S(1)} %bitcast.15), channel_id=1, replica_groups=mesh['dp'=16,'fsdp'=32] {'dp'}, dimensions={0} | all-to-all | bytes 2228224 | tf_op jit(solution)/shard_map/all_to_all | solution.py:42
  134.1 30.3 %all_to_all.26.in_ref = bf16[32,8,384]{2,1,0:T(8,128)(2,1)S(1)} all-to-all(bf16[32,8,384]{2,1,0:T(8,128)(2,1)S(1)} %fold_dp.1), channel_id=1, replica_groups=mesh['dp'=16,'fsdp'=32] {'fsdp'}, dimensions={0} | all-to-all | bytes 393216 | tf_op jit(solution)/shard_map/all_to_all | solution.py:42
  164.5 12.0 %all_to_all.27.in_ref = f32[16,8,384]{2,1,0:T(8,128)S(1)} all-to-all(f32[16,8,384]{2,1,0:T(8,128)S(1)} %fold_fsdp.1), channel_id=1, replica_groups=mesh['dp'=16,'fsdp'=32] {'dp'}, dimensions={0} | all-to-all | bytes 393216 | tf_op jit(solution)/shard_map/all_to_all | solution.py:42
  (69 shorter events, 10.9 us)
Async XLA Ops:
  0.6 17.6 %copy-start = (bf16[256,64]{0,1:T(8,128)(2,1)S(1)}, bf16[256,64]{0,1:T(8,128)(2,1)}, u32[]{:S(2)}) copy-start(bf16[256,64]{0,1:T(8,128)(2,1)} %param.11) | copy-start | bytes 98308
  0.6 30.2 %collective-permute-start = (bf16[128,512]{1,0:T(8,128)(2,1)}, bf16[128,512]{1,0:T(8,128)(2,1)S(1)}, u32[]{:S(2)}, u32[]{:S(2)}) collective-permute-start(bf16[128,512]{1,0:T(8,128)(2,1)} %param.9), channel_id=1, source_target_pairs={{0,3},{1,4},{2,5},{3,6},{4,7},{5,8},{6,9},{7,10},{8,11},{9,12},{10... | collective-permute-start | bytes 393224 | tf_op jit(solution)/shard_map/ppermute | solution.py:38
  7.7 23.1 %collective-permute-start.1 = (bf16[128,512]{1,0:T(8,128)(2,1)}, bf16[128,512]{1,0:T(8,128)(2,1)S(1)}, u32[]{:S(2)}, u32[]{:S(2)}) collective-permute-start(bf16[128,512]{1,0:T(8,128)(2,1)} %param.9), channel_id=1, source_target_pairs={{0,2},{1,3},{2,4},{3,5},{4,6},{5,7},{6,8},{7,9},{8,10},{9,11},{10,... | collective-permute-start | bytes 393224 | tf_op jit(solution)/shard_map/ppermute | solution.py:38
  13.9 21.8 %collective-permute-start.3 = (bf16[128,512]{1,0:T(8,128)(2,1)}, bf16[128,512]{1,0:T(8,128)(2,1)S(1)}, u32[]{:S(2)}, u32[]{:S(2)}) collective-permute-start(bf16[128,512]{1,0:T(8,128)(2,1)} %param.9), channel_id=1, source_target_pairs={{0,1},{1,2},{2,3},{3,4},{4,5},{5,6},{6,7},{7,8},{8,9},{9,10},{10,1... | collective-permute-start | bytes 393224 | tf_op jit(solution)/shard_map/ppermute | solution.py:38
  18.9 27.0 %all-to-all-start = ((bf16[32,16,128]{2,1,0:T(8,128)(2,1)}), bf16[32,16,128]{2,1,0:T(8,128)(2,1)S(1)}, u32[]{:S(2)}, u32[]{:S(2)}) async-start(bf16[32,16,128]{2,1,0:T(8,128)(2,1)} %broadcast_in_dim.28), calls=%async_computation | async-start | bytes 262144 | tf_op jit(solution)/shard_map/all_to_all | solution.py:42
  30.8 4.8 %copy-start.11 = (bf16[128,512]{1,0:T(8,128)(2,1)S(1)}, bf16[128,512]{1,0:T(8,128)(2,1)}, u32[]{:S(2)}) copy-start(bf16[128,512]{1,0:T(8,128)(2,1)} %param.9) | copy-start | bytes 393220
  30.9 27.0 %copy-start.12 = (bf16[256,512]{1,0:T(8,128)(2,1)}, bf16[256,512]{1,0:T(8,128)(2,1)S(1)}, u32[]{:S(2)}) copy-start(bf16[256,512]{1,0:T(8,128)(2,1)S(1)} %constant_dynamic-update-slice_fusion.keys1_ref) | copy-start | bytes 786436
  30.9 25.6 %collective-permute-start.2 = (bf16[256,512]{1,0:T(8,128)(2,1)S(1)}, bf16[256,512]{1,0:T(8,128)(2,1)}, u32[]{:S(2)}, u32[]{:S(2)}) collective-permute-start(bf16[256,512]{1,0:T(8,128)(2,1)S(1)} %constant_dynamic-update-slice_fusion.keys1_ref), channel_id=1, source_target_pairs={{0,2},{1,3},{2,4},{3,5},{4,6},{5,7},{6,8},{7,9},{8,10},{9,11},{10,... | collective-permute-start | bytes 786440 | tf_op jit(solution)/shard_map/ppermute | solution.py:38
  47.0 26.6 %all-to-all-start.1 = ((bf16[16,8,4096]{2,1,0:T(8,128)(2,1)}), bf16[16,8,4096]{2,1,0:T(8,128)(2,1)S(1)}, u32[]{:S(2)}, u32[]{:S(2)}) async-start(bf16[16,8,4096]{2,1,0:T(8,128)(2,1)} %broadcast_in_dim.30), calls=%async_computation.1 | async-start | bytes 2097152 | tf_op jit(solution)/shard_map/all_to_all | solution.py:42
  56.6 20.7 %collective-permute-start.4 = (bf16[256,512]{1,0:T(8,128)(2,1)}, bf16[256,512]{1,0:T(8,128)(2,1)S(1)}, u32[]{:S(2)}, u32[]{:S(2)}) collective-permute-start(bf16[256,512]{1,0:T(8,128)(2,1)} %collective-permute-done.2.keys2_ref), channel_id=1, source_target_pairs={{0,2},{1,3},{2,4},{3,5},{4,6},{5,7},{6,8},{7,9},{8,10},{9,11},{10,... | collective-permute-start | bytes 786440 | tf_op jit(solution)/shard_map/ppermute | solution.py:38
  59.1 14.5 %copy-start.2 = (bf16[128,8192]{1,0:T(8,128)(2,1)S(1)}, bf16[128,8192]{1,0:T(8,128)(2,1)}, u32[]{:S(2)}) copy-start(bf16[128,8192]{1,0:T(8,128)(2,1)} %hidden_ref.3) | copy-start | bytes 6291460
  73.6 2.5 %copy-start.5 = (bf16[64,512]{1,0:T(8,128)(2,1)S(1)}, bf16[64,512]{1,0:T(8,128)(2,1)}, u32[]{:S(2)}) copy-start(bf16[64,512]{1,0:T(8,128)(2,1)} %up_ref) | copy-start | bytes 196612
  74.4 6.0 %copy-start.1 = (f32[1024,128]{1,0:T(8,128)S(1)}, f32[1024,128]{1,0:T(8,128)}, u32[]{:S(2)}) copy-start(f32[1024,128]{1,0:T(8,128)} %fusion.1.bias_ref) | copy-start | bytes 1572868
  74.4 6.0 %copy-start.3 = (bf16[128,4096]{1,0:T(8,128)(2,1)S(1)}, bf16[128,4096]{1,0:T(8,128)(2,1)}, u32[]{:S(2)}) copy-start(bf16[128,4096]{1,0:T(8,128)(2,1)} %query_ref.3) | copy-start | bytes 3145732
  74.4 2.8 %collective-permute-start.5 = (bf16[64,128]{1,0:T(8,128)(2,1)S(1)}, bf16[64,128]{1,0:T(8,128)(2,1)S(1)}, u32[]{:S(2)}, u32[]{:S(2)}) collective-permute-start(bf16[64,128]{1,0:T(8,128)(2,1)S(1)} %lowrank.1), channel_id=1, source_target_pairs={{0,1},{1,2},{2,3},{3,4},{4,5},{5,6},{6,7},{7,8},{8,9},{9,10},{10,1... | collective-permute-start | bytes 49160 | tf_op jit(solution)/shard_map/ppermute | solution.py:38
  77.2 5.4 %copy-start.7 = (bf16[256,4096]{1,0:T(8,128)(2,1)S(1)}, bf16[256,4096]{1,0:T(8,128)(2,1)}, u32[]{:S(2)}) copy-start(bf16[256,4096]{1,0:T(8,128)(2,1)} %get-tuple-element.27.w2_ref) | copy-start | bytes 6291460
  77.3 5.4 %copy-start.10 = (f32[8,4096]{1,0:T(8,128)S(1)}, f32[8,4096]{1,0:T(8,128)}, u32[]{:S(2)}) copy-start(f32[8,4096]{1,0:T(8,128)} %get-tuple-element.29.stats_ref) | copy-start | bytes 393220
  77.3 5.3 %collective-permute-start.6 = (bf16[64,256]{1,0:T(8,128)(2,1)S(1)}, bf16[64,256]{1,0:T(8,128)(2,1)S(1)}, u32[]{:S(2)}, u32[]{:S(2)}) collective-permute-start(bf16[64,256]{1,0:T(8,128)(2,1)S(1)} %pad_maximum_fusion.2), channel_id=1, source_target_pairs={{0,2},{1,3},{2,4},{3,5},{4,6},{5,7},{6,8},{7,9},{8,10},{9,11},{10,... | collective-permute-start | bytes 98312 | tf_op jit(solution)/shard_map/ppermute | solution.py:38
  82.6 10.6 %copy-start.8 = (bf16[256,4096]{1,0:T(8,128)(2,1)S(1)}, bf16[256,4096]{1,0:T(8,128)(2,1)}, u32[]{:S(2)}) copy-start(bf16[256,4096]{1,0:T(8,128)(2,1)} %get-tuple-element.20.w1_ref) | copy-start | bytes 6291460
  82.6 10.6 %copy-start.9 = (bf16[256,4096]{1,0:T(8,128)(2,1)S(1)}, bf16[256,4096]{1,0:T(8,128)(2,1)}, u32[]{:S(2)}) copy-start(bf16[256,4096]{1,0:T(8,128)(2,1)} %get-tuple-element.21.w0_ref) | copy-start | bytes 6291460
  84.0 10.5 %collective-permute-start.7 = (bf16[64,512]{1,0:T(8,128)(2,1)S(1)}, bf16[64,512]{1,0:T(8,128)(2,1)S(1)}, u32[]{:S(2)}, u32[]{:S(2)}) collective-permute-start(bf16[64,512]{1,0:T(8,128)(2,1)S(1)} %get-tuple-element.32), channel_id=1, source_target_pairs={{4,0},{5,1},{6,2},{7,3},{8,4},{9,5},{10,6},{11,7},{12,8},{13,9},{1... | collective-permute-start | bytes 196616 | tf_op jit(solution)/shard_map/ppermute | solution.py:38
  85.3 10.6 %collective-permute-start.10 = (bf16[64,512]{1,0:T(8,128)(2,1)S(1)}, bf16[64,512]{1,0:T(8,128)(2,1)S(1)}, u32[]{:S(2)}, u32[]{:S(2)}) collective-permute-start(bf16[64,512]{1,0:T(8,128)(2,1)S(1)} %pad_maximum_fusion.1), channel_id=1, source_target_pairs={{0,4},{1,5},{2,6},{3,7},{4,8},{5,9},{6,10},{7,11},{8,12},{9,13},{1... | collective-permute-start | bytes 196616 | tf_op jit(solution)/shard_map/ppermute | solution.py:38
  94.6 6.2 %collective-permute-start.8 = (f32[64,256]{1,0:T(8,128)S(1)}, f32[64,256]{1,0:T(8,128)S(1)}, u32[]{:S(2)}, u32[]{:S(2)}) collective-permute-start(f32[64,256]{1,0:T(8,128)S(1)} %slice.27), channel_id=1, source_target_pairs={{2,0},{3,1},{4,2},{5,3},{6,4},{7,5},{8,6},{9,7},{10,8},{11,9},{12,... | collective-permute-start | bytes 196616 | tf_op jit(solution)/shard_map/ppermute | solution.py:38
  100.8 4.7 %collective-permute-start.9 = (f32[64,128]{1,0:T(8,128)S(1)}, f32[64,128]{1,0:T(8,128)S(1)}, u32[]{:S(2)}, u32[]{:S(2)}) collective-permute-start(f32[64,128]{1,0:T(8,128)S(1)} %slice.29), channel_id=1, source_target_pairs={{1,0},{2,1},{3,2},{4,3},{5,4},{6,5},{7,6},{8,7},{9,8},{10,9},{11,1... | collective-permute-start | bytes 98312 | tf_op jit(solution)/shard_map/ppermute | solution.py:38
  (2 other events, 3.1 us)

commit v7 on v6

--- a/solution.py
+++ b/solution.py
@@ -19,6 +19,7 @@
 N_FSDP = 32
 MODEL_WIDTH = 8192
 GROUP = QUERY_HEADS // KEY_HEADS
+ORDER = (7, 3, 5, 1, 6, 2, 4, 0)
 COST = pl.CostEstimate(flops=10**10, bytes_accessed=2**27, transcendentals=0)
 BF16 = jnp.bfloat16
 F32 = jnp.float32
@@ -72,36 +73,29 @@
 
 
 def score_kernel(
-    query_ref,
-    keys2_ref,
-    keys1_ref,
-    keys0_ref,
-    bias_ref,
-    w2_ref,
-    w1_ref,
-    w0_ref,
-    stats_ref,
+    query_ref, keys1_ref, keys0_ref, bias_ref, w1_ref, w0_ref, stats_ref
 ):
-    refs = ((keys2_ref, w2_ref), (keys1_ref, w1_ref), (keys0_ref, w0_ref))
-    for i, (keys_ref, w_ref) in enumerate(refs):
-        rows = slice(256 + i * 256, 512 + i * 256)
+    for i, (keys_ref, w_ref) in enumerate(((keys1_ref, w1_ref), (keys0_ref, w0_ref))):
+        rows = slice(512 + i * 256, 768 + i * 256)
         score_pair(query_ref, keys_ref[...], bias_ref, rows, w_ref, stats_ref, 2 * i)
-    stats_ref[6:8, :] = jnp.zeros((2, GROUP * TOKENS), F32)
-
-
-def last_score_kernel(query_ref, keys_ref, bias_ref, weights_ref, stats_ref):
+    stats_ref[4:8, :] = jnp.zeros((4, GROUP * TOKENS), F32)
+
+
+def last_score_kernel(query_ref, keys_ref, bias_ref, w3_ref, w2_ref, stats_ref):
     def key_head(g, carry):
         keys = keys_ref[:, pl.ds(pl.multiple_of(g * HEAD_SIZE, HEAD_SIZE), HEAD_SIZE)]
         lanes = pl.ds(pl.multiple_of(g * GROUP * 128, 128), GROUP * 128)
-        score_pair(
-            query_ref.at[:, lanes],
-            keys,
-            bias_ref,
-            slice(0, 256),
-            weights_ref.at[:, lanes],
-            stats_ref.at[:, lanes],
-            0,
-        )
+        for i, w_ref in enumerate((w3_ref, w2_ref)):
+            rows = slice(i * 256, i * 256 + 256)
+            score_pair(
+                query_ref.at[:, lanes],
+                keys[rows],
+                bias_ref,
+                rows,
+                w_ref.at[:, lanes],
+                stats_ref.at[:, lanes],
+                2 * i,
+            )
         return carry
 
     lax.fori_loop(0, KEY_HEADS, key_head, 0)
@@ -126,7 +120,7 @@
 
 
 def far_kernel(w3_ref, w2_ref, last_ref, stats_ref, reached_ref, far_ref, scale_ref):
-    stats = [last_ref[...]] + [stats_ref[2 * i : 2 * i + 2, :] for i in range(3)]
+    stats = [ref[2 * i : 2 * i + 2, :] for ref in (last_ref, stats_ref) for i in range(2)]
     top = stats[0][0:1]
     for s in stats[1:]:
         top = jnp.maximum(top, s[0:1])
@@ -244,7 +238,8 @@
     member = lax.axis_index("dp")
     half, part = member // 8, member % 8
 
-    keys1, keys2, keys3 = [from_behind(keys, distance) for distance in (1, 2, 3)]
+    pair0 = jnp.concatenate([from_behind(keys, 4), keys], axis=0)
+    pair1 = from_behind(pair0, 2)
     weight_slice = lax.dynamic_slice(adapter_down_weight.T, (part * 8, half * 128), (8, 128))
     slot = jnp.concatenate(
         [
@@ -259,20 +254,18 @@
     )
     slots = jnp.broadcast_to(slot[None], (N_FSDP, 16, 128))
     row_parts = exchange(slots, "fsdp")
-    pair0 = jnp.concatenate([keys1, keys], axis=0)
-    pair1 = jnp.concatenate([keys3, keys2], axis=0)
-    pair2 = from_behind(pair1, 2)
     weight_part = row_parts[:, :8].transpose(1, 0, 2).reshape(1, 8, DOWN)
     docs = row_parts[:, 8].astype(jnp.int32)
     weight_slots = jnp.broadcast_to(weight_part, (N_DP, 8, DOWN))
     weight = exchange(weight_slots, "dp").reshape(2, ADAPTER_RANK, DOWN)
-    pair2 = lax.optimization_barrier((pair2, weight_slots))[0]
-    pair3 = from_behind(pair2, 2)
+    pair1 = lax.optimization_barrier((pair1, weight_slots))[0]
+    quad = from_behind(jnp.concatenate([pair1, pair0], axis=0), 1)
 
     padded = jnp.concatenate([jnp.full((SPAN - 1, TOKENS), -1, jnp.int32), docs], axis=0)
-    window_docs = lax.dynamic_slice(padded, (position, 0), (SPAN, TOKENS)).reshape(WINDOW)
+    window_docs = lax.dynamic_slice(padded, (position, 0), (SPAN, TOKENS))
+    window_docs = jnp.concatenate([window_docs[7 - d : 8 - d] for d in ORDER]).reshape(WINDOW)
     own_docs = docs_row[0]
-    key_pos = jnp.arange(WINDOW, dtype=jnp.int32) - (SPAN - 1) * TOKENS
+    key_pos = jnp.concatenate([jnp.arange(TOKENS, dtype=jnp.int32) - d * TOKENS for d in ORDER])
     visible = (window_docs[:, None] == own_docs[None, :]) & (
         key_pos[:, None] <= jnp.arange(TOKENS, dtype=jnp.int32)[None, :]
     )
@@ -281,15 +274,14 @@
     columns_of = QUERY_HEADS * TOKENS
     queries_by, keys_by, weights_by = columns(TOKENS, lanes), columns(256, 128), columns(256, lanes)
     weights_shape = jax.ShapeDtypeStruct((2 * TOKENS, columns_of), BF16)
-    w2, w1, w0, stats = by_steps(
+    w1, w0, stats = by_steps(
         score_kernel,
         "score",
         KEY_HEADS,
-        [weights_by] * 3 + [columns(8, lanes)],
-        [weights_shape] * 3 + [jax.ShapeDtypeStruct((8, columns_of), F32)],
+        [weights_by] * 2 + [columns(8, lanes)],
+        [weights_shape] * 2 + [jax.ShapeDtypeStruct((8, columns_of), F32)],
         [
             (queries_by, queries),
-            (keys_by, pair2),
             (keys_by, pair1),
             (keys_by, pair0),
             (fixed(WINDOW, TOKENS), bias),
@@ -305,18 +297,17 @@
     rank = plain(
         lowrank_kernel, "lowrank", jax.ShapeDtypeStruct((ADAPTER_RANK, TOKENS), BF16), weight, hidden
     )
-    rank1 = jnp.concatenate([from_behind(rank, 1), rank], axis=1)
-    pair3, rank1, stats = lax.optimization_barrier((pair3, rank1, stats))
+    rank1 = jnp.concatenate([from_behind(rank, 4), rank], axis=1)
+    quad, rank, stats = lax.optimization_barrier((quad, rank, stats))
     rank2 = jnp.concatenate([from_behind(rank1, 2), rank1], axis=1)
-    w3, last = plain(
+    w3, w2, last = plain(
         last_score_kernel,
         "last_score",
-        (weights_shape, jax.ShapeDtypeStruct((2, columns_of), F32)),
+        (weights_shape, weights_shape, jax.ShapeDtypeStruct((4, columns_of), F32)),
         queries,
-        pair3,
+        quad,
         bias,
     )
-    w3, rank2 = lax.optimization_barrier((w3, rank2))
     far, scale = plain(
         far_kernel,
         "far",
@@ -339,12 +330,12 @@
         scale,
         reached,
     )
-    came = from_behind(far, -4)
+    came = from_behind(far, -1)
     near = near + came.astype(F32)
-    rank3 = jnp.concatenate([from_behind(rank2, 4), rank2], axis=1)
+    rank3 = jnp.concatenate([from_behind(rank2, 1), rank2], axis=1)
     came = from_behind(near[:, :256], -2)
     near = near[:, 256:] + came
-    came = from_behind(near[:, :128], -1)
+    came = from_behind(near[:, :128], -4)
     ups = [
         plain(
             functools.partial(mixed_kernel, first),

time: 178 us -> 182 us (1.022)
  starting transfers between devices: 60.1 us -> 48.4 us
  blocking collectives: 70.4 us -> 78.4 us
  waiting for transfers between devices: 19.8 us -> 23.8 us
  local copies, waits for them, and re-layouts: 2.6 us -> 5.46 us
    ppermute x11 -> x9, starting transfers between devices: 39.3 us -> 26.4 us  [from_behind(): return lax.ppermute(block, 'fsdp', route)]
    all_to_all x3, blocking collectives: 70.4 us -> 78.4 us  [exchange(): return lax.all_to_all(slots, axis, 0, 0, tiled=True)]
    ppermute x11 -> x9, waiting for transfers between devices: 3.42 us -> 7.75 us  [from_behind(): return lax.ppermute(block, 'fsdp', route)]
    unnamed x29 -> x34, local copies, waits for them, and re-layouts: 0.73 us -> 3.49 us
    pallas_call x12, Pallas kernels: 12.9 us -> 15.4 us  [plain(): pl.pallas_call(kernel, in_specs=whole(*arrays), out_specs=jax.tree.map(la...]
  transfers between devices with their start and end apart: 13 -> 11, of which waited for: 4 -> 4; matrix products, arithmetic and copies ran while one was open for 3% -> 3% of each run, Pallas kernels for 10% -> 11%
where the time goes in v7:
time: 182 us
  blocking collectives  78.4 us (43%)
  starting transfers between devices  48.4 us (27%)
  waiting for transfers between devices  23.8 us (13%)
  Pallas kernels  21.5 us (12%)
  local copies, waits for them, and re-layouts  5.46 us (3%)
  other arithmetic  2.86 us (2%)
    all_to_all x3, blocking collectives, exchange(): return lax.all_to_all(slots, axis, 0, 0, tiled=True)  78.4 us
    ppermute x9, starting transfers between devices, from_behind(): return lax.ppermute(block, 'fsdp', route)  26.4 us
    all_to_all x2, starting transfers between devices, exchange(): return lax.all_to_all(slots, axis, 0, 0, tiled=True)  22.1 us
    all_to_all x2, waiting for transfers between devices, exchange(): return lax.all_to_all(slots, axis, 0, 0, tiled=True)  16.1 us
    pallas_call x12, Pallas kernels, plain(): pl.pallas_call(kernel, in_specs=whole(*arrays), out_specs=jax.tree.map(la...  15.4 us
    ppermute x9, waiting for transfers between devices, from_behind(): return lax.ppermute(block, 'fsdp', route)  7.75 us
    pallas_call x1, Pallas kernels, by_steps(): pl.pallas_call(kernel, grid=(steps,), in_specs=[spec for spec, _ in given...  6.09 us
  transfers between devices with their start and end apart: 11, of which 4 were waited for; matrix products, arithmetic and copies ran while one was open for 3% of the time, Pallas kernels for 11%

profile of v7, /device:TPU:1, one launch (start us, length us, event | category | flops | bytes accessed | tf_op | source)
XLA Modules:
  0.0 181.6 jit_solution(3091206667742230185)
XLA Ops:
  0.6 9.7 %collective-permute-start = (bf16[128,512]{1,0:T(8,128)(2,1)}, bf16[128,512]{1,0:T(8,128)(2,1)S(1)}, u32[]{:S(2)}, u32[]{:S(2)}) collective-permute-start(bf16[128,512]{1,0:T(8,128)(2,1)} %param.9), channel_id=1, source_target_pairs={{0,4},{1,5},{2,6},{3,7},{4,8},{5,9},{6,10},{7,11},{8,12},{9,13},{1... | collective-permute-start | bytes 393224 | tf_op jit(solution)/shard_map/ppermute | solution.py:39
  11.8 13.0 %all-to-all-start = ((bf16[32,16,128]{2,1,0:T(8,128)(2,1)}), bf16[32,16,128]{2,1,0:T(8,128)(2,1)S(1)}, u32[]{:S(2)}, u32[]{:S(2)}) async-start(bf16[32,16,128]{2,1,0:T(8,128)(2,1)} %broadcast_in_dim.28), calls=%async_computation | async-start | bytes 262144 | tf_op jit(solution)/shard_map/all_to_all | solution.py:43
  26.4 4.0 %collective-permute-start.1 = (bf16[256,512]{1,0:T(8,128)(2,1)S(1)}, bf16[256,512]{1,0:T(8,128)(2,1)S(1)}, u32[]{:S(2)}, u32[]{:S(2)}) collective-permute-start(bf16[256,512]{1,0:T(8,128)(2,1)S(1)} %constant_dynamic-update-slice_fusion.keys0_ref), channel_id=1, source_target_pairs={{0,2},{1,3},{2,4},{3,5},{4,6},{5,7},{6,8},{7,9},{8,10},{9,11},{10,... | collective-permute-start | bytes 786440 | tf_op jit(solution)/shard_map/ppermute | solution.py:39
  30.5 10.8 %all-to-all-done = bf16[32,16,128]{2,1,0:T(8,128)(2,1)S(1)} async-done(((bf16[32,16,128]{2,1,0:T(8,128)(2,1)}), bf16[32,16,128]{2,1,0:T(8,128)(2,1)S(1)}, u32[]{:S(2)}, u32[]{:S(2)}) %all-to-all-start) | async-done | bytes 131104 | tf_op jit(solution)/shard_map/all_to_all | solution.py:43
  42.4 9.0 %all-to-all-start.1 = ((bf16[16,8,4096]{2,1,0:T(8,128)(2,1)}), bf16[16,8,4096]{2,1,0:T(8,128)(2,1)S(1)}, u32[]{:S(2)}, u32[]{:S(2)}) async-start(bf16[16,8,4096]{2,1,0:T(8,128)(2,1)} %broadcast_in_dim.30), calls=%async_computation.1 | async-start | bytes 2097152 | tf_op jit(solution)/shard_map/all_to_all | solution.py:43
  52.4 2.1 %collective-permute-start.2 = (bf16[512,512]{1,0:T(8,128)(2,1)}, bf16[512,512]{1,0:T(8,128)(2,1)}, u32[]{:S(2)}, u32[]{:S(2)}) collective-permute-start(bf16[512,512]{1,0:T(8,128)(2,1)} %pad_maximum_fusion), channel_id=1, source_target_pairs={{0,1},{1,2},{2,3},{3,4},{4,5},{5,6},{6,7},{7,8},{8,9},{9,10},{10,1... | collective-permute-start | bytes 1572872 | tf_op jit(solution)/shard_map/ppermute | solution.py:39
  55.7 6.1 %score.1 = (bf16[256,4096]{1,0:T(8,128)(2,1)}, bf16[256,4096]{1,0:T(8,128)(2,1)}, f32[8,4096]{1,0:T(8,128)}) custom-call(bf16[128,4096]{1,0:T(8,128)(2,1)} %query_ref.3, bf16[256,512]{1,0:T(8,128)(2,1)} %copy-done.14, bf16[256,512]{1,0:T(8,128)(2,1)} %copy-done.15, f32[1024,128]{1,0:T(8,128)} %fusion.1.bias_ref), custom_call_target="tpu_custom_call" | custom-call | flops 10000000000 | bytes 134217728 | tf_op jit(solution)/shard_map/score/pallas_call | solution.py:213
  64.9 5.3 %all-to-all-done.1 = bf16[16,8,4096]{2,1,0:T(8,128)(2,1)S(1)} async-done(((bf16[16,8,4096]{2,1,0:T(8,128)(2,1)}), bf16[16,8,4096]{2,1,0:T(8,128)(2,1)S(1)}, u32[]{:S(2)}, u32[]{:S(2)}) %all-to-all-start.1) | async-done | bytes 1048608 | tf_op jit(solution)/shard_map/all_to_all | solution.py:43
  71.1 1.4 collective-permute-start.6
  72.6 4.7 %last_score.1 = (bf16[256,4096]{1,0:T(8,128)(2,1)S(1)}, bf16[256,4096]{1,0:T(8,128)(2,1)S(1)}, f32[4,4096]{1,0:T(4,128)S(1)}) custom-call(bf16[128,4096]{1,0:T(8,128)(2,1)S(1)} %copy-done.3, bf16[512,512]{1,0:T(8,128)(2,1)} %collective-permute-done.2.keys_ref, f32[1024,128]{1,0:T(8,128)S(1)} %copy-done.1), custom_call_target="tpu_custom_call" | custom-call | flops 10000000000 | bytes 134217728 | tf_op jit(solution)/shard_map/last_score/pallas_call | solution.py:201
  77.3 1.3 far.1
  78.6 1.3 collective-permute-start.3
  79.9 1.3 collective-permute-start.7
  81.3 1.3 near.1
  82.6 4.0 %collective-permute-start.8 = (bf16[64,512]{1,0:T(8,128)(2,1)S(1)}, bf16[64,512]{1,0:T(8,128)(2,1)S(1)}, u32[]{:S(2)}, u32[]{:S(2)}) collective-permute-start(bf16[64,512]{1,0:T(8,128)(2,1)S(1)} %pad_maximum_fusion.2), channel_id=1, source_target_pairs={{0,1},{1,2},{2,3},{3,4},{4,5},{5,6},{6,7},{7,8},{8,9},{9,10},{10,1... | collective-permute-start | bytes 196616 | tf_op jit(solution)/shard_map/ppermute | solution.py:39
  86.6 1.3 collective-permute-start.4
  88.0 2.4 %mixed.2.up0_ref = f32[64,256]{1,0:T(8,128)S(1)} custom-call(bf16[256,4096]{1,0:T(8,128)(2,1)S(1)} %get-tuple-element.21.w3_ref, bf16[256,4096]{1,0:T(8,128)(2,1)S(1)} %get-tuple-element.22.w2_ref, bf16[256,4096]{1,0:T(8,128)(2,1)S(1)} %copy-done.8, bf16[256,4096]{1,0:T(8,128)(2,1)S(1)} %copy-done.9, f32[4,4096]{1,0:T(4,128)S(1)} %get-tuple-element.26.scale_ref, ...), custom_call_target="tpu_custom_call" | custom-call | flops 10000000000 | bytes 134217728 | tf_op jit(solution)/shard_map/mixed/pallas_call | solution.py:201
  90.4 2.9 %collective-permute-done.4 = f32[64,256]{1,0:T(8,128)S(1)} collective-permute-done((f32[64,256]{1,0:T(8,128)S(1)}, f32[64,256]{1,0:T(8,128)S(1)}, u32[]{:S(2)}, u32[]{:S(2)}) %collective-permute-start.4) | collective-permute-done | bytes 65568 | tf_op jit(solution)/shard_map/ppermute | solution.py:39
  93.3 1.3 collective-permute-start.5
  94.6 2.4 %mixed.3.up1_ref = f32[64,256]{1,0:T(8,128)S(1)} custom-call(bf16[256,4096]{1,0:T(8,128)(2,1)S(1)} %get-tuple-element.21.w3_ref, bf16[256,4096]{1,0:T(8,128)(2,1)S(1)} %get-tuple-element.22.w2_ref, bf16[256,4096]{1,0:T(8,128)(2,1)S(1)} %copy-done.8, bf16[256,4096]{1,0:T(8,128)(2,1)S(1)} %copy-done.9, f32[4,4096]{1,0:T(4,128)S(1)} %get-tuple-element.26.scale_ref, ...), custom_call_target="tpu_custom_call" | custom-call | flops 10000000000 | bytes 134217728 | tf_op jit(solution)/shard_map/mixed/pallas_call | solution.py:201
  97.0 4.9 %collective-permute-done.5 = f32[64,128]{1,0:T(8,128)S(1)} collective-permute-done((f32[64,128]{1,0:T(8,128)S(1)}, f32[64,128]{1,0:T(8,128)S(1)}, u32[]{:S(2)}, u32[]{:S(2)}) %collective-permute-start.5) | collective-permute-done | bytes 32800 | tf_op jit(solution)/shard_map/ppermute | solution.py:39
  102.3 31.4 %all_to_all.25.in_ref = bf16[16,8,4352]{2,1,0:T(8,128)(2,1)S(1)} all-to-all(bf16[16,8,4352]{2,1,0:T(8,128)(2,1)S(1)} %bitcast.14), channel_id=1, replica_groups=mesh['dp'=16,'fsdp'=32] {'dp'}, dimensions={0} | all-to-all | bytes 2228224 | tf_op jit(solution)/shard_map/all_to_all | solution.py:43
  133.8 35.0 %all_to_all.26.in_ref = bf16[32,8,384]{2,1,0:T(8,128)(2,1)S(1)} all-to-all(bf16[32,8,384]{2,1,0:T(8,128)(2,1)S(1)} %fold_dp.1), channel_id=1, replica_groups=mesh['dp'=16,'fsdp'=32] {'fsdp'}, dimensions={0} | all-to-all | bytes 393216 | tf_op jit(solution)/shard_map/all_to_all | solution.py:43
  168.8 12.0 %all_to_all.27.in_ref = f32[16,8,384]{2,1,0:T(8,128)S(1)} all-to-all(f32[16,8,384]{2,1,0:T(8,128)S(1)} %fold_fsdp.1), channel_id=1, replica_groups=mesh['dp'=16,'fsdp'=32] {'dp'}, dimensions={0} | all-to-all | bytes 393216 | tf_op jit(solution)/shard_map/all_to_all | solution.py:43
  (80 shorter events, 11.6 us)
Async XLA Ops:
  0.6 10.4 %copy-start = (bf16[256,64]{0,1:T(8,128)(2,1)S(1)}, bf16[256,64]{0,1:T(8,128)(2,1)}, u32[]{:S(2)}) copy-start(bf16[256,64]{0,1:T(8,128)(2,1)} %param.11) | copy-start | bytes 98308
  0.6 25.0 %collective-permute-start = (bf16[128,512]{1,0:T(8,128)(2,1)}, bf16[128,512]{1,0:T(8,128)(2,1)S(1)}, u32[]{:S(2)}, u32[]{:S(2)}) collective-permute-start(bf16[128,512]{1,0:T(8,128)(2,1)} %param.9), channel_id=1, source_target_pairs={{0,4},{1,5},{2,6},{3,7},{4,8},{5,9},{6,10},{7,11},{8,12},{9,13},{1... | collective-permute-start | bytes 393224 | tf_op jit(solution)/shard_map/ppermute | solution.py:39
  11.8 29.4 %all-to-all-start = ((bf16[32,16,128]{2,1,0:T(8,128)(2,1)}), bf16[32,16,128]{2,1,0:T(8,128)(2,1)S(1)}, u32[]{:S(2)}, u32[]{:S(2)}) async-start(bf16[32,16,128]{2,1,0:T(8,128)(2,1)} %broadcast_in_dim.28), calls=%async_computation | async-start | bytes 262144 | tf_op jit(solution)/shard_map/all_to_all | solution.py:43
  26.4 26.0 %copy-start.15 = (bf16[256,512]{1,0:T(8,128)(2,1)}, bf16[256,512]{1,0:T(8,128)(2,1)S(1)}, u32[]{:S(2)}) copy-start(bf16[256,512]{1,0:T(8,128)(2,1)S(1)} %constant_dynamic-update-slice_fusion.keys0_ref) | copy-start | bytes 786436
  26.4 25.0 %collective-permute-start.1 = (bf16[256,512]{1,0:T(8,128)(2,1)S(1)}, bf16[256,512]{1,0:T(8,128)(2,1)S(1)}, u32[]{:S(2)}, u32[]{:S(2)}) collective-permute-start(bf16[256,512]{1,0:T(8,128)(2,1)S(1)} %constant_dynamic-update-slice_fusion.keys0_ref), channel_id=1, source_target_pairs={{0,2},{1,3},{2,4},{3,5},{4,6},{5,7},{6,8},{7,9},{8,10},{9,11},{10,... | collective-permute-start | bytes 786440 | tf_op jit(solution)/shard_map/ppermute | solution.py:39
  42.4 27.8 %all-to-all-start.1 = ((bf16[16,8,4096]{2,1,0:T(8,128)(2,1)}), bf16[16,8,4096]{2,1,0:T(8,128)(2,1)S(1)}, u32[]{:S(2)}, u32[]{:S(2)}) async-start(bf16[16,8,4096]{2,1,0:T(8,128)(2,1)} %broadcast_in_dim.30), calls=%async_computation.1 | async-start | bytes 2097152 | tf_op jit(solution)/shard_map/all_to_all | solution.py:43
  51.5 4.2 %copy-start.14 = (bf16[256,512]{1,0:T(8,128)(2,1)}, bf16[256,512]{1,0:T(8,128)(2,1)S(1)}, u32[]{:S(2)}) copy-start(bf16[256,512]{1,0:T(8,128)(2,1)S(1)} %collective-permute-done.1.keys1_ref) | copy-start | bytes 786436
  52.4 20.1 %collective-permute-start.2 = (bf16[512,512]{1,0:T(8,128)(2,1)}, bf16[512,512]{1,0:T(8,128)(2,1)}, u32[]{:S(2)}, u32[]{:S(2)}) collective-permute-start(bf16[512,512]{1,0:T(8,128)(2,1)} %pad_maximum_fusion), channel_id=1, source_target_pairs={{0,1},{1,2},{2,3},{3,4},{4,5},{5,6},{6,7},{7,8},{8,9},{9,10},{10,1... | collective-permute-start | bytes 1572872 | tf_op jit(solution)/shard_map/ppermute | solution.py:39
  55.7 6.1 %copy-start.6 = (bf16[64,512]{1,0:T(8,128)(2,1)S(1)}, bf16[64,512]{1,0:T(8,128)(2,1)}, u32[]{:S(2)}) copy-start(bf16[64,512]{1,0:T(8,128)(2,1)} %up_ref) | copy-start | bytes 196612
  61.8 1.2 copy-start.4
  63.0 7.2 %copy-start.2 = (bf16[128,8192]{1,0:T(8,128)(2,1)S(1)}, bf16[128,8192]{1,0:T(8,128)(2,1)}, u32[]{:S(2)}) copy-start(bf16[128,8192]{1,0:T(8,128)(2,1)} %hidden_ref.3) | copy-start | bytes 6291460
  70.2 2.3 %copy-start.1 = (f32[1024,128]{1,0:T(8,128)S(1)}, f32[1024,128]{1,0:T(8,128)}, u32[]{:S(2)}) copy-start(f32[1024,128]{1,0:T(8,128)} %fusion.1.bias_ref) | copy-start | bytes 1572868
  70.2 2.3 %copy-start.3 = (bf16[128,4096]{1,0:T(8,128)(2,1)S(1)}, bf16[128,4096]{1,0:T(8,128)(2,1)}, u32[]{:S(2)}) copy-start(bf16[128,4096]{1,0:T(8,128)(2,1)} %query_ref.3) | copy-start | bytes 3145732
  71.1 6.2 %copy-start.11 = (bf16[64,4096]{1,0:T(8,128)(2,1)S(1)}, bf16[64,4096]{1,0:T(8,128)(2,1)}, u32[]{:S(2)}) copy-start(bf16[64,4096]{1,0:T(8,128)(2,1)} %copy-done.10) | copy-start | bytes 1572868
  71.1 6.2 %copy-start.12 = (f32[8,4096]{1,0:T(8,128)S(1)}, f32[8,4096]{1,0:T(8,128)}, u32[]{:S(2)}) copy-start(f32[8,4096]{1,0:T(8,128)} %get-tuple-element.24.stats_ref) | copy-start | bytes 393220
  71.1 8.8 %collective-permute-start.6 = (bf16[64,128]{1,0:T(8,128)(2,1)S(1)}, bf16[64,128]{1,0:T(8,128)(2,1)S(1)}, u32[]{:S(2)}, u32[]{:S(2)}) collective-permute-start(bf16[64,128]{1,0:T(8,128)(2,1)S(1)} %lowrank.1), channel_id=1, source_target_pairs={{0,4},{1,5},{2,6},{3,7},{4,8},{5,9},{6,10},{7,11},{8,12},{9,13},{1... | collective-permute-start | bytes 49160 | tf_op jit(solution)/shard_map/ppermute | solution.py:39
  77.3 4.0 %copy-start.8 = (bf16[256,4096]{1,0:T(8,128)(2,1)S(1)}, bf16[256,4096]{1,0:T(8,128)(2,1)}, u32[]{:S(2)}) copy-start(bf16[256,4096]{1,0:T(8,128)(2,1)} %get-tuple-element.17.w1_ref) | copy-start | bytes 6291460
  77.3 4.0 %copy-start.9 = (bf16[256,4096]{1,0:T(8,128)(2,1)S(1)}, bf16[256,4096]{1,0:T(8,128)(2,1)}, u32[]{:S(2)}) copy-start(bf16[256,4096]{1,0:T(8,128)(2,1)} %get-tuple-element.18.w0_ref) | copy-start | bytes 6291460
  78.6 8.0 %collective-permute-start.3 = (bf16[64,512]{1,0:T(8,128)(2,1)S(1)}, bf16[64,512]{1,0:T(8,128)(2,1)S(1)}, u32[]{:S(2)}, u32[]{:S(2)}) collective-permute-start(bf16[64,512]{1,0:T(8,128)(2,1)S(1)} %get-tuple-element.27), channel_id=1, source_target_pairs={{1,0},{2,1},{3,2},{4,3},{5,4},{6,5},{7,6},{8,7},{9,8},{10,9},{11,1... | collective-permute-start | bytes 196616 | tf_op jit(solution)/shard_map/ppermute | solution.py:39
  79.9 2.6 %collective-permute-start.7 = (bf16[64,256]{1,0:T(8,128)(2,1)S(1)}, bf16[64,256]{1,0:T(8,128)(2,1)S(1)}, u32[]{:S(2)}, u32[]{:S(2)}) collective-permute-start(bf16[64,256]{1,0:T(8,128)(2,1)S(1)} %pad_maximum_fusion.3), channel_id=1, source_target_pairs={{0,2},{1,3},{2,4},{3,5},{4,6},{5,7},{6,8},{7,9},{8,10},{9,11},{10,... | collective-permute-start | bytes 98312 | tf_op jit(solution)/shard_map/ppermute | solution.py:39
  81.2 6.7 %copy-start.5 = (bf16[128,4096]{1,0:T(8,128)(2,1)S(1)}, bf16[128,4096]{1,0:T(8,128)(2,1)}, u32[]{:S(2)}) copy-start(bf16[128,4096]{1,0:T(8,128)(2,1)} %gradient_ref.5) | copy-start | bytes 3145732
  82.6 5.3 %collective-permute-start.8 = (bf16[64,512]{1,0:T(8,128)(2,1)S(1)}, bf16[64,512]{1,0:T(8,128)(2,1)S(1)}, u32[]{:S(2)}, u32[]{:S(2)}) collective-permute-start(bf16[64,512]{1,0:T(8,128)(2,1)S(1)} %pad_maximum_fusion.2), channel_id=1, source_target_pairs={{0,1},{1,2},{2,3},{3,4},{4,5},{5,6},{6,7},{7,8},{8,9},{9,10},{10,1... | collective-permute-start | bytes 196616 | tf_op jit(solution)/shard_map/ppermute | solution.py:39
  86.6 6.6 %collective-permute-start.4 = (f32[64,256]{1,0:T(8,128)S(1)}, f32[64,256]{1,0:T(8,128)S(1)}, u32[]{:S(2)}, u32[]{:S(2)}) collective-permute-start(f32[64,256]{1,0:T(8,128)S(1)} %slice.59), channel_id=1, source_target_pairs={{2,0},{3,1},{4,2},{5,3},{6,4},{7,5},{8,6},{9,7},{10,8},{11,9},{12,... | collective-permute-start | bytes 196616 | tf_op jit(solution)/shard_map/ppermute | solution.py:39
  93.3 8.6 %collective-permute-start.5 = (f32[64,128]{1,0:T(8,128)S(1)}, f32[64,128]{1,0:T(8,128)S(1)}, u32[]{:S(2)}, u32[]{:S(2)}) collective-permute-start(f32[64,128]{1,0:T(8,128)S(1)} %slice.61), channel_id=1, source_target_pairs={{4,0},{5,1},{6,2},{7,3},{8,4},{9,5},{10,6},{11,7},{12,8},{13,9},{1... | collective-permute-start | bytes 98312 | tf_op jit(solution)/shard_map/ppermute | solution.py:39
  (3 other events, 2.3 us)

commit v8 on v7

--- a/solution.py
+++ b/solution.py
@@ -43,10 +43,6 @@
     return lax.all_to_all(slots, axis, 0, 0, tiled=True)
 
 
-def docs_kernel(in_ref, out_ref):
-    out_ref[...] = in_ref[...]
-
-
 def lowrank_kernel(weight_ref, hidden_ref, out_ref):
     total = jnp.zeros((ADAPTER_RANK, TOKENS), F32)
     for f in range(N_FSDP):
@@ -238,8 +234,7 @@
     member = lax.axis_index("dp")
     half, part = member // 8, member % 8
 
-    pair0 = jnp.concatenate([from_behind(keys, 4), keys], axis=0)
-    pair1 = from_behind(pair0, 2)
+    keys4 = from_behind(keys, 4)
     weight_slice = lax.dynamic_slice(adapter_down_weight.T, (part * 8, half * 128), (8, 128))
     slot = jnp.concatenate(
         [
@@ -249,22 +244,21 @@
         ],
         axis=0,
     )
-    docs_row = plain(
-        docs_kernel, "docs", jax.ShapeDtypeStruct((1, TOKENS), jnp.int32), document_numbers
-    )
     slots = jnp.broadcast_to(slot[None], (N_FSDP, 16, 128))
     row_parts = exchange(slots, "fsdp")
     weight_part = row_parts[:, :8].transpose(1, 0, 2).reshape(1, 8, DOWN)
     docs = row_parts[:, 8].astype(jnp.int32)
     weight_slots = jnp.broadcast_to(weight_part, (N_DP, 8, DOWN))
     weight = exchange(weight_slots, "dp").reshape(2, ADAPTER_RANK, DOWN)
-    pair1 = lax.optimization_barrier((pair1, weight_slots))[0]
+    keys4 = lax.optimization_barrier((keys4, weight_slots))[0]
+    pair0 = jnp.concatenate([keys4, keys], axis=0)
+    pair1 = from_behind(pair0, 2)
     quad = from_behind(jnp.concatenate([pair1, pair0], axis=0), 1)
 
     padded = jnp.concatenate([jnp.full((SPAN - 1, TOKENS), -1, jnp.int32), docs], axis=0)
     window_docs = lax.dynamic_slice(padded, (position, 0), (SPAN, TOKENS))
     window_docs = jnp.concatenate([window_docs[7 - d : 8 - d] for d in ORDER]).reshape(WINDOW)
-    own_docs = docs_row[0]
+    own_docs = document_numbers.reshape(TOKENS)
     key_pos = jnp.concatenate([jnp.arange(TOKENS, dtype=jnp.int32) - d * TOKENS for d in ORDER])
     visible = (window_docs[:, None] == own_docs[None, :]) & (
         key_pos[:, None] <= jnp.arange(TOKENS, dtype=jnp.int32)[None, :]
@@ -298,7 +292,7 @@
         lowrank_kernel, "lowrank", jax.ShapeDtypeStruct((ADAPTER_RANK, TOKENS), BF16), weight, hidden
     )
     rank1 = jnp.concatenate([from_behind(rank, 4), rank], axis=1)
-    quad, rank, stats = lax.optimization_barrier((quad, rank, stats))
+    quad, rank1, stats = lax.optimization_barrier((quad, rank1, stats))
     rank2 = jnp.concatenate([from_behind(rank1, 2), rank1], axis=1)
     w3, w2, last = plain(
         last_score_kernel,
@@ -308,6 +302,7 @@
         quad,
         bias,
     )
+    w3, rank2 = lax.optimization_barrier((w3, rank2))
     far, scale = plain(
         far_kernel,
         "far",

time: 182 us -> 197 us (1.082)
  waiting for transfers between devices: 23.8 us -> 32.3 us
  starting transfers between devices: 48.4 us -> 56.1 us
  local copies, waits for them, and re-layouts: 5.46 us -> 2.04 us
    ppermute x9, starting transfers between devices: 26.4 us -> 35.7 us  [from_behind(): return lax.ppermute(block, 'fsdp', route)]
    ppermute x9, waiting for transfers between devices: 7.75 us -> 16 us  [from_behind(): return lax.ppermute(block, 'fsdp', route)]
    unnamed x34 -> x29, local copies, waits for them, and re-layouts: 3.49 us -> 0.09 us
    pallas_call x12 -> x11, Pallas kernels: 15.4 us -> 15.4 us  [plain(): pl.pallas_call(kernel, in_specs=whole(*arrays), out_specs=jax.tree.map(la...]
  transfers between devices with their start and end apart: 11 -> 11, of which waited for: 4 -> 4; matrix products, arithmetic and copies ran while one was open for 3% -> 2% of each run, Pallas kernels for 11% -> 10%
where the time goes in v8:
time: 197 us; the launch traced here: 196 us
  blocking collectives  80.1 us (41%)
  starting transfers between devices  56.1 us (28%)
  waiting for transfers between devices  32.3 us (16%)
  Pallas kernels  21.4 us (11%)
  other arithmetic  2.9 us (1%)
  local copies, waits for them, and re-layouts  2.04 us (1%)
    all_to_all x3, blocking collectives, exchange(): return lax.all_to_all(slots, axis, 0, 0, tiled=True)  80.1 us
    ppermute x9, starting transfers between devices, from_behind(): return lax.ppermute(block, 'fsdp', route)  35.7 us
    all_to_all x2, starting transfers between devices, exchange(): return lax.all_to_all(slots, axis, 0, 0, tiled=True)  20.5 us
    all_to_all x2, waiting for transfers between devices, exchange(): return lax.all_to_all(slots, axis, 0, 0, tiled=True)  16.3 us
    ppermute x9, waiting for transfers between devices, from_behind(): return lax.ppermute(block, 'fsdp', route)  16 us
    pallas_call x11, Pallas kernels, plain(): pl.pallas_call(kernel, in_specs=whole(*arrays), out_specs=jax.tree.map(la...  15.4 us
    pallas_call x1, Pallas kernels, by_steps(): pl.pallas_call(kernel, grid=(steps,), in_specs=[spec for spec, _ in given...  5.98 us
  transfers between devices with their start and end apart: 11, of which 4 were waited for; matrix products, arithmetic and copies ran while one was open for 2% of the time, Pallas kernels for 10%

profile of v8, /device:TPU:1, one launch (start us, length us, event | category | flops | bytes accessed | tf_op | source)
XLA Modules:
  0.0 195.9 jit_solution(7739446489309289796)
XLA Ops:
  0.7 9.8 %collective-permute-start = (bf16[128,512]{1,0:T(8,128)(2,1)}, bf16[128,512]{1,0:T(8,128)(2,1)S(1)}, u32[]{:S(2)}, u32[]{:S(2)}) collective-permute-start(bf16[128,512]{1,0:T(8,128)(2,1)} %param.9), channel_id=1, source_target_pairs={{0,4},{1,5},{2,6},{3,7},{4,8},{5,9},{6,10},{7,11},{8,12},{9,13},{1... | collective-permute-start | bytes 393224 | tf_op jit(solution)/shard_map/ppermute | solution.py:39
  12.0 13.2 %all-to-all-start = ((bf16[32,16,128]{2,1,0:T(8,128)(2,1)}), bf16[32,16,128]{2,1,0:T(8,128)(2,1)S(1)}, u32[]{:S(2)}, u32[]{:S(2)}) async-start(bf16[32,16,128]{2,1,0:T(8,128)(2,1)} %broadcast_in_dim.28), calls=%async_computation | async-start | bytes 262144 | tf_op jit(solution)/shard_map/all_to_all | solution.py:43
  25.2 16.3 %all-to-all-done = bf16[32,16,128]{2,1,0:T(8,128)(2,1)S(1)} async-done(((bf16[32,16,128]{2,1,0:T(8,128)(2,1)}), bf16[32,16,128]{2,1,0:T(8,128)(2,1)S(1)}, u32[]{:S(2)}, u32[]{:S(2)}) %all-to-all-start) | async-done | bytes 131104 | tf_op jit(solution)/shard_map/all_to_all | solution.py:43
  42.7 7.3 %all-to-all-start.1 = ((bf16[16,8,4096]{2,1,0:T(8,128)(2,1)}), bf16[16,8,4096]{2,1,0:T(8,128)(2,1)S(1)}, u32[]{:S(2)}, u32[]{:S(2)}) async-start(bf16[16,8,4096]{2,1,0:T(8,128)(2,1)} %broadcast_in_dim.30), calls=%async_computation.1 | async-start | bytes 2097152 | tf_op jit(solution)/shard_map/all_to_all | solution.py:43
  50.0 1.9 collective-permute-start.1
  53.2 5.8 %collective-permute-done.1.keys1_ref = bf16[256,512]{1,0:T(8,128)(2,1)S(1)} collective-permute-done((bf16[256,512]{1,0:T(8,128)(2,1)S(1)}, bf16[256,512]{1,0:T(8,128)(2,1)S(1)}, u32[]{:S(2)}, u32[]{:S(2)}) %collective-permute-start.1) | collective-permute-done | bytes 262176 | tf_op jit(solution)/shard_map/ppermute | solution.py:39
  59.9 8.3 %collective-permute-start.2 = (bf16[512,512]{1,0:T(8,128)(2,1)}, bf16[512,512]{1,0:T(8,128)(2,1)}, u32[]{:S(2)}, u32[]{:S(2)}) collective-permute-start(bf16[512,512]{1,0:T(8,128)(2,1)} %pad_maximum_fusion), channel_id=1, source_target_pairs={{0,1},{1,2},{2,3},{3,4},{4,5},{5,6},{6,7},{7,8},{8,9},{9,10},{10,1... | collective-permute-start | bytes 1572872 | tf_op jit(solution)/shard_map/ppermute | solution.py:39
  68.2 6.0 %score.1 = (bf16[256,4096]{1,0:T(8,128)(2,1)}, bf16[256,4096]{1,0:T(8,128)(2,1)}, f32[8,4096]{1,0:T(8,128)}) custom-call(bf16[128,4096]{1,0:T(8,128)(2,1)} %query_ref.3, bf16[256,512]{1,0:T(8,128)(2,1)} %copy-done.10, bf16[256,512]{1,0:T(8,128)(2,1)} %copy-done.11, f32[1024,128]{1,0:T(8,128)} %fusion.1.bias_ref), custom_call_target="tpu_custom_call" | custom-call | flops 10000000000 | bytes 134217728 | tf_op jit(solution)/shard_map/score/pallas_call | solution.py:209
  75.1 5.6 %collective-permute-start.3 = (bf16[64,128]{1,0:T(8,128)(2,1)S(1)}, bf16[64,128]{1,0:T(8,128)(2,1)S(1)}, u32[]{:S(2)}, u32[]{:S(2)}) collective-permute-start(bf16[64,128]{1,0:T(8,128)(2,1)S(1)} %lowrank.1), channel_id=1, source_target_pairs={{0,4},{1,5},{2,6},{3,7},{4,8},{5,9},{6,10},{7,11},{8,12},{9,13},{1... | collective-permute-start | bytes 49160 | tf_op jit(solution)/shard_map/ppermute | solution.py:39
  82.0 1.8 collective-permute-start.4
  83.8 4.7 %last_score.1 = (bf16[256,4096]{1,0:T(8,128)(2,1)S(1)}, bf16[256,4096]{1,0:T(8,128)(2,1)S(1)}, f32[4,4096]{1,0:T(4,128)S(1)}) custom-call(bf16[128,4096]{1,0:T(8,128)(2,1)S(1)} %copy-done.3, bf16[512,512]{1,0:T(8,128)(2,1)} %collective-permute-done.2.keys_ref, f32[1024,128]{1,0:T(8,128)S(1)} %copy-done.1), custom_call_target="tpu_custom_call" | custom-call | flops 10000000000 | bytes 134217728 | tf_op jit(solution)/shard_map/last_score/pallas_call | solution.py:197
  88.5 1.3 far.1
  89.9 1.3 collective-permute-start.5
  91.2 4.3 %collective-permute-start.8 = (bf16[64,512]{1,0:T(8,128)(2,1)S(1)}, bf16[64,512]{1,0:T(8,128)(2,1)S(1)}, u32[]{:S(2)}, u32[]{:S(2)}) collective-permute-start(bf16[64,512]{1,0:T(8,128)(2,1)S(1)} %pad_maximum_fusion.1), channel_id=1, source_target_pairs={{0,1},{1,2},{2,3},{3,4},{4,5},{5,6},{6,7},{7,8},{8,9},{9,10},{10,1... | collective-permute-start | bytes 196616 | tf_op jit(solution)/shard_map/ppermute | solution.py:39
  95.5 1.3 near.1
  96.9 1.3 collective-permute-start.6
  98.2 2.4 %mixed.2.up0_ref = f32[64,256]{1,0:T(8,128)S(1)} custom-call(bf16[256,4096]{1,0:T(8,128)(2,1)S(1)} %get-tuple-element.26.w3_ref, bf16[256,4096]{1,0:T(8,128)(2,1)S(1)} %get-tuple-element.27.w2_ref, bf16[256,4096]{1,0:T(8,128)(2,1)S(1)} %copy-done.6, bf16[256,4096]{1,0:T(8,128)(2,1)S(1)} %copy-done.7, f32[4,4096]{1,0:T(4,128)S(1)} %get-tuple-element.31.scale_ref, ...), custom_call_target="tpu_custom_call" | custom-call | flops 10000000000 | bytes 134217728 | tf_op jit(solution)/shard_map/mixed/pallas_call | solution.py:197
  100.6 5.3 %collective-permute-done.6 = f32[64,256]{1,0:T(8,128)S(1)} collective-permute-done((f32[64,256]{1,0:T(8,128)S(1)}, f32[64,256]{1,0:T(8,128)S(1)}, u32[]{:S(2)}, u32[]{:S(2)}) %collective-permute-start.6) | collective-permute-done | bytes 65568 | tf_op jit(solution)/shard_map/ppermute | solution.py:39
  106.0 1.3 collective-permute-start.7
  107.3 2.4 %mixed.3.up1_ref = f32[64,256]{1,0:T(8,128)S(1)} custom-call(bf16[256,4096]{1,0:T(8,128)(2,1)S(1)} %get-tuple-element.26.w3_ref, bf16[256,4096]{1,0:T(8,128)(2,1)S(1)} %get-tuple-element.27.w2_ref, bf16[256,4096]{1,0:T(8,128)(2,1)S(1)} %copy-done.6, bf16[256,4096]{1,0:T(8,128)(2,1)S(1)} %copy-done.7, f32[4,4096]{1,0:T(4,128)S(1)} %get-tuple-element.31.scale_ref, ...), custom_call_target="tpu_custom_call" | custom-call | flops 10000000000 | bytes 134217728 | tf_op jit(solution)/shard_map/mixed/pallas_call | solution.py:197
  109.7 4.9 %collective-permute-done.7 = f32[64,128]{1,0:T(8,128)S(1)} collective-permute-done((f32[64,128]{1,0:T(8,128)S(1)}, f32[64,128]{1,0:T(8,128)S(1)}, u32[]{:S(2)}, u32[]{:S(2)}) %collective-permute-start.7) | collective-permute-done | bytes 32800 | tf_op jit(solution)/shard_map/ppermute | solution.py:39
  115.0 27.4 %all_to_all.25.in_ref = bf16[16,8,4352]{2,1,0:T(8,128)(2,1)S(1)} all-to-all(bf16[16,8,4352]{2,1,0:T(8,128)(2,1)S(1)} %bitcast.14), channel_id=1, replica_groups=mesh['dp'=16,'fsdp'=32] {'dp'}, dimensions={0} | all-to-all | bytes 2228224 | tf_op jit(solution)/shard_map/all_to_all | solution.py:43
  142.5 40.6 %all_to_all.26.in_ref = bf16[32,8,384]{2,1,0:T(8,128)(2,1)S(1)} all-to-all(bf16[32,8,384]{2,1,0:T(8,128)(2,1)S(1)} %fold_dp.1), channel_id=1, replica_groups=mesh['dp'=16,'fsdp'=32] {'fsdp'}, dimensions={0} | all-to-all | bytes 393216 | tf_op jit(solution)/shard_map/all_to_all | solution.py:43
  183.2 12.0 %all_to_all.27.in_ref = f32[16,8,384]{2,1,0:T(8,128)S(1)} all-to-all(f32[16,8,384]{2,1,0:T(8,128)S(1)} %fold_fsdp.1), channel_id=1, replica_groups=mesh['dp'=16,'fsdp'=32] {'dp'}, dimensions={0} | all-to-all | bytes 393216 | tf_op jit(solution)/shard_map/all_to_all | solution.py:43
  (74 shorter events, 8.3 us)
Async XLA Ops:
  0.6 10.6 %copy-start = (bf16[256,64]{0,1:T(8,128)(2,1)S(1)}, bf16[256,64]{0,1:T(8,128)(2,1)}, u32[]{:S(2)}) copy-start(bf16[256,64]{0,1:T(8,128)(2,1)} %param.11) | copy-start | bytes 98308
  0.6 49.4 %copy-start.9 = (bf16[128,512]{1,0:T(8,128)(2,1)S(1)}, bf16[128,512]{1,0:T(8,128)(2,1)}, u32[]{:S(2)}) copy-start(bf16[128,512]{1,0:T(8,128)(2,1)} %param.9) | copy-start | bytes 393220
  0.7 49.3 %collective-permute-start = (bf16[128,512]{1,0:T(8,128)(2,1)}, bf16[128,512]{1,0:T(8,128)(2,1)S(1)}, u32[]{:S(2)}, u32[]{:S(2)}) collective-permute-start(bf16[128,512]{1,0:T(8,128)(2,1)} %param.9), channel_id=1, source_target_pairs={{0,4},{1,5},{2,6},{3,7},{4,8},{5,9},{6,10},{7,11},{8,12},{9,13},{1... | collective-permute-start | bytes 393224 | tf_op jit(solution)/shard_map/ppermute | solution.py:39
  12.0 40.1 %copy-start.12 = (s32[1,128]{1,0:T(1,128)S(1)}, s32[1,128]{1,0:T(1,128)}, u32[]{:S(2)}) copy-start(s32[1,128]{1,0:T(1,128)} %param.10) | copy-start | bytes 1540
  12.0 29.6 %all-to-all-start = ((bf16[32,16,128]{2,1,0:T(8,128)(2,1)}), bf16[32,16,128]{2,1,0:T(8,128)(2,1)S(1)}, u32[]{:S(2)}, u32[]{:S(2)}) async-start(bf16[32,16,128]{2,1,0:T(8,128)(2,1)} %broadcast_in_dim.28), calls=%async_computation | async-start | bytes 262144 | tf_op jit(solution)/shard_map/all_to_all | solution.py:43
  42.7 31.6 %all-to-all-start.1 = ((bf16[16,8,4096]{2,1,0:T(8,128)(2,1)}), bf16[16,8,4096]{2,1,0:T(8,128)(2,1)S(1)}, u32[]{:S(2)}, u32[]{:S(2)}) async-start(bf16[16,8,4096]{2,1,0:T(8,128)(2,1)} %broadcast_in_dim.30), calls=%async_computation.1 | async-start | bytes 2097152 | tf_op jit(solution)/shard_map/all_to_all | solution.py:43
  50.0 9.0 %copy-start.11 = (bf16[256,512]{1,0:T(8,128)(2,1)}, bf16[256,512]{1,0:T(8,128)(2,1)S(1)}, u32[]{:S(2)}) copy-start(bf16[256,512]{1,0:T(8,128)(2,1)S(1)} %constant_dynamic-update-slice_fusion.keys0_ref) | copy-start | bytes 786436
  50.0 8.9 %collective-permute-start.1 = (bf16[256,512]{1,0:T(8,128)(2,1)S(1)}, bf16[256,512]{1,0:T(8,128)(2,1)S(1)}, u32[]{:S(2)}, u32[]{:S(2)}) collective-permute-start(bf16[256,512]{1,0:T(8,128)(2,1)S(1)} %constant_dynamic-update-slice_fusion.keys0_ref), channel_id=1, source_target_pairs={{0,2},{1,3},{2,4},{3,5},{4,6},{5,7},{6,8},{7,9},{8,10},{9,11},{10,... | collective-permute-start | bytes 786440 | tf_op jit(solution)/shard_map/ppermute | solution.py:39
  59.0 9.3 %copy-start.10 = (bf16[256,512]{1,0:T(8,128)(2,1)}, bf16[256,512]{1,0:T(8,128)(2,1)S(1)}, u32[]{:S(2)}) copy-start(bf16[256,512]{1,0:T(8,128)(2,1)S(1)} %collective-permute-done.1.keys1_ref) | copy-start | bytes 786436
  59.9 14.3 %copy-start.2 = (bf16[128,8192]{1,0:T(8,128)(2,1)S(1)}, bf16[128,8192]{1,0:T(8,128)(2,1)}, u32[]{:S(2)}) copy-start(bf16[128,8192]{1,0:T(8,128)(2,1)} %hidden_ref.3) | copy-start | bytes 6291460
  59.9 22.1 %collective-permute-start.2 = (bf16[512,512]{1,0:T(8,128)(2,1)}, bf16[512,512]{1,0:T(8,128)(2,1)}, u32[]{:S(2)}, u32[]{:S(2)}) collective-permute-start(bf16[512,512]{1,0:T(8,128)(2,1)} %pad_maximum_fusion), channel_id=1, source_target_pairs={{0,1},{1,2},{2,3},{3,4},{4,5},{5,6},{6,7},{7,8},{8,9},{9,10},{10,1... | collective-permute-start | bytes 1572872 | tf_op jit(solution)/shard_map/ppermute | solution.py:39
  74.2 6.5 %copy-start.4 = (bf16[128,4096]{1,0:T(8,128)(2,1)S(1)}, bf16[128,4096]{1,0:T(8,128)(2,1)}, u32[]{:S(2)}) copy-start(bf16[128,4096]{1,0:T(8,128)(2,1)} %gradient_ref.5) | copy-start | bytes 3145732
  74.3 6.5 %copy-start.5 = (bf16[64,512]{1,0:T(8,128)(2,1)S(1)}, bf16[64,512]{1,0:T(8,128)(2,1)}, u32[]{:S(2)}) copy-start(bf16[64,512]{1,0:T(8,128)(2,1)} %up_ref) | copy-start | bytes 196612
  75.1 8.7 %copy-start.1 = (f32[1024,128]{1,0:T(8,128)S(1)}, f32[1024,128]{1,0:T(8,128)}, u32[]{:S(2)}) copy-start(f32[1024,128]{1,0:T(8,128)} %fusion.1.bias_ref) | copy-start | bytes 1572868
  75.1 8.7 %copy-start.3 = (bf16[128,4096]{1,0:T(8,128)(2,1)S(1)}, bf16[128,4096]{1,0:T(8,128)(2,1)}, u32[]{:S(2)}) copy-start(bf16[128,4096]{1,0:T(8,128)(2,1)} %query_ref.3) | copy-start | bytes 3145732
  75.1 6.8 %collective-permute-start.3 = (bf16[64,128]{1,0:T(8,128)(2,1)S(1)}, bf16[64,128]{1,0:T(8,128)(2,1)S(1)}, u32[]{:S(2)}, u32[]{:S(2)}) collective-permute-start(bf16[64,128]{1,0:T(8,128)(2,1)S(1)} %lowrank.1), channel_id=1, source_target_pairs={{0,4},{1,5},{2,6},{3,7},{4,8},{5,9},{6,10},{7,11},{8,12},{9,13},{1... | collective-permute-start | bytes 49160 | tf_op jit(solution)/shard_map/ppermute | solution.py:39
  82.0 6.5 %copy-start.8 = (f32[8,4096]{1,0:T(8,128)S(1)}, f32[8,4096]{1,0:T(8,128)}, u32[]{:S(2)}) copy-start(f32[8,4096]{1,0:T(8,128)} %get-tuple-element.29.stats_ref) | copy-start | bytes 393220
  82.0 6.5 %collective-permute-start.4 = (bf16[64,256]{1,0:T(8,128)(2,1)S(1)}, bf16[64,256]{1,0:T(8,128)(2,1)S(1)}, u32[]{:S(2)}, u32[]{:S(2)}) collective-permute-start(bf16[64,256]{1,0:T(8,128)(2,1)S(1)} %pad_maximum_fusion.2), channel_id=1, source_target_pairs={{0,2},{1,3},{2,4},{3,5},{4,6},{5,7},{6,8},{7,9},{8,10},{9,11},{10,... | collective-permute-start | bytes 98312 | tf_op jit(solution)/shard_map/ppermute | solution.py:39
  88.5 7.0 %copy-start.6 = (bf16[256,4096]{1,0:T(8,128)(2,1)S(1)}, bf16[256,4096]{1,0:T(8,128)(2,1)}, u32[]{:S(2)}) copy-start(bf16[256,4096]{1,0:T(8,128)(2,1)} %get-tuple-element.20.w1_ref) | copy-start | bytes 6291460
  88.5 7.0 %copy-start.7 = (bf16[256,4096]{1,0:T(8,128)(2,1)S(1)}, bf16[256,4096]{1,0:T(8,128)(2,1)}, u32[]{:S(2)}) copy-start(bf16[256,4096]{1,0:T(8,128)(2,1)} %get-tuple-element.21.w0_ref) | copy-start | bytes 6291460
  89.9 7.0 %collective-permute-start.5 = (bf16[64,512]{1,0:T(8,128)(2,1)S(1)}, bf16[64,512]{1,0:T(8,128)(2,1)S(1)}, u32[]{:S(2)}, u32[]{:S(2)}) collective-permute-start(bf16[64,512]{1,0:T(8,128)(2,1)S(1)} %get-tuple-element.32), channel_id=1, source_target_pairs={{1,0},{2,1},{3,2},{4,3},{5,4},{6,5},{7,6},{8,7},{9,8},{10,9},{11,1... | collective-permute-start | bytes 196616 | tf_op jit(solution)/shard_map/ppermute | solution.py:39
  91.2 7.0 %collective-permute-start.8 = (bf16[64,512]{1,0:T(8,128)(2,1)S(1)}, bf16[64,512]{1,0:T(8,128)(2,1)S(1)}, u32[]{:S(2)}, u32[]{:S(2)}) collective-permute-start(bf16[64,512]{1,0:T(8,128)(2,1)S(1)} %pad_maximum_fusion.1), channel_id=1, source_target_pairs={{0,1},{1,2},{2,3},{3,4},{4,5},{5,6},{6,7},{7,8},{8,9},{9,10},{10,1... | collective-permute-start | bytes 196616 | tf_op jit(solution)/shard_map/ppermute | solution.py:39
  96.9 9.1 %collective-permute-start.6 = (f32[64,256]{1,0:T(8,128)S(1)}, f32[64,256]{1,0:T(8,128)S(1)}, u32[]{:S(2)}, u32[]{:S(2)}) collective-permute-start(f32[64,256]{1,0:T(8,128)S(1)} %slice.59), channel_id=1, source_target_pairs={{2,0},{3,1},{4,2},{5,3},{6,4},{7,5},{8,6},{9,7},{10,8},{11,9},{12,... | collective-permute-start | bytes 196616 | tf_op jit(solution)/shard_map/ppermute | solution.py:39
  106.0 8.6 %collective-permute-start.7 = (f32[64,128]{1,0:T(8,128)S(1)}, f32[64,128]{1,0:T(8,128)S(1)}, u32[]{:S(2)}, u32[]{:S(2)}) collective-permute-start(f32[64,128]{1,0:T(8,128)S(1)} %slice.61), channel_id=1, source_target_pairs={{4,0},{5,1},{6,2},{7,3},{8,4},{9,5},{10,6},{11,7},{12,8},{13,9},{1... | collective-permute-start | bytes 98312 | tf_op jit(solution)/shard_map/ppermute | solution.py:39

commit v9 on v6

--- a/solution.py
+++ b/solution.py
@@ -154,7 +154,10 @@
             lanes = slice(h * 128, h * 128 + 128)
             mixed = jnp.zeros((ADAPTER_RANK, TOKENS), F32)
             for i, ref in enumerate((w3_ref, w2_ref, w1_ref, w0_ref)):
-                rank = rank_ref[:, i * 256 : i * 256 + 256]
+                at = (0, 2, 1, 3)[i] * 128
+                rank = jnp.concatenate(
+                    [rank_ref[:, at : at + 128], rank_ref[:, 512 + at : 640 + at]], axis=1
+                )
                 part = jnp.dot(rank, ref[:, lanes], preferred_element_type=F32)
                 mixed += part * scale_ref[i : i + 1, lanes]
             share += jnp.dot(
@@ -305,7 +308,7 @@
     rank = plain(
         lowrank_kernel, "lowrank", jax.ShapeDtypeStruct((ADAPTER_RANK, TOKENS), BF16), weight, hidden
     )
-    rank1 = jnp.concatenate([from_behind(rank, 1), rank], axis=1)
+    rank1 = jnp.concatenate([from_behind(rank, 4), rank], axis=1)
     pair3, rank1, stats = lax.optimization_barrier((pair3, rank1, stats))
     rank2 = jnp.concatenate([from_behind(rank1, 2), rank1], axis=1)
     w3, last = plain(
@@ -341,7 +344,7 @@
     )
     came = from_behind(far, -4)
     near = near + came.astype(F32)
-    rank3 = jnp.concatenate([from_behind(rank2, 4), rank2], axis=1)
+    rank3 = jnp.concatenate([from_behind(rank2, 1), rank2], axis=1)
     came = from_behind(near[:, :256], -2)
     near = near[:, 256:] + came
     came = from_behind(near[:, :128], -1)

time: 178 us -> 184 us (1.034)
  waiting for transfers between devices: 19.8 us -> 28.9 us
  starting transfers between devices: 60.1 us -> 51.8 us
  blocking collectives: 70.4 us -> 75.3 us
    ppermute x11, waiting for transfers between devices: 3.42 us -> 12.5 us  [from_behind(): return lax.ppermute(block, 'fsdp', route)]
    ppermute x11, starting transfers between devices: 39.3 us -> 31 us  [from_behind(): return lax.ppermute(block, 'fsdp', route)]
    all_to_all x3, blocking collectives: 70.4 us -> 75.3 us  [exchange(): return lax.all_to_all(slots, axis, 0, 0, tiled=True)]
  transfers between devices with their start and end apart: 13 -> 13, of which waited for: 4 -> 5; matrix products, arithmetic and copies ran while one was open for 3% -> 2% of each run, Pallas kernels for 10% -> 10%
where the time goes in v9:
time: 184 us; the launch traced here: 183 us
  blocking collectives  75.3 us (41%)
  starting transfers between devices  51.8 us (28%)
  waiting for transfers between devices  28.9 us (16%)
  Pallas kernels  20.5 us (11%)
  other arithmetic  2.7 us (1%)
  local copies, waits for them, and re-layouts  2.6 us (1%)
    all_to_all x3, blocking collectives, exchange(): return lax.all_to_all(slots, axis, 0, 0, tiled=True)  75.3 us
    ppermute x11, starting transfers between devices, from_behind(): return lax.ppermute(block, 'fsdp', route)  31 us
    all_to_all x2, starting transfers between devices, exchange(): return lax.all_to_all(slots, axis, 0, 0, tiled=True)  20.8 us
    all_to_all x2, waiting for transfers between devices, exchange(): return lax.all_to_all(slots, axis, 0, 0, tiled=True)  16.4 us
    pallas_call x12, Pallas kernels, plain(): pl.pallas_call(kernel, in_specs=whole(*arrays), out_specs=jax.tree.map(la...  12.9 us
    ppermute x11, waiting for transfers between devices, from_behind(): return lax.ppermute(block, 'fsdp', route)  12.5 us
    pallas_call x1, Pallas kernels, by_steps(): pl.pallas_call(kernel, grid=(steps,), in_specs=[spec for spec, _ in given...  7.66 us
  transfers between devices with their start and end apart: 13, of which 5 were waited for; matrix products, arithmetic and copies ran while one was open for 2% of the time, Pallas kernels for 10%

profile of v9, /device:TPU:1, one launch (start us, length us, event | category | flops | bytes accessed | tf_op | source)
XLA Modules:
  0.0 182.9 jit_solution(9977381978034695724)
XLA Ops:
  0.6 7.1 %collective-permute-start = (bf16[128,512]{1,0:T(8,128)(2,1)}, bf16[128,512]{1,0:T(8,128)(2,1)S(1)}, u32[]{:S(2)}, u32[]{:S(2)}) collective-permute-start(bf16[128,512]{1,0:T(8,128)(2,1)} %param.9), channel_id=1, source_target_pairs={{0,3},{1,4},{2,5},{3,6},{4,7},{5,8},{6,9},{7,10},{8,11},{9,12},{10... | collective-permute-start | bytes 393224 | tf_op jit(solution)/shard_map/ppermute | solution.py:38
  7.7 6.1 %collective-permute-start.1 = (bf16[128,512]{1,0:T(8,128)(2,1)}, bf16[128,512]{1,0:T(8,128)(2,1)S(1)}, u32[]{:S(2)}, u32[]{:S(2)}) collective-permute-start(bf16[128,512]{1,0:T(8,128)(2,1)} %param.9), channel_id=1, source_target_pairs={{0,2},{1,3},{2,4},{3,5},{4,6},{5,7},{6,8},{7,9},{8,10},{9,11},{10,... | collective-permute-start | bytes 393224 | tf_op jit(solution)/shard_map/ppermute | solution.py:38
  13.9 3.5 %collective-permute-start.3 = (bf16[128,512]{1,0:T(8,128)(2,1)}, bf16[128,512]{1,0:T(8,128)(2,1)S(1)}, u32[]{:S(2)}, u32[]{:S(2)}) collective-permute-start(bf16[128,512]{1,0:T(8,128)(2,1)} %param.9), channel_id=1, source_target_pairs={{0,1},{1,2},{2,3},{3,4},{4,5},{5,6},{6,7},{7,8},{8,9},{9,10},{10,1... | collective-permute-start | bytes 393224 | tf_op jit(solution)/shard_map/ppermute | solution.py:38
  18.9 11.2 %all-to-all-start = ((bf16[32,16,128]{2,1,0:T(8,128)(2,1)}), bf16[32,16,128]{2,1,0:T(8,128)(2,1)S(1)}, u32[]{:S(2)}, u32[]{:S(2)}) async-start(bf16[32,16,128]{2,1,0:T(8,128)(2,1)} %broadcast_in_dim.28), calls=%async_computation | async-start | bytes 262144 | tf_op jit(solution)/shard_map/all_to_all | solution.py:42
  30.9 4.8 %collective-permute-start.2 = (bf16[256,512]{1,0:T(8,128)(2,1)S(1)}, bf16[256,512]{1,0:T(8,128)(2,1)}, u32[]{:S(2)}, u32[]{:S(2)}) collective-permute-start(bf16[256,512]{1,0:T(8,128)(2,1)S(1)} %constant_dynamic-update-slice_fusion.keys1_ref), channel_id=1, source_target_pairs={{0,2},{1,3},{2,4},{3,5},{4,6},{5,7},{6,8},{7,9},{8,10},{9,11},{10,... | collective-permute-start | bytes 786440 | tf_op jit(solution)/shard_map/ppermute | solution.py:38
  36.4 9.5 %all-to-all-done = bf16[32,16,128]{2,1,0:T(8,128)(2,1)S(1)} async-done(((bf16[32,16,128]{2,1,0:T(8,128)(2,1)}), bf16[32,16,128]{2,1,0:T(8,128)(2,1)S(1)}, u32[]{:S(2)}, u32[]{:S(2)}) %all-to-all-start) | async-done | bytes 131104 | tf_op jit(solution)/shard_map/all_to_all | solution.py:42
  47.0 9.5 %all-to-all-start.1 = ((bf16[16,8,4096]{2,1,0:T(8,128)(2,1)}), bf16[16,8,4096]{2,1,0:T(8,128)(2,1)S(1)}, u32[]{:S(2)}, u32[]{:S(2)}) async-start(bf16[16,8,4096]{2,1,0:T(8,128)(2,1)} %broadcast_in_dim.30), calls=%async_computation.1 | async-start | bytes 2097152 | tf_op jit(solution)/shard_map/all_to_all | solution.py:42
  56.6 1.3 collective-permute-start.4
  59.1 7.7 %score.1 = (bf16[256,4096]{1,0:T(8,128)(2,1)}, bf16[256,4096]{1,0:T(8,128)(2,1)}, bf16[256,4096]{1,0:T(8,128)(2,1)}, f32[8,4096]{1,0:T(8,128)}) custom-call(bf16[128,4096]{1,0:T(8,128)(2,1)} %query_ref.3, bf16[256,512]{1,0:T(8,128)(2,1)} %collective-permute-done.2.keys2_ref, bf16[256,512]{1,0:T(8,128)(2,1)} %copy-done.12, ...), custom_call_target="tpu_custom_call" | custom-call | flops 10000000000 | bytes 134217728 | tf_op jit(solution)/shard_map/score/pallas_call | solution.py:222
  66.7 6.8 %all-to-all-done.1 = bf16[16,8,4096]{2,1,0:T(8,128)(2,1)S(1)} async-done(((bf16[16,8,4096]{2,1,0:T(8,128)(2,1)}), bf16[16,8,4096]{2,1,0:T(8,128)(2,1)S(1)}, u32[]{:S(2)}, u32[]{:S(2)}) %all-to-all-start.1) | async-done | bytes 1048608 | tf_op jit(solution)/shard_map/all_to_all | solution.py:42
  74.4 1.4 collective-permute-start.5
  77.1 1.4 collective-permute-start.6
  78.6 2.1 %last_score.1 = (bf16[256,4096]{1,0:T(8,128)(2,1)S(1)}, f32[2,4096]{1,0:T(2,128)S(1)}) custom-call(bf16[128,4096]{1,0:T(8,128)(2,1)S(1)} %copy-done.3, bf16[256,512]{1,0:T(8,128)(2,1)S(1)} %collective-permute-done.4.keys_ref, f32[1024,128]{1,0:T(8,128)S(1)} %copy-done.1), custom_call_target="tpu_custom_call" | custom-call | flops 10000000000 | bytes 134217728 | tf_op jit(solution)/shard_map/last_score/pallas_call | solution.py:210
  80.7 1.3 far.1
  83.4 1.5 collective-permute-start.10
  84.9 1.3 near.1
  86.2 8.1 %collective-permute-done.7 = bf16[64,512]{1,0:T(8,128)(2,1)S(1)} collective-permute-done((bf16[64,512]{1,0:T(8,128)(2,1)S(1)}, bf16[64,512]{1,0:T(8,128)(2,1)S(1)}, u32[]{:S(2)}, u32[]{:S(2)}) %collective-permute-start.7) | collective-permute-done | bytes 65568 | tf_op jit(solution)/shard_map/ppermute | solution.py:38
  95.7 2.4 %mixed.2.up0_ref = f32[64,256]{1,0:T(8,128)S(1)} custom-call(bf16[256,4096]{1,0:T(8,128)(2,1)S(1)} %get-tuple-element.26.w3_ref, bf16[256,4096]{1,0:T(8,128)(2,1)S(1)} %copy-done.7, bf16[256,4096]{1,0:T(8,128)(2,1)S(1)} %copy-done.8, bf16[256,4096]{1,0:T(8,128)(2,1)S(1)} %copy-done.9, f32[4,4096]{1,0:T(4,128)S(1)} %get-tuple-element.31.scale_ref, ...), custom_call_target="tpu_custom_call" | custom-call | flops 10000000000 | bytes 134217728 | tf_op jit(solution)/shard_map/mixed/pallas_call | solution.py:210
  98.1 2.8 %collective-permute-done.8 = f32[64,256]{1,0:T(8,128)S(1)} collective-permute-done((f32[64,256]{1,0:T(8,128)S(1)}, f32[64,256]{1,0:T(8,128)S(1)}, u32[]{:S(2)}, u32[]{:S(2)}) %collective-permute-start.8) | collective-permute-done | bytes 65568 | tf_op jit(solution)/shard_map/ppermute | solution.py:38
  102.2 2.4 %mixed.3.up1_ref = f32[64,256]{1,0:T(8,128)S(1)} custom-call(bf16[256,4096]{1,0:T(8,128)(2,1)S(1)} %get-tuple-element.26.w3_ref, bf16[256,4096]{1,0:T(8,128)(2,1)S(1)} %copy-done.7, bf16[256,4096]{1,0:T(8,128)(2,1)S(1)} %copy-done.8, bf16[256,4096]{1,0:T(8,128)(2,1)S(1)} %copy-done.9, f32[4,4096]{1,0:T(4,128)S(1)} %get-tuple-element.31.scale_ref, ...), custom_call_target="tpu_custom_call" | custom-call | flops 10000000000 | bytes 134217728 | tf_op jit(solution)/shard_map/mixed/pallas_call | solution.py:210
  104.6 1.6 collective-permute-done.9
  106.7 29.6 %all_to_all.25.in_ref = bf16[16,8,4352]{2,1,0:T(8,128)(2,1)S(1)} all-to-all(bf16[16,8,4352]{2,1,0:T(8,128)(2,1)S(1)} %bitcast.15), channel_id=1, replica_groups=mesh['dp'=16,'fsdp'=32] {'dp'}, dimensions={0} | all-to-all | bytes 2228224 | tf_op jit(solution)/shard_map/all_to_all | solution.py:42
  136.4 33.7 %all_to_all.26.in_ref = bf16[32,8,384]{2,1,0:T(8,128)(2,1)S(1)} all-to-all(bf16[32,8,384]{2,1,0:T(8,128)(2,1)S(1)} %fold_dp.1), channel_id=1, replica_groups=mesh['dp'=16,'fsdp'=32] {'fsdp'}, dimensions={0} | all-to-all | bytes 393216 | tf_op jit(solution)/shard_map/all_to_all | solution.py:42
  170.2 12.0 %all_to_all.27.in_ref = f32[16,8,384]{2,1,0:T(8,128)S(1)} all-to-all(f32[16,8,384]{2,1,0:T(8,128)S(1)} %fold_fsdp.1), channel_id=1, replica_groups=mesh['dp'=16,'fsdp'=32] {'dp'}, dimensions={0} | all-to-all | bytes 393216 | tf_op jit(solution)/shard_map/all_to_all | solution.py:42
  (69 shorter events, 12.5 us)
Async XLA Ops:
  0.6 17.6 %copy-start = (bf16[256,64]{0,1:T(8,128)(2,1)S(1)}, bf16[256,64]{0,1:T(8,128)(2,1)}, u32[]{:S(2)}) copy-start(bf16[256,64]{0,1:T(8,128)(2,1)} %param.11) | copy-start | bytes 98308
  0.6 30.2 %collective-permute-start = (bf16[128,512]{1,0:T(8,128)(2,1)}, bf16[128,512]{1,0:T(8,128)(2,1)S(1)}, u32[]{:S(2)}, u32[]{:S(2)}) collective-permute-start(bf16[128,512]{1,0:T(8,128)(2,1)} %param.9), channel_id=1, source_target_pairs={{0,3},{1,4},{2,5},{3,6},{4,7},{5,8},{6,9},{7,10},{8,11},{9,12},{10... | collective-permute-start | bytes 393224 | tf_op jit(solution)/shard_map/ppermute | solution.py:38
  7.7 23.1 %collective-permute-start.1 = (bf16[128,512]{1,0:T(8,128)(2,1)}, bf16[128,512]{1,0:T(8,128)(2,1)S(1)}, u32[]{:S(2)}, u32[]{:S(2)}) collective-permute-start(bf16[128,512]{1,0:T(8,128)(2,1)} %param.9), channel_id=1, source_target_pairs={{0,2},{1,3},{2,4},{3,5},{4,6},{5,7},{6,8},{7,9},{8,10},{9,11},{10,... | collective-permute-start | bytes 393224 | tf_op jit(solution)/shard_map/ppermute | solution.py:38
  13.9 21.8 %collective-permute-start.3 = (bf16[128,512]{1,0:T(8,128)(2,1)}, bf16[128,512]{1,0:T(8,128)(2,1)S(1)}, u32[]{:S(2)}, u32[]{:S(2)}) collective-permute-start(bf16[128,512]{1,0:T(8,128)(2,1)} %param.9), channel_id=1, source_target_pairs={{0,1},{1,2},{2,3},{3,4},{4,5},{5,6},{6,7},{7,8},{8,9},{9,10},{10,1... | collective-permute-start | bytes 393224 | tf_op jit(solution)/shard_map/ppermute | solution.py:38
  18.9 27.0 %all-to-all-start = ((bf16[32,16,128]{2,1,0:T(8,128)(2,1)}), bf16[32,16,128]{2,1,0:T(8,128)(2,1)S(1)}, u32[]{:S(2)}, u32[]{:S(2)}) async-start(bf16[32,16,128]{2,1,0:T(8,128)(2,1)} %broadcast_in_dim.28), calls=%async_computation | async-start | bytes 262144 | tf_op jit(solution)/shard_map/all_to_all | solution.py:42
  30.8 4.8 %copy-start.11 = (bf16[128,512]{1,0:T(8,128)(2,1)S(1)}, bf16[128,512]{1,0:T(8,128)(2,1)}, u32[]{:S(2)}) copy-start(bf16[128,512]{1,0:T(8,128)(2,1)} %param.9) | copy-start | bytes 393220
  30.9 27.0 %copy-start.12 = (bf16[256,512]{1,0:T(8,128)(2,1)}, bf16[256,512]{1,0:T(8,128)(2,1)S(1)}, u32[]{:S(2)}) copy-start(bf16[256,512]{1,0:T(8,128)(2,1)S(1)} %constant_dynamic-update-slice_fusion.keys1_ref) | copy-start | bytes 786436
  30.9 25.6 %collective-permute-start.2 = (bf16[256,512]{1,0:T(8,128)(2,1)S(1)}, bf16[256,512]{1,0:T(8,128)(2,1)}, u32[]{:S(2)}, u32[]{:S(2)}) collective-permute-start(bf16[256,512]{1,0:T(8,128)(2,1)S(1)} %constant_dynamic-update-slice_fusion.keys1_ref), channel_id=1, source_target_pairs={{0,2},{1,3},{2,4},{3,5},{4,6},{5,7},{6,8},{7,9},{8,10},{9,11},{10,... | collective-permute-start | bytes 786440 | tf_op jit(solution)/shard_map/ppermute | solution.py:38
  47.0 26.6 %all-to-all-start.1 = ((bf16[16,8,4096]{2,1,0:T(8,128)(2,1)}), bf16[16,8,4096]{2,1,0:T(8,128)(2,1)S(1)}, u32[]{:S(2)}, u32[]{:S(2)}) async-start(bf16[16,8,4096]{2,1,0:T(8,128)(2,1)} %broadcast_in_dim.30), calls=%async_computation.1 | async-start | bytes 2097152 | tf_op jit(solution)/shard_map/all_to_all | solution.py:42
  56.6 20.5 %collective-permute-start.4 = (bf16[256,512]{1,0:T(8,128)(2,1)}, bf16[256,512]{1,0:T(8,128)(2,1)S(1)}, u32[]{:S(2)}, u32[]{:S(2)}) collective-permute-start(bf16[256,512]{1,0:T(8,128)(2,1)} %collective-permute-done.2.keys2_ref), channel_id=1, source_target_pairs={{0,2},{1,3},{2,4},{3,5},{4,6},{5,7},{6,8},{7,9},{8,10},{9,11},{10,... | collective-permute-start | bytes 786440 | tf_op jit(solution)/shard_map/ppermute | solution.py:38
  59.1 14.5 %copy-start.2 = (bf16[128,8192]{1,0:T(8,128)(2,1)S(1)}, bf16[128,8192]{1,0:T(8,128)(2,1)}, u32[]{:S(2)}) copy-start(bf16[128,8192]{1,0:T(8,128)(2,1)} %hidden_ref.3) | copy-start | bytes 6291460
  73.6 2.3 %copy-start.5 = (bf16[64,512]{1,0:T(8,128)(2,1)S(1)}, bf16[64,512]{1,0:T(8,128)(2,1)}, u32[]{:S(2)}) copy-start(bf16[64,512]{1,0:T(8,128)(2,1)} %up_ref) | copy-start | bytes 196612
  74.4 4.1 %copy-start.1 = (f32[1024,128]{1,0:T(8,128)S(1)}, f32[1024,128]{1,0:T(8,128)}, u32[]{:S(2)}) copy-start(f32[1024,128]{1,0:T(8,128)} %fusion.1.bias_ref) | copy-start | bytes 1572868
  74.4 4.1 %copy-start.3 = (bf16[128,4096]{1,0:T(8,128)(2,1)S(1)}, bf16[128,4096]{1,0:T(8,128)(2,1)}, u32[]{:S(2)}) copy-start(bf16[128,4096]{1,0:T(8,128)(2,1)} %query_ref.3) | copy-start | bytes 3145732
  74.4 2.6 %collective-permute-start.5 = (bf16[64,128]{1,0:T(8,128)(2,1)S(1)}, bf16[64,128]{1,0:T(8,128)(2,1)S(1)}, u32[]{:S(2)}, u32[]{:S(2)}) collective-permute-start(bf16[64,128]{1,0:T(8,128)(2,1)S(1)} %lowrank.1), channel_id=1, source_target_pairs={{0,4},{1,5},{2,6},{3,7},{4,8},{5,9},{6,10},{7,11},{8,12},{9,13},{1... | collective-permute-start | bytes 49160 | tf_op jit(solution)/shard_map/ppermute | solution.py:38
  77.1 3.6 %copy-start.7 = (bf16[256,4096]{1,0:T(8,128)(2,1)S(1)}, bf16[256,4096]{1,0:T(8,128)(2,1)}, u32[]{:S(2)}) copy-start(bf16[256,4096]{1,0:T(8,128)(2,1)} %get-tuple-element.27.w2_ref) | copy-start | bytes 6291460
  77.1 3.6 %copy-start.10 = (f32[8,4096]{1,0:T(8,128)S(1)}, f32[8,4096]{1,0:T(8,128)}, u32[]{:S(2)}) copy-start(f32[8,4096]{1,0:T(8,128)} %get-tuple-element.29.stats_ref) | copy-start | bytes 393220
  77.1 3.6 %collective-permute-start.6 = (bf16[64,256]{1,0:T(8,128)(2,1)S(1)}, bf16[64,256]{1,0:T(8,128)(2,1)S(1)}, u32[]{:S(2)}, u32[]{:S(2)}) collective-permute-start(bf16[64,256]{1,0:T(8,128)(2,1)S(1)} %pad_maximum_fusion.2), channel_id=1, source_target_pairs={{0,2},{1,3},{2,4},{3,5},{4,6},{5,7},{6,8},{7,9},{8,10},{9,11},{10,... | collective-permute-start | bytes 98312 | tf_op jit(solution)/shard_map/ppermute | solution.py:38
  80.7 4.1 %copy-start.8 = (bf16[256,4096]{1,0:T(8,128)(2,1)S(1)}, bf16[256,4096]{1,0:T(8,128)(2,1)}, u32[]{:S(2)}) copy-start(bf16[256,4096]{1,0:T(8,128)(2,1)} %get-tuple-element.20.w1_ref) | copy-start | bytes 6291460
  80.7 4.1 %copy-start.9 = (bf16[256,4096]{1,0:T(8,128)(2,1)S(1)}, bf16[256,4096]{1,0:T(8,128)(2,1)}, u32[]{:S(2)}) copy-start(bf16[256,4096]{1,0:T(8,128)(2,1)} %get-tuple-element.21.w0_ref) | copy-start | bytes 6291460
  82.1 12.2 %collective-permute-start.7 = (bf16[64,512]{1,0:T(8,128)(2,1)S(1)}, bf16[64,512]{1,0:T(8,128)(2,1)S(1)}, u32[]{:S(2)}, u32[]{:S(2)}) collective-permute-start(bf16[64,512]{1,0:T(8,128)(2,1)S(1)} %get-tuple-element.32), channel_id=1, source_target_pairs={{4,0},{5,1},{6,2},{7,3},{8,4},{9,5},{10,6},{11,7},{12,8},{13,9},{1... | collective-permute-start | bytes 196616 | tf_op jit(solution)/shard_map/ppermute | solution.py:38
  83.4 12.3 %collective-permute-start.10 = (bf16[64,512]{1,0:T(8,128)(2,1)S(1)}, bf16[64,512]{1,0:T(8,128)(2,1)S(1)}, u32[]{:S(2)}, u32[]{:S(2)}) collective-permute-start(bf16[64,512]{1,0:T(8,128)(2,1)S(1)} %pad_maximum_fusion.1), channel_id=1, source_target_pairs={{0,1},{1,2},{2,3},{3,4},{4,5},{5,6},{6,7},{7,8},{8,9},{9,10},{10,1... | collective-permute-start | bytes 196616 | tf_op jit(solution)/shard_map/ppermute | solution.py:38
  94.3 6.6 %collective-permute-start.8 = (f32[64,256]{1,0:T(8,128)S(1)}, f32[64,256]{1,0:T(8,128)S(1)}, u32[]{:S(2)}, u32[]{:S(2)}) collective-permute-start(f32[64,256]{1,0:T(8,128)S(1)} %slice.27), channel_id=1, source_target_pairs={{2,0},{3,1},{4,2},{5,3},{6,4},{7,5},{8,6},{9,7},{10,8},{11,9},{12,... | collective-permute-start | bytes 196616 | tf_op jit(solution)/shard_map/ppermute | solution.py:38
  100.9 5.3 %collective-permute-start.9 = (f32[64,128]{1,0:T(8,128)S(1)}, f32[64,128]{1,0:T(8,128)S(1)}, u32[]{:S(2)}, u32[]{:S(2)}) collective-permute-start(f32[64,128]{1,0:T(8,128)S(1)} %slice.29), channel_id=1, source_target_pairs={{1,0},{2,1},{3,2},{4,3},{5,4},{6,5},{7,6},{8,7},{9,8},{10,9},{11,1... | collective-permute-start | bytes 98312 | tf_op jit(solution)/shard_map/ppermute | solution.py:38
  (2 other events, 3.0 us)

commit v10 on v6

--- a/solution.py
+++ b/solution.py
@@ -316,7 +316,6 @@
         pair3,
         bias,
     )
-    w3, rank2 = lax.optimization_barrier((w3, rank2))
     far, scale = plain(
         far_kernel,
         "far",

time: 178 us -> 179 us (level)
  starting transfers between devices: 60.1 us -> 62.4 us
    ppermute x11, starting transfers between devices: 39.3 us -> 41.6 us  [from_behind(): return lax.ppermute(block, 'fsdp', route)]
  transfers between devices with their start and end apart: 13 -> 13, of which waited for: 4 -> 4; matrix products, arithmetic and copies ran while one was open for 3% -> 3% of each run, Pallas kernels for 10% -> 9%
where the time goes in v10:
time: 179 us; the launch traced here: 178 us
  blocking collectives  69.2 us (39%)
  starting transfers between devices  62.4 us (35%)
  Pallas kernels  20.5 us (11%)
  waiting for transfers between devices  20 us (11%)
  other arithmetic  2.71 us (2%)
  local copies, waits for them, and re-layouts  2.6 us (1%)
    all_to_all x3, blocking collectives, exchange(): return lax.all_to_all(slots, axis, 0, 0, tiled=True)  69.2 us
    ppermute x11, starting transfers between devices, from_behind(): return lax.ppermute(block, 'fsdp', route)  41.6 us
    all_to_all x2, starting transfers between devices, exchange(): return lax.all_to_all(slots, axis, 0, 0, tiled=True)  20.8 us
    all_to_all x2, waiting for transfers between devices, exchange(): return lax.all_to_all(slots, axis, 0, 0, tiled=True)  16.4 us
    pallas_call x12, Pallas kernels, plain(): pl.pallas_call(kernel, in_specs=whole(*arrays), out_specs=jax.tree.map(la...  12.8 us
    pallas_call x1, Pallas kernels, by_steps(): pl.pallas_call(kernel, grid=(steps,), in_specs=[spec for spec, _ in given...  7.66 us
    ppermute x11, waiting for transfers between devices, from_behind(): return lax.ppermute(block, 'fsdp', route)  3.65 us
  transfers between devices with their start and end apart: 13, of which 4 were waited for; matrix products, arithmetic and copies ran while one was open for 3% of the time, Pallas kernels for 9%

profile of v10, /device:TPU:1, one launch (start us, length us, event | category | flops | bytes accessed | tf_op | source)
XLA Modules:
  0.0 178.5 jit_solution(14794061073350462814)
XLA Ops:
  0.6 7.1 %collective-permute-start = (bf16[128,512]{1,0:T(8,128)(2,1)}, bf16[128,512]{1,0:T(8,128)(2,1)S(1)}, u32[]{:S(2)}, u32[]{:S(2)}) collective-permute-start(bf16[128,512]{1,0:T(8,128)(2,1)} %param.9), channel_id=1, source_target_pairs={{0,3},{1,4},{2,5},{3,6},{4,7},{5,8},{6,9},{7,10},{8,11},{9,12},{10... | collective-permute-start | bytes 393224 | tf_op jit(solution)/shard_map/ppermute | solution.py:38
  7.7 6.1 %collective-permute-start.1 = (bf16[128,512]{1,0:T(8,128)(2,1)}, bf16[128,512]{1,0:T(8,128)(2,1)S(1)}, u32[]{:S(2)}, u32[]{:S(2)}) collective-permute-start(bf16[128,512]{1,0:T(8,128)(2,1)} %param.9), channel_id=1, source_target_pairs={{0,2},{1,3},{2,4},{3,5},{4,6},{5,7},{6,8},{7,9},{8,10},{9,11},{10,... | collective-permute-start | bytes 393224 | tf_op jit(solution)/shard_map/ppermute | solution.py:38
  13.9 3.5 %collective-permute-start.3 = (bf16[128,512]{1,0:T(8,128)(2,1)}, bf16[128,512]{1,0:T(8,128)(2,1)S(1)}, u32[]{:S(2)}, u32[]{:S(2)}) collective-permute-start(bf16[128,512]{1,0:T(8,128)(2,1)} %param.9), channel_id=1, source_target_pairs={{0,1},{1,2},{2,3},{3,4},{4,5},{5,6},{6,7},{7,8},{8,9},{9,10},{10,1... | collective-permute-start | bytes 393224 | tf_op jit(solution)/shard_map/ppermute | solution.py:38
  18.9 11.2 %all-to-all-start = ((bf16[32,16,128]{2,1,0:T(8,128)(2,1)}), bf16[32,16,128]{2,1,0:T(8,128)(2,1)S(1)}, u32[]{:S(2)}, u32[]{:S(2)}) async-start(bf16[32,16,128]{2,1,0:T(8,128)(2,1)} %broadcast_in_dim.28), calls=%async_computation | async-start | bytes 262144 | tf_op jit(solution)/shard_map/all_to_all | solution.py:42
  30.9 4.8 %collective-permute-start.2 = (bf16[256,512]{1,0:T(8,128)(2,1)S(1)}, bf16[256,512]{1,0:T(8,128)(2,1)}, u32[]{:S(2)}, u32[]{:S(2)}) collective-permute-start(bf16[256,512]{1,0:T(8,128)(2,1)S(1)} %constant_dynamic-update-slice_fusion.keys1_ref), channel_id=1, source_target_pairs={{0,2},{1,3},{2,4},{3,5},{4,6},{5,7},{6,8},{7,9},{8,10},{9,11},{10,... | collective-permute-start | bytes 786440 | tf_op jit(solution)/shard_map/ppermute | solution.py:38
  36.4 9.5 %all-to-all-done = bf16[32,16,128]{2,1,0:T(8,128)(2,1)S(1)} async-done(((bf16[32,16,128]{2,1,0:T(8,128)(2,1)}), bf16[32,16,128]{2,1,0:T(8,128)(2,1)S(1)}, u32[]{:S(2)}, u32[]{:S(2)}) %all-to-all-start) | async-done | bytes 131104 | tf_op jit(solution)/shard_map/all_to_all | solution.py:42
  47.0 9.5 %all-to-all-start.1 = ((bf16[16,8,4096]{2,1,0:T(8,128)(2,1)}), bf16[16,8,4096]{2,1,0:T(8,128)(2,1)S(1)}, u32[]{:S(2)}, u32[]{:S(2)}) async-start(bf16[16,8,4096]{2,1,0:T(8,128)(2,1)} %broadcast_in_dim.30), calls=%async_computation.1 | async-start | bytes 2097152 | tf_op jit(solution)/shard_map/all_to_all | solution.py:42
  56.6 1.3 collective-permute-start.4
  59.1 7.7 %score.1 = (bf16[256,4096]{1,0:T(8,128)(2,1)}, bf16[256,4096]{1,0:T(8,128)(2,1)}, bf16[256,4096]{1,0:T(8,128)(2,1)}, f32[8,4096]{1,0:T(8,128)}) custom-call(bf16[128,4096]{1,0:T(8,128)(2,1)} %query_ref.3, bf16[256,512]{1,0:T(8,128)(2,1)} %collective-permute-done.2.keys2_ref, bf16[256,512]{1,0:T(8,128)(2,1)} %copy-done.12, ...), custom_call_target="tpu_custom_call" | custom-call | flops 10000000000 | bytes 134217728 | tf_op jit(solution)/shard_map/score/pallas_call | solution.py:219
  66.7 6.8 %all-to-all-done.1 = bf16[16,8,4096]{2,1,0:T(8,128)(2,1)S(1)} async-done(((bf16[16,8,4096]{2,1,0:T(8,128)(2,1)}), bf16[16,8,4096]{2,1,0:T(8,128)(2,1)S(1)}, u32[]{:S(2)}, u32[]{:S(2)}) %all-to-all-start.1) | async-done | bytes 1048608 | tf_op jit(solution)/shard_map/all_to_all | solution.py:42
  74.4 1.6 collective-permute-start.5
  77.3 2.1 %last_score.1 = (bf16[256,4096]{1,0:T(8,128)(2,1)S(1)}, f32[2,4096]{1,0:T(2,128)S(1)}) custom-call(bf16[128,4096]{1,0:T(8,128)(2,1)S(1)} %copy-done.3, bf16[256,512]{1,0:T(8,128)(2,1)S(1)} %collective-permute-done.4.keys_ref, f32[1024,128]{1,0:T(8,128)S(1)} %copy-done.1), custom_call_target="tpu_custom_call" | custom-call | flops 10000000000 | bytes 134217728 | tf_op jit(solution)/shard_map/last_score/pallas_call | solution.py:207
  79.5 1.3 far.1
  80.8 1.3 collective-permute-start.6
  82.1 3.0 %collective-permute-start.9 = (bf16[64,256]{1,0:T(8,128)(2,1)S(1)}, bf16[64,256]{1,0:T(8,128)(2,1)S(1)}, u32[]{:S(2)}, u32[]{:S(2)}) collective-permute-start(bf16[64,256]{1,0:T(8,128)(2,1)S(1)} %pad_maximum_fusion.2), channel_id=1, source_target_pairs={{0,2},{1,3},{2,4},{3,5},{4,6},{5,7},{6,8},{7,9},{8,10},{9,11},{10,... | collective-permute-start | bytes 98312 | tf_op jit(solution)/shard_map/ppermute | solution.py:38
  85.1 1.3 near.1
  86.5 10.3 %collective-permute-start.10 = (bf16[64,512]{1,0:T(8,128)(2,1)S(1)}, bf16[64,512]{1,0:T(8,128)(2,1)S(1)}, u32[]{:S(2)}, u32[]{:S(2)}) collective-permute-start(bf16[64,512]{1,0:T(8,128)(2,1)S(1)} %pad_maximum_fusion.1), channel_id=1, source_target_pairs={{0,4},{1,5},{2,6},{3,7},{4,8},{5,9},{6,10},{7,11},{8,12},{9,13},{1... | collective-permute-start | bytes 196616 | tf_op jit(solution)/shard_map/ppermute | solution.py:38
  98.2 2.4 %mixed.2.up0_ref = f32[64,256]{1,0:T(8,128)S(1)} custom-call(bf16[256,4096]{1,0:T(8,128)(2,1)S(1)} %get-tuple-element.22.w3_ref, bf16[256,4096]{1,0:T(8,128)(2,1)S(1)} %copy-done.7, bf16[256,4096]{1,0:T(8,128)(2,1)S(1)} %copy-done.8, bf16[256,4096]{1,0:T(8,128)(2,1)S(1)} %copy-done.9, f32[4,4096]{1,0:T(4,128)S(1)} %get-tuple-element.27.scale_ref, ...), custom_call_target="tpu_custom_call" | custom-call | flops 10000000000 | bytes 134217728 | tf_op jit(solution)/shard_map/mixed/pallas_call | solution.py:207
  100.6 2.2 %collective-permute-done.7 = f32[64,256]{1,0:T(8,128)S(1)} collective-permute-done((f32[64,256]{1,0:T(8,128)S(1)}, f32[64,256]{1,0:T(8,128)S(1)}, u32[]{:S(2)}, u32[]{:S(2)}) %collective-permute-start.7) | collective-permute-done | bytes 65568 | tf_op jit(solution)/shard_map/ppermute | solution.py:38
  104.1 2.4 %mixed.3.up1_ref = f32[64,256]{1,0:T(8,128)S(1)} custom-call(bf16[256,4096]{1,0:T(8,128)(2,1)S(1)} %get-tuple-element.22.w3_ref, bf16[256,4096]{1,0:T(8,128)(2,1)S(1)} %copy-done.7, bf16[256,4096]{1,0:T(8,128)(2,1)S(1)} %copy-done.8, bf16[256,4096]{1,0:T(8,128)(2,1)S(1)} %copy-done.9, f32[4,4096]{1,0:T(4,128)S(1)} %get-tuple-element.27.scale_ref, ...), custom_call_target="tpu_custom_call" | custom-call | flops 10000000000 | bytes 134217728 | tf_op jit(solution)/shard_map/mixed/pallas_call | solution.py:207
  106.5 1.5 collective-permute-done.8
  108.4 28.2 %all_to_all.25.in_ref = bf16[16,8,4352]{2,1,0:T(8,128)(2,1)S(1)} all-to-all(bf16[16,8,4352]{2,1,0:T(8,128)(2,1)S(1)} %bitcast.15), channel_id=1, replica_groups=mesh['dp'=16,'fsdp'=32] {'dp'}, dimensions={0} | all-to-all | bytes 2228224 | tf_op jit(solution)/shard_map/all_to_all | solution.py:42
  136.7 29.0 %all_to_all.26.in_ref = bf16[32,8,384]{2,1,0:T(8,128)(2,1)S(1)} all-to-all(bf16[32,8,384]{2,1,0:T(8,128)(2,1)S(1)} %fold_dp.1), channel_id=1, replica_groups=mesh['dp'=16,'fsdp'=32] {'fsdp'}, dimensions={0} | all-to-all | bytes 393216 | tf_op jit(solution)/shard_map/all_to_all | solution.py:42
  165.7 12.0 %all_to_all.27.in_ref = f32[16,8,384]{2,1,0:T(8,128)S(1)} all-to-all(f32[16,8,384]{2,1,0:T(8,128)S(1)} %fold_fsdp.1), channel_id=1, replica_groups=mesh['dp'=16,'fsdp'=32] {'dp'}, dimensions={0} | all-to-all | bytes 393216 | tf_op jit(solution)/shard_map/all_to_all | solution.py:42
  (70 shorter events, 11.2 us)
Async XLA Ops:
  0.6 17.6 %copy-start = (bf16[256,64]{0,1:T(8,128)(2,1)S(1)}, bf16[256,64]{0,1:T(8,128)(2,1)}, u32[]{:S(2)}) copy-start(bf16[256,64]{0,1:T(8,128)(2,1)} %param.11) | copy-start | bytes 98308
  0.6 30.2 %collective-permute-start = (bf16[128,512]{1,0:T(8,128)(2,1)}, bf16[128,512]{1,0:T(8,128)(2,1)S(1)}, u32[]{:S(2)}, u32[]{:S(2)}) collective-permute-start(bf16[128,512]{1,0:T(8,128)(2,1)} %param.9), channel_id=1, source_target_pairs={{0,3},{1,4},{2,5},{3,6},{4,7},{5,8},{6,9},{7,10},{8,11},{9,12},{10... | collective-permute-start | bytes 393224 | tf_op jit(solution)/shard_map/ppermute | solution.py:38
  7.7 23.1 %collective-permute-start.1 = (bf16[128,512]{1,0:T(8,128)(2,1)}, bf16[128,512]{1,0:T(8,128)(2,1)S(1)}, u32[]{:S(2)}, u32[]{:S(2)}) collective-permute-start(bf16[128,512]{1,0:T(8,128)(2,1)} %param.9), channel_id=1, source_target_pairs={{0,2},{1,3},{2,4},{3,5},{4,6},{5,7},{6,8},{7,9},{8,10},{9,11},{10,... | collective-permute-start | bytes 393224 | tf_op jit(solution)/shard_map/ppermute | solution.py:38
  13.9 21.8 %collective-permute-start.3 = (bf16[128,512]{1,0:T(8,128)(2,1)}, bf16[128,512]{1,0:T(8,128)(2,1)S(1)}, u32[]{:S(2)}, u32[]{:S(2)}) collective-permute-start(bf16[128,512]{1,0:T(8,128)(2,1)} %param.9), channel_id=1, source_target_pairs={{0,1},{1,2},{2,3},{3,4},{4,5},{5,6},{6,7},{7,8},{8,9},{9,10},{10,1... | collective-permute-start | bytes 393224 | tf_op jit(solution)/shard_map/ppermute | solution.py:38
  18.9 27.0 %all-to-all-start = ((bf16[32,16,128]{2,1,0:T(8,128)(2,1)}), bf16[32,16,128]{2,1,0:T(8,128)(2,1)S(1)}, u32[]{:S(2)}, u32[]{:S(2)}) async-start(bf16[32,16,128]{2,1,0:T(8,128)(2,1)} %broadcast_in_dim.28), calls=%async_computation | async-start | bytes 262144 | tf_op jit(solution)/shard_map/all_to_all | solution.py:42
  30.8 4.8 %copy-start.11 = (bf16[128,512]{1,0:T(8,128)(2,1)S(1)}, bf16[128,512]{1,0:T(8,128)(2,1)}, u32[]{:S(2)}) copy-start(bf16[128,512]{1,0:T(8,128)(2,1)} %param.9) | copy-start | bytes 393220
  30.9 27.0 %copy-start.12 = (bf16[256,512]{1,0:T(8,128)(2,1)}, bf16[256,512]{1,0:T(8,128)(2,1)S(1)}, u32[]{:S(2)}) copy-start(bf16[256,512]{1,0:T(8,128)(2,1)S(1)} %constant_dynamic-update-slice_fusion.keys1_ref) | copy-start | bytes 786436
  30.9 25.6 %collective-permute-start.2 = (bf16[256,512]{1,0:T(8,128)(2,1)S(1)}, bf16[256,512]{1,0:T(8,128)(2,1)}, u32[]{:S(2)}, u32[]{:S(2)}) collective-permute-start(bf16[256,512]{1,0:T(8,128)(2,1)S(1)} %constant_dynamic-update-slice_fusion.keys1_ref), channel_id=1, source_target_pairs={{0,2},{1,3},{2,4},{3,5},{4,6},{5,7},{6,8},{7,9},{8,10},{9,11},{10,... | collective-permute-start | bytes 786440 | tf_op jit(solution)/shard_map/ppermute | solution.py:38
  47.0 26.6 %all-to-all-start.1 = ((bf16[16,8,4096]{2,1,0:T(8,128)(2,1)}), bf16[16,8,4096]{2,1,0:T(8,128)(2,1)S(1)}, u32[]{:S(2)}, u32[]{:S(2)}) async-start(bf16[16,8,4096]{2,1,0:T(8,128)(2,1)} %broadcast_in_dim.30), calls=%async_computation.1 | async-start | bytes 2097152 | tf_op jit(solution)/shard_map/all_to_all | solution.py:42
  56.6 20.7 %collective-permute-start.4 = (bf16[256,512]{1,0:T(8,128)(2,1)}, bf16[256,512]{1,0:T(8,128)(2,1)S(1)}, u32[]{:S(2)}, u32[]{:S(2)}) collective-permute-start(bf16[256,512]{1,0:T(8,128)(2,1)} %collective-permute-done.2.keys2_ref), channel_id=1, source_target_pairs={{0,2},{1,3},{2,4},{3,5},{4,6},{5,7},{6,8},{7,9},{8,10},{9,11},{10,... | collective-permute-start | bytes 786440 | tf_op jit(solution)/shard_map/ppermute | solution.py:38
  59.1 14.5 %copy-start.2 = (bf16[128,8192]{1,0:T(8,128)(2,1)S(1)}, bf16[128,8192]{1,0:T(8,128)(2,1)}, u32[]{:S(2)}) copy-start(bf16[128,8192]{1,0:T(8,128)(2,1)} %hidden_ref.3) | copy-start | bytes 6291460
  73.6 2.5 %copy-start.4 = (bf16[128,4096]{1,0:T(8,128)(2,1)S(1)}, bf16[128,4096]{1,0:T(8,128)(2,1)}, u32[]{:S(2)}) copy-start(bf16[128,4096]{1,0:T(8,128)(2,1)} %gradient_ref.5) | copy-start | bytes 3145732
  73.6 2.5 %copy-start.5 = (bf16[64,512]{1,0:T(8,128)(2,1)S(1)}, bf16[64,512]{1,0:T(8,128)(2,1)}, u32[]{:S(2)}) copy-start(bf16[64,512]{1,0:T(8,128)(2,1)} %up_ref) | copy-start | bytes 196612
  74.4 2.9 %copy-start.1 = (f32[1024,128]{1,0:T(8,128)S(1)}, f32[1024,128]{1,0:T(8,128)}, u32[]{:S(2)}) copy-start(f32[1024,128]{1,0:T(8,128)} %fusion.1.bias_ref) | copy-start | bytes 1572868
  74.4 2.9 %copy-start.3 = (bf16[128,4096]{1,0:T(8,128)(2,1)S(1)}, bf16[128,4096]{1,0:T(8,128)(2,1)}, u32[]{:S(2)}) copy-start(bf16[128,4096]{1,0:T(8,128)(2,1)} %query_ref.3) | copy-start | bytes 3145732
  74.4 2.8 %collective-permute-start.5 = (bf16[64,128]{1,0:T(8,128)(2,1)S(1)}, bf16[64,128]{1,0:T(8,128)(2,1)S(1)}, u32[]{:S(2)}, u32[]{:S(2)}) collective-permute-start(bf16[64,128]{1,0:T(8,128)(2,1)S(1)} %lowrank.1), channel_id=1, source_target_pairs={{0,1},{1,2},{2,3},{3,4},{4,5},{5,6},{6,7},{7,8},{8,9},{9,10},{10,1... | collective-permute-start | bytes 49160 | tf_op jit(solution)/shard_map/ppermute | solution.py:38
  77.2 2.2 %copy-start.7 = (bf16[256,4096]{1,0:T(8,128)(2,1)S(1)}, bf16[256,4096]{1,0:T(8,128)(2,1)}, u32[]{:S(2)}) copy-start(bf16[256,4096]{1,0:T(8,128)(2,1)} %get-tuple-element.23.w2_ref) | copy-start | bytes 6291460
  79.4 5.7 %copy-start.8 = (bf16[256,4096]{1,0:T(8,128)(2,1)S(1)}, bf16[256,4096]{1,0:T(8,128)(2,1)}, u32[]{:S(2)}) copy-start(bf16[256,4096]{1,0:T(8,128)(2,1)} %get-tuple-element.18.w1_ref) | copy-start | bytes 6291460
  79.5 5.7 %copy-start.9 = (bf16[256,4096]{1,0:T(8,128)(2,1)S(1)}, bf16[256,4096]{1,0:T(8,128)(2,1)}, u32[]{:S(2)}) copy-start(bf16[256,4096]{1,0:T(8,128)(2,1)} %get-tuple-element.19.w0_ref) | copy-start | bytes 6291460
  80.8 16.0 %collective-permute-start.6 = (bf16[64,512]{1,0:T(8,128)(2,1)S(1)}, bf16[64,512]{1,0:T(8,128)(2,1)S(1)}, u32[]{:S(2)}, u32[]{:S(2)}) collective-permute-start(bf16[64,512]{1,0:T(8,128)(2,1)S(1)} %get-tuple-element.28), channel_id=1, source_target_pairs={{4,0},{5,1},{6,2},{7,3},{8,4},{9,5},{10,6},{11,7},{12,8},{13,9},{1... | collective-permute-start | bytes 196616 | tf_op jit(solution)/shard_map/ppermute | solution.py:38
  82.1 4.3 %collective-permute-start.9 = (bf16[64,256]{1,0:T(8,128)(2,1)S(1)}, bf16[64,256]{1,0:T(8,128)(2,1)S(1)}, u32[]{:S(2)}, u32[]{:S(2)}) collective-permute-start(bf16[64,256]{1,0:T(8,128)(2,1)S(1)} %pad_maximum_fusion.2), channel_id=1, source_target_pairs={{0,2},{1,3},{2,4},{3,5},{4,6},{5,7},{6,8},{7,9},{8,10},{9,11},{10,... | collective-permute-start | bytes 98312 | tf_op jit(solution)/shard_map/ppermute | solution.py:38
  86.5 11.7 %collective-permute-start.10 = (bf16[64,512]{1,0:T(8,128)(2,1)S(1)}, bf16[64,512]{1,0:T(8,128)(2,1)S(1)}, u32[]{:S(2)}, u32[]{:S(2)}) collective-permute-start(bf16[64,512]{1,0:T(8,128)(2,1)S(1)} %pad_maximum_fusion.1), channel_id=1, source_target_pairs={{0,4},{1,5},{2,6},{3,7},{4,8},{5,9},{6,10},{7,11},{8,12},{9,13},{1... | collective-permute-start | bytes 196616 | tf_op jit(solution)/shard_map/ppermute | solution.py:38
  96.8 5.9 %collective-permute-start.7 = (f32[64,256]{1,0:T(8,128)S(1)}, f32[64,256]{1,0:T(8,128)S(1)}, u32[]{:S(2)}, u32[]{:S(2)}) collective-permute-start(f32[64,256]{1,0:T(8,128)S(1)} %slice.27), channel_id=1, source_target_pairs={{2,0},{3,1},{4,2},{5,3},{6,4},{7,5},{8,6},{9,7},{10,8},{11,9},{12,... | collective-permute-start | bytes 196616 | tf_op jit(solution)/shard_map/ppermute | solution.py:38
  102.8 5.2 %collective-permute-start.8 = (f32[64,128]{1,0:T(8,128)S(1)}, f32[64,128]{1,0:T(8,128)S(1)}, u32[]{:S(2)}, u32[]{:S(2)}) collective-permute-start(f32[64,128]{1,0:T(8,128)S(1)} %slice.29), channel_id=1, source_target_pairs={{1,0},{2,1},{3,2},{4,3},{5,4},{6,5},{7,6},{8,7},{9,8},{10,9},{11,1... | collective-permute-start | bytes 98312 | tf_op jit(solution)/shard_map/ppermute | solution.py:38
  (2 other events, 2.8 us)

commit v11 on v5

--- a/solution.py
+++ b/solution.py
@@ -40,6 +40,10 @@
 
 def exchange(slots, axis):
     return lax.all_to_all(slots, axis, 0, 0, tiled=True)
+
+
+def docs_kernel(in_ref, out_ref):
+    out_ref[...] = in_ref[...]
 
 
 def lowrank_kernel(weight_ref, hidden_ref, out_ref):
@@ -253,8 +257,17 @@
 
     keys1, keys2, keys3 = [from_behind(keys, distance) for distance in (1, 2, 3)]
     weight_slice = lax.dynamic_slice(adapter_down_weight.T, (part * 8, half * 128), (8, 128))
-    docs_row = document_numbers.reshape(1, TOKENS).astype(BF16)
-    slot = jnp.concatenate([weight_slice, docs_row, jnp.zeros((7, 128), BF16)], axis=0)
+    slot = jnp.concatenate(
+        [
+            weight_slice,
+            document_numbers.reshape(1, TOKENS).astype(BF16),
+            jnp.zeros((7, 128), BF16),
+        ],
+        axis=0,
+    )
+    docs_row = plain(
+        docs_kernel, "docs", jax.ShapeDtypeStruct((1, TOKENS), jnp.int32), document_numbers
+    )
     slots = jnp.broadcast_to(slot[None], (N_FSDP, 16, 128))
     row_parts = exchange(slots, "fsdp")
     pair0 = jnp.concatenate([keys1, keys], axis=0)
@@ -269,7 +282,7 @@
 
     padded = jnp.concatenate([jnp.full((SPAN - 1, TOKENS), -1, jnp.int32), docs], axis=0)
     window_docs = lax.dynamic_slice(padded, (position, 0), (SPAN, TOKENS)).reshape(WINDOW)
-    own_docs = document_numbers.reshape(TOKENS)
+    own_docs = docs_row[0]
     key_pos = jnp.arange(WINDOW, dtype=jnp.int32) - (SPAN - 1) * TOKENS
     visible = (window_docs[:, None] == own_docs[None, :]) & (
         key_pos[:, None] <= jnp.arange(TOKENS, dtype=jnp.int32)[None, :]
@@ -312,7 +325,7 @@
         (weights_shape, jax.ShapeDtypeStruct((2, columns_of), F32)),
         queries,
         pair3,
-        bias[:256],
+        bias,
     )
     w3, rank2 = lax.optimization_barrier((w3, rank2))
     far, scale = plain(

time: 189 us -> 176 us (0.931)
  starting transfers between devices: 79.3 us -> 68 us
  blocking collectives: 65 us -> 57.7 us
  waiting for transfers between devices: 15.5 us -> 22.2 us
    all_to_all x2, waiting for transfers between devices: 5.79 us -> 16.4 us  [exchange(): return lax.all_to_all(slots, axis, 0, 0, tiled=True)]
    ppermute x11, starting transfers between devices: 47.8 us -> 39.3 us  [from_behind(): return lax.ppermute(block, 'fsdp', route)]
    all_to_all x2, blocking collectives: 49.9 us -> 42.9 us  [exchange(): return lax.all_to_all(slots, axis, 0, 0, tiled=True)]
    all_to_all x2, starting transfers between devices: 24.9 us -> 20.8 us  [exchange(): return lax.all_to_all(slots, axis, 0, 0, tiled=True)]
    ppermute x11, waiting for transfers between devices: 7.31 us -> 3.43 us  [from_behind(): return lax.ppermute(block, 'fsdp', route)]
    pallas_call x11 -> x12, Pallas kernels: 12.4 us -> 12.4 us  [plain(): pl.pallas_call(kernel, in_specs=whole(*arrays), out_specs=jax.tree.map(la...]
where the time goes in v11:
time: 176 us; the launch traced here: 175 us
  starting transfers between devices  68 us (39%)
  blocking collectives  57.7 us (33%)
  waiting for transfers between devices  22.2 us (13%)
  Pallas kernels  20.5 us (12%)
  other arithmetic  2.71 us (2%)
  local copies, waits for them, and re-layouts  2.59 us (1%)
    all_to_all x2, blocking collectives, exchange(): return lax.all_to_all(slots, axis, 0, 0, tiled=True)  42.9 us
    ppermute x11, starting transfers between devices, from_behind(): return lax.ppermute(block, 'fsdp', route)  39.3 us
    all_to_all x2, starting transfers between devices, exchange(): return lax.all_to_all(slots, axis, 0, 0, tiled=True)  20.8 us
    all_to_all x2, waiting for transfers between devices, exchange(): return lax.all_to_all(slots, axis, 0, 0, tiled=True)  16.4 us
    all_to_all x1, blocking collectives, local(): lax.all_to_all(shares, 'dp', 0, 0, axis_index_groups=groups, tiled=True)  14.7 us
    pallas_call x12, Pallas kernels, plain(): pl.pallas_call(kernel, in_specs=whole(*arrays), out_specs=jax.tree.map(la...  12.4 us
    ppermute x1, starting transfers between devices, local(): other = lax.ppermute(other, 'dp', [(d, d ^ 1) for d in range(N_DP)])  7.93 us
    pallas_call x1, Pallas kernels, by_steps(): pl.pallas_call(kernel, grid=(steps,), in_specs=[spec for spec, _ in given...  7.64 us
  transfers between devices with their start and end apart: 14, of which 5 were waited for; matrix products, arithmetic and copies ran while one was open for 3% of the time, Pallas kernels for 10%

profile of v11, /device:TPU:1, one launch (start us, length us, event | category | flops | bytes accessed | tf_op | source)
XLA Modules:
  0.0 174.7 jit_solution(3246101827963325745)
XLA Ops:
  0.6 7.1 %collective-permute-start = (bf16[128,512]{1,0:T(8,128)(2,1)}, bf16[128,512]{1,0:T(8,128)(2,1)S(1)}, u32[]{:S(2)}, u32[]{:S(2)}) collective-permute-start(bf16[128,512]{1,0:T(8,128)(2,1)} %param.9), channel_id=1, source_target_pairs={{0,3},{1,4},{2,5},{3,6},{4,7},{5,8},{6,9},{7,10},{8,11},{9,12},{10... | collective-permute-start | bytes 393224 | tf_op jit(solution)/shard_map/ppermute | solution.py:38
  7.7 6.1 %collective-permute-start.1 = (bf16[128,512]{1,0:T(8,128)(2,1)}, bf16[128,512]{1,0:T(8,128)(2,1)S(1)}, u32[]{:S(2)}, u32[]{:S(2)}) collective-permute-start(bf16[128,512]{1,0:T(8,128)(2,1)} %param.9), channel_id=1, source_target_pairs={{0,2},{1,3},{2,4},{3,5},{4,6},{5,7},{6,8},{7,9},{8,10},{9,11},{10,... | collective-permute-start | bytes 393224 | tf_op jit(solution)/shard_map/ppermute | solution.py:38
  13.9 3.5 %collective-permute-start.3 = (bf16[128,512]{1,0:T(8,128)(2,1)}, bf16[128,512]{1,0:T(8,128)(2,1)S(1)}, u32[]{:S(2)}, u32[]{:S(2)}) collective-permute-start(bf16[128,512]{1,0:T(8,128)(2,1)} %param.9), channel_id=1, source_target_pairs={{0,1},{1,2},{2,3},{3,4},{4,5},{5,6},{6,7},{7,8},{8,9},{9,10},{10,1... | collective-permute-start | bytes 393224 | tf_op jit(solution)/shard_map/ppermute | solution.py:38
  18.9 11.2 %all-to-all-start = ((bf16[32,16,128]{2,1,0:T(8,128)(2,1)}), bf16[32,16,128]{2,1,0:T(8,128)(2,1)S(1)}, u32[]{:S(2)}, u32[]{:S(2)}) async-start(bf16[32,16,128]{2,1,0:T(8,128)(2,1)} %broadcast_in_dim.28), calls=%async_computation | async-start | bytes 262144 | tf_op jit(solution)/shard_map/all_to_all | solution.py:42
  30.9 4.8 %collective-permute-start.2 = (bf16[256,512]{1,0:T(8,128)(2,1)S(1)}, bf16[256,512]{1,0:T(8,128)(2,1)}, u32[]{:S(2)}, u32[]{:S(2)}) collective-permute-start(bf16[256,512]{1,0:T(8,128)(2,1)S(1)} %constant_dynamic-update-slice_fusion.keys1_ref), channel_id=1, source_target_pairs={{0,2},{1,3},{2,4},{3,5},{4,6},{5,7},{6,8},{7,9},{8,10},{9,11},{10,... | collective-permute-start | bytes 786440 | tf_op jit(solution)/shard_map/ppermute | solution.py:38
  36.4 9.5 %all-to-all-done = bf16[32,16,128]{2,1,0:T(8,128)(2,1)S(1)} async-done(((bf16[32,16,128]{2,1,0:T(8,128)(2,1)}), bf16[32,16,128]{2,1,0:T(8,128)(2,1)S(1)}, u32[]{:S(2)}, u32[]{:S(2)}) %all-to-all-start) | async-done | bytes 131104 | tf_op jit(solution)/shard_map/all_to_all | solution.py:42
  47.0 9.5 %all-to-all-start.1 = ((bf16[16,8,4096]{2,1,0:T(8,128)(2,1)}), bf16[16,8,4096]{2,1,0:T(8,128)(2,1)S(1)}, u32[]{:S(2)}, u32[]{:S(2)}) async-start(bf16[16,8,4096]{2,1,0:T(8,128)(2,1)} %broadcast_in_dim.30), calls=%async_computation.1 | async-start | bytes 2097152 | tf_op jit(solution)/shard_map/all_to_all | solution.py:42
  56.6 1.3 collective-permute-start.4
  59.1 7.6 %score.1 = (bf16[256,4096]{1,0:T(8,128)(2,1)}, bf16[256,4096]{1,0:T(8,128)(2,1)}, bf16[256,4096]{1,0:T(8,128)(2,1)}, f32[8,4096]{1,0:T(8,128)}) custom-call(bf16[128,4096]{1,0:T(8,128)(2,1)} %query_ref.3, bf16[256,512]{1,0:T(8,128)(2,1)} %collective-permute-done.2.keys2_ref, bf16[256,512]{1,0:T(8,128)(2,1)} %copy-done.12, ...), custom_call_target="tpu_custom_call" | custom-call | flops 10000000000 | bytes 134217728 | tf_op jit(solution)/shard_map/score/pallas_call | solution.py:230
  66.7 6.8 %all-to-all-done.1 = bf16[16,8,4096]{2,1,0:T(8,128)(2,1)S(1)} async-done(((bf16[16,8,4096]{2,1,0:T(8,128)(2,1)}), bf16[16,8,4096]{2,1,0:T(8,128)(2,1)S(1)}, u32[]{:S(2)}, u32[]{:S(2)}) %all-to-all-start.1) | async-done | bytes 1048608 | tf_op jit(solution)/shard_map/all_to_all | solution.py:42
  74.4 1.6 collective-permute-start.5
  77.3 3.1 %collective-permute-start.6 = (bf16[64,256]{1,0:T(8,128)(2,1)S(1)}, bf16[64,256]{1,0:T(8,128)(2,1)S(1)}, u32[]{:S(2)}, u32[]{:S(2)}) collective-permute-start(bf16[64,256]{1,0:T(8,128)(2,1)S(1)} %pad_maximum_fusion.2), channel_id=1, source_target_pairs={{0,2},{1,3},{2,4},{3,5},{4,6},{5,7},{6,8},{7,9},{8,10},{9,11},{10,... | collective-permute-start | bytes 98312 | tf_op jit(solution)/shard_map/ppermute | solution.py:38
  80.4 2.1 %last_score.1 = (bf16[256,4096]{1,0:T(8,128)(2,1)S(1)}, f32[2,4096]{1,0:T(2,128)S(1)}) custom-call(bf16[128,4096]{1,0:T(8,128)(2,1)S(1)} %copy-done.3, bf16[256,512]{1,0:T(8,128)(2,1)S(1)} %collective-permute-done.4.keys_ref, f32[1024,128]{1,0:T(8,128)S(1)} %copy-done.1), custom_call_target="tpu_custom_call" | custom-call | flops 10000000000 | bytes 134217728 | tf_op jit(solution)/shard_map/last_score/pallas_call | solution.py:218
  82.6 1.3 far.1
  85.3 7.9 %collective-permute-start.10 = (bf16[64,512]{1,0:T(8,128)(2,1)S(1)}, bf16[64,512]{1,0:T(8,128)(2,1)S(1)}, u32[]{:S(2)}, u32[]{:S(2)}) collective-permute-start(bf16[64,512]{1,0:T(8,128)(2,1)S(1)} %pad_maximum_fusion.1), channel_id=1, source_target_pairs={{0,4},{1,5},{2,6},{3,7},{4,8},{5,9},{6,10},{7,11},{8,12},{9,13},{1... | collective-permute-start | bytes 196616 | tf_op jit(solution)/shard_map/ppermute | solution.py:38
  93.2 1.3 near.1
  95.9 2.4 %mixed.2.up0_ref = f32[64,256]{1,0:T(8,128)S(1)} custom-call(bf16[256,4096]{1,0:T(8,128)(2,1)S(1)} %get-tuple-element.28.w3_ref, bf16[256,4096]{1,0:T(8,128)(2,1)S(1)} %copy-done.7, bf16[256,4096]{1,0:T(8,128)(2,1)S(1)} %copy-done.8, bf16[256,4096]{1,0:T(8,128)(2,1)S(1)} %copy-done.9, f32[4,4096]{1,0:T(4,128)S(1)} %get-tuple-element.33.scale_ref, ...), custom_call_target="tpu_custom_call" | custom-call | flops 10000000000 | bytes 134217728 | tf_op jit(solution)/shard_map/mixed/pallas_call | solution.py:218
  98.3 2.4 %collective-permute-done.8 = f32[64,256]{1,0:T(8,128)S(1)} collective-permute-done((f32[64,256]{1,0:T(8,128)S(1)}, f32[64,256]{1,0:T(8,128)S(1)}, u32[]{:S(2)}, u32[]{:S(2)}) %collective-permute-start.8) | collective-permute-done | bytes 65568 | tf_op jit(solution)/shard_map/ppermute | solution.py:38
  102.1 2.4 %mixed.3.up1_ref = f32[64,256]{1,0:T(8,128)S(1)} custom-call(bf16[256,4096]{1,0:T(8,128)(2,1)S(1)} %get-tuple-element.28.w3_ref, bf16[256,4096]{1,0:T(8,128)(2,1)S(1)} %copy-done.7, bf16[256,4096]{1,0:T(8,128)(2,1)S(1)} %copy-done.8, bf16[256,4096]{1,0:T(8,128)(2,1)S(1)} %copy-done.9, f32[4,4096]{1,0:T(4,128)S(1)} %get-tuple-element.33.scale_ref, ...), custom_call_target="tpu_custom_call" | custom-call | flops 10000000000 | bytes 134217728 | tf_op jit(solution)/shard_map/mixed/pallas_call | solution.py:218
  105.9 7.9 %collective-permute-start.11 = (f32[64,4352]{1,0:T(8,128)S(1)}, f32[64,4352]{1,0:T(8,128)S(1)}, u32[]{:S(2)}, u32[]{:S(2)}) collective-permute-start(f32[64,4352]{1,0:T(8,128)S(1)} %get-tuple-element.37), channel_id=1, source_target_pairs={{0,32},{32,0},{64,96},{96,64},{128,160},{160,128},{192,224},{224,1... | collective-permute-start | bytes 3342344 | tf_op jit(solution)/shard_map/ppermute | solution.py:386
  113.8 2.4 %collective-permute-done.11.other_ref = f32[64,4352]{1,0:T(8,128)S(1)} collective-permute-done((f32[64,4352]{1,0:T(8,128)S(1)}, f32[64,4352]{1,0:T(8,128)S(1)}, u32[]{:S(2)}, u32[]{:S(2)}) %collective-permute-start.11) | collective-permute-done | bytes 1114144 | tf_op jit(solution)/shard_map/ppermute | solution.py:386
  116.3 14.7 %all_to_all.25.in_ref = bf16[8,8,4352]{2,1,0:T(8,128)(2,1)S(1)} all-to-all(bf16[8,8,4352]{2,1,0:T(8,128)(2,1)S(1)} %add.47), channel_id=1, replica_groups={{0,64,128,192,256,320,384,448},{32,96,160,224,288,352,416,480},{1,65,12..., dimensions={0} | all-to-all | bytes 1114112 | tf_op jit(solution)/shard_map/all_to_all | solution.py:391
  131.1 29.2 %all_to_all.26.in_ref = bf16[32,8,384]{2,1,0:T(8,128)(2,1)S(1)} all-to-all(bf16[32,8,384]{2,1,0:T(8,128)(2,1)S(1)} %fold_dp.1), channel_id=1, replica_groups=mesh['dp'=16,'fsdp'=32] {'fsdp'}, dimensions={0} | all-to-all | bytes 393216 | tf_op jit(solution)/shard_map/all_to_all | solution.py:42
  160.3 13.8 %all_to_all.27.in_ref = f32[16,8,384]{2,1,0:T(8,128)S(1)} all-to-all(f32[16,8,384]{2,1,0:T(8,128)S(1)} %fold_fsdp.1), channel_id=1, replica_groups=mesh['dp'=16,'fsdp'=32] {'dp'}, dimensions={0} | all-to-all | bytes 393216 | tf_op jit(solution)/shard_map/all_to_all | solution.py:42
  (72 shorter events, 13.5 us)
Async XLA Ops:
  0.6 17.6 %copy-start = (bf16[256,64]{0,1:T(8,128)(2,1)S(1)}, bf16[256,64]{0,1:T(8,128)(2,1)}, u32[]{:S(2)}) copy-start(bf16[256,64]{0,1:T(8,128)(2,1)} %param.11) | copy-start | bytes 98308
  0.6 30.2 %collective-permute-start = (bf16[128,512]{1,0:T(8,128)(2,1)}, bf16[128,512]{1,0:T(8,128)(2,1)S(1)}, u32[]{:S(2)}, u32[]{:S(2)}) collective-permute-start(bf16[128,512]{1,0:T(8,128)(2,1)} %param.9), channel_id=1, source_target_pairs={{0,3},{1,4},{2,5},{3,6},{4,7},{5,8},{6,9},{7,10},{8,11},{9,12},{10... | collective-permute-start | bytes 393224 | tf_op jit(solution)/shard_map/ppermute | solution.py:38
  7.7 23.1 %collective-permute-start.1 = (bf16[128,512]{1,0:T(8,128)(2,1)}, bf16[128,512]{1,0:T(8,128)(2,1)S(1)}, u32[]{:S(2)}, u32[]{:S(2)}) collective-permute-start(bf16[128,512]{1,0:T(8,128)(2,1)} %param.9), channel_id=1, source_target_pairs={{0,2},{1,3},{2,4},{3,5},{4,6},{5,7},{6,8},{7,9},{8,10},{9,11},{10,... | collective-permute-start | bytes 393224 | tf_op jit(solution)/shard_map/ppermute | solution.py:38
  13.9 21.8 %collective-permute-start.3 = (bf16[128,512]{1,0:T(8,128)(2,1)}, bf16[128,512]{1,0:T(8,128)(2,1)S(1)}, u32[]{:S(2)}, u32[]{:S(2)}) collective-permute-start(bf16[128,512]{1,0:T(8,128)(2,1)} %param.9), channel_id=1, source_target_pairs={{0,1},{1,2},{2,3},{3,4},{4,5},{5,6},{6,7},{7,8},{8,9},{9,10},{10,1... | collective-permute-start | bytes 393224 | tf_op jit(solution)/shard_map/ppermute | solution.py:38
  18.9 27.0 %all-to-all-start = ((bf16[32,16,128]{2,1,0:T(8,128)(2,1)}), bf16[32,16,128]{2,1,0:T(8,128)(2,1)S(1)}, u32[]{:S(2)}, u32[]{:S(2)}) async-start(bf16[32,16,128]{2,1,0:T(8,128)(2,1)} %broadcast_in_dim.28), calls=%async_computation | async-start | bytes 262144 | tf_op jit(solution)/shard_map/all_to_all | solution.py:42
  30.8 4.8 %copy-start.11 = (bf16[128,512]{1,0:T(8,128)(2,1)S(1)}, bf16[128,512]{1,0:T(8,128)(2,1)}, u32[]{:S(2)}) copy-start(bf16[128,512]{1,0:T(8,128)(2,1)} %param.9) | copy-start | bytes 393220
  30.9 27.0 %copy-start.12 = (bf16[256,512]{1,0:T(8,128)(2,1)}, bf16[256,512]{1,0:T(8,128)(2,1)S(1)}, u32[]{:S(2)}) copy-start(bf16[256,512]{1,0:T(8,128)(2,1)S(1)} %constant_dynamic-update-slice_fusion.keys1_ref) | copy-start | bytes 786436
  30.9 25.6 %collective-permute-start.2 = (bf16[256,512]{1,0:T(8,128)(2,1)S(1)}, bf16[256,512]{1,0:T(8,128)(2,1)}, u32[]{:S(2)}, u32[]{:S(2)}) collective-permute-start(bf16[256,512]{1,0:T(8,128)(2,1)S(1)} %constant_dynamic-update-slice_fusion.keys1_ref), channel_id=1, source_target_pairs={{0,2},{1,3},{2,4},{3,5},{4,6},{5,7},{6,8},{7,9},{8,10},{9,11},{10,... | collective-permute-start | bytes 786440 | tf_op jit(solution)/shard_map/ppermute | solution.py:38
  47.0 26.6 %all-to-all-start.1 = ((bf16[16,8,4096]{2,1,0:T(8,128)(2,1)}), bf16[16,8,4096]{2,1,0:T(8,128)(2,1)S(1)}, u32[]{:S(2)}, u32[]{:S(2)}) async-start(bf16[16,8,4096]{2,1,0:T(8,128)(2,1)} %broadcast_in_dim.30), calls=%async_computation.1 | async-start | bytes 2097152 | tf_op jit(solution)/shard_map/all_to_all | solution.py:42
  56.6 20.7 %collective-permute-start.4 = (bf16[256,512]{1,0:T(8,128)(2,1)}, bf16[256,512]{1,0:T(8,128)(2,1)S(1)}, u32[]{:S(2)}, u32[]{:S(2)}) collective-permute-start(bf16[256,512]{1,0:T(8,128)(2,1)} %collective-permute-done.2.keys2_ref), channel_id=1, source_target_pairs={{0,2},{1,3},{2,4},{3,5},{4,6},{5,7},{6,8},{7,9},{8,10},{9,11},{10,... | collective-permute-start | bytes 786440 | tf_op jit(solution)/shard_map/ppermute | solution.py:38
  59.1 14.5 %copy-start.2 = (bf16[128,8192]{1,0:T(8,128)(2,1)S(1)}, bf16[128,8192]{1,0:T(8,128)(2,1)}, u32[]{:S(2)}) copy-start(bf16[128,8192]{1,0:T(8,128)(2,1)} %hidden_ref.3) | copy-start | bytes 6291460
  74.4 6.0 %copy-start.1 = (f32[1024,128]{1,0:T(8,128)S(1)}, f32[1024,128]{1,0:T(8,128)}, u32[]{:S(2)}) copy-start(f32[1024,128]{1,0:T(8,128)} %fusion.1.bias_ref) | copy-start | bytes 1572868
  74.4 6.0 %copy-start.3 = (bf16[128,4096]{1,0:T(8,128)(2,1)S(1)}, bf16[128,4096]{1,0:T(8,128)(2,1)}, u32[]{:S(2)}) copy-start(bf16[128,4096]{1,0:T(8,128)(2,1)} %query_ref.3) | copy-start | bytes 3145732
  74.4 2.8 %collective-permute-start.5 = (bf16[64,128]{1,0:T(8,128)(2,1)S(1)}, bf16[64,128]{1,0:T(8,128)(2,1)S(1)}, u32[]{:S(2)}, u32[]{:S(2)}) collective-permute-start(bf16[64,128]{1,0:T(8,128)(2,1)S(1)} %lowrank.1), channel_id=1, source_target_pairs={{0,1},{1,2},{2,3},{3,4},{4,5},{5,6},{6,7},{7,8},{8,9},{9,10},{10,1... | collective-permute-start | bytes 49160 | tf_op jit(solution)/shard_map/ppermute | solution.py:38
  77.2 5.4 %copy-start.7 = (bf16[256,4096]{1,0:T(8,128)(2,1)S(1)}, bf16[256,4096]{1,0:T(8,128)(2,1)}, u32[]{:S(2)}) copy-start(bf16[256,4096]{1,0:T(8,128)(2,1)} %get-tuple-element.29.w2_ref) | copy-start | bytes 6291460
  77.3 5.4 %copy-start.10 = (f32[8,4096]{1,0:T(8,128)S(1)}, f32[8,4096]{1,0:T(8,128)}, u32[]{:S(2)}) copy-start(f32[8,4096]{1,0:T(8,128)} %get-tuple-element.31.stats_ref) | copy-start | bytes 393220
  77.3 5.3 %collective-permute-start.6 = (bf16[64,256]{1,0:T(8,128)(2,1)S(1)}, bf16[64,256]{1,0:T(8,128)(2,1)S(1)}, u32[]{:S(2)}, u32[]{:S(2)}) collective-permute-start(bf16[64,256]{1,0:T(8,128)(2,1)S(1)} %pad_maximum_fusion.2), channel_id=1, source_target_pairs={{0,2},{1,3},{2,4},{3,5},{4,6},{5,7},{6,8},{7,9},{8,10},{9,11},{10,... | collective-permute-start | bytes 98312 | tf_op jit(solution)/shard_map/ppermute | solution.py:38
  82.6 10.6 %copy-start.8 = (bf16[256,4096]{1,0:T(8,128)(2,1)S(1)}, bf16[256,4096]{1,0:T(8,128)(2,1)}, u32[]{:S(2)}) copy-start(bf16[256,4096]{1,0:T(8,128)(2,1)} %get-tuple-element.22.w1_ref) | copy-start | bytes 6291460
  82.6 10.6 %copy-start.9 = (bf16[256,4096]{1,0:T(8,128)(2,1)S(1)}, bf16[256,4096]{1,0:T(8,128)(2,1)}, u32[]{:S(2)}) copy-start(bf16[256,4096]{1,0:T(8,128)(2,1)} %get-tuple-element.23.w0_ref) | copy-start | bytes 6291460
  84.0 10.5 %collective-permute-start.7 = (bf16[64,512]{1,0:T(8,128)(2,1)S(1)}, bf16[64,512]{1,0:T(8,128)(2,1)S(1)}, u32[]{:S(2)}, u32[]{:S(2)}) collective-permute-start(bf16[64,512]{1,0:T(8,128)(2,1)S(1)} %get-tuple-element.34), channel_id=1, source_target_pairs={{4,0},{5,1},{6,2},{7,3},{8,4},{9,5},{10,6},{11,7},{12,8},{13,9},{1... | collective-permute-start | bytes 196616 | tf_op jit(solution)/shard_map/ppermute | solution.py:38
  85.3 10.6 %collective-permute-start.10 = (bf16[64,512]{1,0:T(8,128)(2,1)S(1)}, bf16[64,512]{1,0:T(8,128)(2,1)S(1)}, u32[]{:S(2)}, u32[]{:S(2)}) collective-permute-start(bf16[64,512]{1,0:T(8,128)(2,1)S(1)} %pad_maximum_fusion.1), channel_id=1, source_target_pairs={{0,4},{1,5},{2,6},{3,7},{4,8},{5,9},{6,10},{7,11},{8,12},{9,13},{1... | collective-permute-start | bytes 196616 | tf_op jit(solution)/shard_map/ppermute | solution.py:38
  94.5 6.2 %collective-permute-start.8 = (f32[64,256]{1,0:T(8,128)S(1)}, f32[64,256]{1,0:T(8,128)S(1)}, u32[]{:S(2)}, u32[]{:S(2)}) collective-permute-start(f32[64,256]{1,0:T(8,128)S(1)} %slice.27), channel_id=1, source_target_pairs={{2,0},{3,1},{4,2},{5,3},{6,4},{7,5},{8,6},{9,7},{10,8},{11,9},{12,... | collective-permute-start | bytes 196616 | tf_op jit(solution)/shard_map/ppermute | solution.py:38
  100.8 4.7 %collective-permute-start.9 = (f32[64,128]{1,0:T(8,128)S(1)}, f32[64,128]{1,0:T(8,128)S(1)}, u32[]{:S(2)}, u32[]{:S(2)}) collective-permute-start(f32[64,128]{1,0:T(8,128)S(1)} %slice.29), channel_id=1, source_target_pairs={{1,0},{2,1},{3,2},{4,3},{5,4},{6,5},{7,6},{8,7},{9,8},{10,9},{11,1... | collective-permute-start | bytes 98312 | tf_op jit(solution)/shard_map/ppermute | solution.py:38
  105.9 10.3 %collective-permute-start.11 = (f32[64,4352]{1,0:T(8,128)S(1)}, f32[64,4352]{1,0:T(8,128)S(1)}, u32[]{:S(2)}, u32[]{:S(2)}) collective-permute-start(f32[64,4352]{1,0:T(8,128)S(1)} %get-tuple-element.37), channel_id=1, source_target_pairs={{0,32},{32,0},{64,96},{96,64},{128,160},{160,128},{192,224},{224,1... | collective-permute-start | bytes 3342344 | tf_op jit(solution)/shard_map/ppermute | solution.py:386
  (3 other events, 5.6 us)
